TPU v7x, 256 devices: a whole 4x4x8 slice. The times are simulated.
256 devices in a mesh: layer: 8 (over y, z_lo), row: 32 (over z_hi, x, core).
Axes of the slice: x: 4, y: 4, z: 8 (z_hi: 4, z_lo: 2; z = z_hi * 2 + z_lo), core: 2. Of those that a mesh axis runs over, the one named last changes fastest.
Arguments:
- q_prev: float32 [32, 2048, 2048], P('layer', 'row'), may hold values from -6 to 6
- q_now: float32 [32, 2048, 2048], P('layer', 'row'), may hold values from -6 to 6
- psi_now: float32 [32, 2048, 2048], P('layer', 'row'), may hold values from -6 to 6
- layers_to_modes: float32 [32, 32], replicated, may hold values from -1 to 1
- modes_to_layers: float32 [32, 32], replicated, may hold values from -7 to 7
- stretch: float32 [32], replicated, may hold values from 6.1035156e-05 to 2
Outputs:
- q_next: float32 [32, 2048, 2048], P('layer', 'row')
- psi_next: float32 [32, 2048, 2048], P('layer', 'row')
All inputs are finite; a program needn't handle non-finite values.
Results may differ from a plain program's by a relative error of at most 0.003.
Values sent between devices are 32-bit elements; how exact they have to be, the bound alone decides.
No kernel may reach another device: no remote copies, remote signals or barrier semaphores. Data moves between devices by JAX's collectives and lax.ppermute only.
A program may use at most 192 MiB of HBM per device.

v0:
```python
import math

import jax
import jax.numpy as jnp
from jax import lax
from jax.sharding import PartitionSpec as P

TIME_STEP = 0.1
VISCOSITY = 0.02
HIGHEST = lax.Precision.HIGHEST


def extended(value, sides, width):
    for axis, dim in sides:
        count, length = (lax.axis_size(axis), value.shape[dim])
        up = [(i, (i + 1) % count) for i in range(count - 1)]
        down = [(j, i) for i, j in up]
        last = lax.slice_in_dim(value, length - width, length, axis=dim)
        initial = lax.slice_in_dim(value, 0, width, axis=dim)
        before = lax.ppermute(last, axis, up)
        after = lax.ppermute(initial, axis, down)
        value = jnp.concatenate([before, value, after], axis=dim)
    return value


def five_point(padded):
    return (
        padded[..., 2:, 1:-1]
        + padded[..., :-2, 1:-1]
        + padded[..., 1:-1, 2:]
        + padded[..., 1:-1, :-2]
        - 4.0 * padded[..., 1:-1, 1:-1]
    )


def offset(source, row_step, col_step):
    height = source.shape[-2]
    width = source.shape[-1]
    return source[..., 1 + row_step : height - 1 + row_step, 1 + col_step : width - 1 + col_step]


def arakawa(stream, vortex):
    first = (offset(stream, 0, 1) - offset(stream, 0, -1)) * (
        offset(vortex, 1, 0) - offset(vortex, -1, 0)
    ) - (offset(stream, 1, 0) - offset(stream, -1, 0)) * (
        offset(vortex, 0, 1) - offset(vortex, 0, -1)
    )
    second = (
        offset(stream, 0, 1) * (offset(vortex, 1, 1) - offset(vortex, -1, 1))
        - offset(stream, 0, -1) * (offset(vortex, 1, -1) - offset(vortex, -1, -1))
        - offset(stream, 1, 0) * (offset(vortex, 1, 1) - offset(vortex, 1, -1))
        + offset(stream, -1, 0) * (offset(vortex, -1, 1) - offset(vortex, -1, -1))
    )
    third = (
        offset(vortex, 1, 0) * (offset(stream, 1, 1) - offset(stream, 1, -1))
        - offset(vortex, -1, 0) * (offset(stream, -1, 1) - offset(stream, -1, -1))
        - offset(vortex, 0, 1) * (offset(stream, 1, 1) - offset(stream, -1, 1))
        + offset(vortex, 0, -1) * (offset(stream, 1, -1) - offset(stream, -1, -1))
    )
    return (first + second + third) / 12.0


def angle_table(first_index, second_index, length):
    product = first_index[:, None] * second_index[None, :] % (2 * (length + 1))
    return jnp.sin(product.astype(jnp.float32) * (math.pi / (length + 1)))


def half_tables(length):
    half_len = length // 2
    positions = jnp.arange(half_len, dtype=jnp.int32)
    even_tab = angle_table(positions + 1, 2 * positions + 1, length)
    odd_tab = angle_table(positions + 1, 2 * positions + 2, length)
    return (even_tab, odd_tab)


def permuted_eigen(positions, length):
    half_len = length // 2
    wavenumber = jnp.where(positions < half_len, 2 * positions, 2 * (positions - half_len) + 1)
    return 2.0 - 2.0 * jnp.cos((wavenumber + 1).astype(jnp.float32) * (math.pi / (length + 1)))


def forward_columns(source):
    length = source.shape[-1]
    half_len = length // 2
    even_tab, odd_tab = half_tables(length)
    lower_half = source[..., :half_len]
    upper_half = jnp.flip(source[..., half_len:], -1)
    even_part = jnp.einsum("mrj,jk->mkr", lower_half + upper_half, even_tab, precision=HIGHEST)
    odd_part = jnp.einsum("mrj,jk->mkr", lower_half - upper_half, odd_tab, precision=HIGHEST)
    return jnp.concatenate([even_part, odd_part], 1)


def forward_last(source):
    length = source.shape[-1]
    half_len = length // 2
    even_tab, odd_tab = half_tables(length)
    lower_half = source[..., :half_len]
    upper_half = jnp.flip(source[..., half_len:], -1)
    even_part = jnp.einsum("mcj,jk->mck", lower_half + upper_half, even_tab, precision=HIGHEST)
    odd_part = jnp.einsum("mcj,jk->mck", lower_half - upper_half, odd_tab, precision=HIGHEST)
    return jnp.concatenate([even_part, odd_part], -1)


def inverse_last(source):
    length = source.shape[-1]
    half_len = length // 2
    even_tab, odd_tab = half_tables(length)
    even_sum = jnp.einsum("mck,jk->mcj", source[..., :half_len], even_tab, precision=HIGHEST)
    odd_sum = jnp.einsum("mck,jk->mcj", source[..., half_len:], odd_tab, precision=HIGHEST)
    joined = jnp.concatenate([even_sum + odd_sum, jnp.flip(even_sum - odd_sum, -1)], -1)
    return joined * (2.0 / (length + 1))


def inverse_columns(source):
    length = source.shape[1]
    half_len = length // 2
    even_tab, odd_tab = half_tables(length)
    even_sum = jnp.einsum("mkr,jk->mrj", source[:, :half_len], even_tab, precision=HIGHEST)
    odd_sum = jnp.einsum("mkr,jk->mrj", source[:, half_len:], odd_tab, precision=HIGHEST)
    joined = jnp.concatenate([even_sum + odd_sum, jnp.flip(even_sum - odd_sum, -1)], -1)
    return joined * (2.0 / (length + 1))


def on_device(q_prev, q_now, psi_now, layers_to_modes, modes_to_layers, stretch):
    layer_count = q_prev.shape[0]
    row_count = q_prev.shape[1]
    total_rows = row_count * lax.axis_size("row")
    near_rims = extended(jnp.stack([psi_now, q_now]), (("row", 2),), 1)
    stream_ext = near_rims[0]
    vortex_ext = near_rims[1]
    friction_ext = extended(q_prev, (("row", 1),), 2)
    column_pad = ((0, 0), (0, 0), (1, 1))
    tendency = -arakawa(jnp.pad(stream_ext, column_pad), jnp.pad(vortex_ext, column_pad))
    inner_lap = five_point(jnp.pad(friction_ext, column_pad))
    global_rows = lax.axis_index("row") * row_count - 1 + jnp.arange(row_count + 2, dtype=jnp.int32)
    inside = (global_rows >= 0) & (global_rows < total_rows)
    inner_lap = jnp.where(inside[None, :, None], inner_lap, 0.0)
    tendency = tendency - VISCOSITY * five_point(jnp.pad(inner_lap, column_pad))
    q_next = q_prev + 2.0 * TIME_STEP * tendency
    row_eigen = permuted_eigen(jnp.arange(total_rows, dtype=jnp.int32), total_rows)
    layer_base = lax.axis_index("layer") * layer_count
    stacked = lax.all_to_all(q_next, "layer", split_axis=1, concat_axis=0, tiled=True)
    modal_rows = jnp.einsum("ml,lrc->mrc", layers_to_modes, stacked, precision=HIGHEST)
    modal_field = lax.all_to_all(modal_rows, "layer", split_axis=0, concat_axis=1, tiled=True)
    column_spectra = forward_columns(modal_field)
    spectra = lax.all_to_all(column_spectra, "row", split_axis=1, concat_axis=2, tiled=True)
    col_count = spectra.shape[1]
    col_positions = lax.axis_index("row") * col_count + jnp.arange(col_count, dtype=jnp.int32)
    col_eigen = permuted_eigen(col_positions, col_count * lax.axis_size("row"))
    stretch_local = lax.dynamic_slice_in_dim(stretch, layer_base, layer_count)
    spectrum = forward_last(spectra)
    solved = -spectrum / (
        col_eigen[None, :, None] + row_eigen[None, None, :] + stretch_local[:, None, None]
    )
    row_physical = inverse_last(solved)
    returned = lax.all_to_all(row_physical, "row", split_axis=2, concat_axis=1, tiled=True)
    psi_modes = inverse_columns(returned)
    stacked_psi = lax.all_to_all(psi_modes, "layer", split_axis=1, concat_axis=0, tiled=True)
    layered = jnp.einsum("lm,mrc->lrc", modes_to_layers, stacked_psi, precision=HIGHEST)
    psi_next = lax.all_to_all(layered, "layer", split_axis=0, concat_axis=1, tiled=True)
    return (q_next, psi_next)


def solution(mesh):
    return jax.shard_map(
        on_device,
        mesh=mesh,
        in_specs=(
            P("layer", "row", None),
            P("layer", "row", None),
            P("layer", "row", None),
            P(),
            P(),
            P(),
        ),
        out_specs=(P("layer", "row", None), P("layer", "row", None)),
        check_vma=False,
    )
```

profile of v0, /device:TPU:32, one launch (start us, length us, event | category | flops | bytes accessed | tf_op | source)
XLA Modules:
  0.0 585.4 jit_solution(16586224659880889240)
XLA Ops:
  0.7 3.1 copy.21
  3.8 1.7 collective-permute-start.3
  5.6 1.3 collective-permute-start.2
  6.9 2.7 copy_bitcast_fusion.5
  9.6 1.3 copy-done.3
  10.9 1.3 collective-permute-start.1
  12.2 4.9 collective-permute-start
  17.2 0.9 collective-permute-done
  18.0 2.4 pad_maximum_fusion
  20.4 0.9 slice_bitcast_fusion.1
  22.0 1.5 constant_dynamic-update-slice_fusion.1
  23.6 3.6 fusion.31
  27.2 17.5 %fusion.38 = f32[4,64,2048]{2,0,1:T(4,128)S(1)} fusion(f32[4,66,2048]{2,0,1:T(4,128)S(1)} %fusion.31, f32[4,66,2048]{2,0,1:T(4,128)S(1)} %get-tuple-element.5, f32[4,66,2048]{2,0,1:T(4,128)S(1)} %get-tuple-element.4, f32[4,64,2048]{2,1,0:T(8,128)S(1)} %copy-done.2), kind=kLoop, calls=%fused_computation.43 | loop fusion | flops 22020096 | bytes 25362432 | tf_op jit(solution)/shard_map/add | solution.py:139
  44.7 32.4 %all_to_all.108 = f32[4,64,2048]{2,0,1:T(4,128)S(1)} all-to-all(f32[4,64,2048]{2,0,1:T(4,128)S(1)} %fusion.38), channel_id=1, replica_groups=mesh['layer'=8,'row'=32] {'layer'}, dimensions={1} | all-to-all | bytes 4194304 | tf_op jit(solution)/shard_map/all_to_all | solution.py:142
  77.1 1.5 copy.47
  78.6 2.9 all_to_all.81
  81.5 3.6 convolution_bitcast_fusion.1
  85.1 2.5 copy.23
  87.6 5.4 all-to-all-start.1
  93.1 27.1 %all-to-all-done.1 = f32[32,8,2048]{2,1,0:T(8,128)} async-done(((f32[32,8,2048]{2,1,0:T(8,128)}), f32[32,8,2048]{2,1,0:T(8,128)}, u32[]{:S(2)}, u32[]{:S(2)}) %all-to-all-start.1) | async-done | bytes 2097184 | tf_op jit(solution)/shard_map/all_to_all | solution.py:144
  120.1 1.7 copy.46
  121.9 1.3 copy-done.7
  123.3 3.2 rev.13
  126.5 21.6 %fusion.85 = f32[4,1024,64]{1,2,0:T(8,128)S(1)} fusion(s32[1024]{0:T(1024)S(1)} %get-tuple-element.18, s32[1024]{0:T(1024)S(1)} %get-tuple-element.19, f32[4,64,1024]{2,1,0:T(8,128)} %rev.13, f32[4,64,2048]{2,1,0:T(8,128)} %bitcast.95), kind=kOutput, calls=%fused_computation.91 | convolution fusion | flops 3230924800 | bytes 3153920 | tf_op jit(solution)/shard_map/mrj,jk->mkr/dot_general | solution.py:89
  148.2 20.4 %fusion.82 = f32[4,1024,64]{1,2,0:T(8,128)S(1)} fusion(s32[1024]{0:T(1024)S(1)} %fusion.112, s32[1024]{0:T(1024)S(1)} %get-tuple-element.19, f32[4,64,1024]{2,1,0:T(8,128)S(1)} %copy-done.13, f32[4,64,2048]{2,1,0:T(8,128)S(1)} %bitcast.96), kind=kOutput, calls=%fused_computation.90 | convolution fusion | flops 3230924800 | bytes 3153920 | tf_op jit(solution)/shard_map/mrj,jk->mkr/dot_general | solution.py:88
  168.6 1.5 pad_maximum_fusion.1
  170.0 4.8 copy.25
  174.8 6.3 %reshape.93 = f32[32,1,16384]{2,1,0:T(1,128)} reshape(f32[2048,4,64]{2,1,0:T(4,128)} %bitcast.85) | data formatting | bytes 4194304
  181.1 13.5 %all-to-all-start.2 = ((f32[32,1,16384]{2,1,0:T(1,128)}), f32[32,1,16384]{2,1,0:T(1,128)}, u32[]{:S(2)}, u32[]{:S(2)}) async-start(f32[32,1,16384]{2,1,0:T(1,128)} %reshape.93), calls=%async_computation.2 | async-start | bytes 4194304 | tf_op jit(solution)/shard_map/all_to_all | solution.py:146
  194.8 1.0 broadcast_add_fusion
  195.8 43.4 %all-to-all-done.2 = f32[32,1,16384]{2,1,0:T(1,128)} async-done(((f32[32,1,16384]{2,1,0:T(1,128)}), f32[32,1,16384]{2,1,0:T(1,128)}, u32[]{:S(2)}, u32[]{:S(2)}) %all-to-all-start.2) | async-done | bytes 2097184 | tf_op jit(solution)/shard_map/all_to_all | solution.py:146
  239.7 8.7 %reduce = f32[32,16384]{1,0:T(8,128)} reduce(f32[32,1,16384]{2,1,0:T(1,128)} %all-to-all-done.2, f32[]{:T(128)} %broadcast.260), dimensions={1}, to_apply=%all_to_all.86.reduce_sub_computation | reduce | bytes 4194308 | tf_op jit(solution)/shard_map/all_to_all | solution.py:146
  248.4 5.4 reshape.94
  253.8 6.6 %copy.26 = f32[4,64,32,64]{3,2,1,0:T(8,128)} copy(f32[4,64,32,64]{3,0,1,2:T(4,128)} %bitcast.87) | data formatting | bytes 4194304 | tf_op jit(solution)/shard_map/all_to_all | solution.py:146
  260.4 5.0 all_to_all.89
  265.4 1.2 slice-done
  266.6 3.4 rev.14
  270.1 21.6 %fusion.14 = f32[4,64,1024]{2,1,0:T(8,128)S(1)} fusion(s32[1024]{0:T(1024)S(1)} %get-tuple-element.18, s32[1024]{0:T(1024)S(1)} %get-tuple-element.19, f32[4,64,1024]{2,1,0:T(8,128)} %rev.14, f32[4,64,2048]{2,1,0:T(8,128)} %all_to_all.89), kind=kOutput, calls=%fused_computation.17 | convolution fusion | flops 3230924800 | bytes 3153920 | tf_op jit(solution)/shard_map/mcj,jk->mck/dot_general | solution.py:100
  291.7 19.9 %fusion.24 = f32[4,64,1024]{2,1,0:T(8,128)S(1)} fusion(s32[1024]{0:T(1024)S(1)} %fusion.112, s32[1024]{0:T(1024)S(1)} %get-tuple-element.19, f32[4,64,1024]{2,1,0:T(8,128)S(1)} %copy-done.14, f32[4,64,2048]{2,1,0:T(8,128)S(1)} %copy-done.6), kind=kOutput, calls=%fused_computation.24 | convolution fusion | flops 3230924800 | bytes 3153920 | tf_op jit(solution)/shard_map/mcj,jk->mck/dot_general | solution.py:99
  312.1 20.0 %fusion.12 = f32[4,64,1024]{2,1,0:T(8,128)S(1)} fusion(s32[1024]{0:T(1024)S(1)} %get-tuple-element.18, s32[1024]{0:T(1024)S(1)} %get-tuple-element.19, f32[4,64,2048]{2,1,0:T(8,128)S(1)} %fusion.41), kind=kOutput, calls=%fused_computation.16 | convolution fusion | flops 3230662656 | bytes 2105344 | tf_op jit(solution)/shard_map/mck,jk->mcj/dot_general | solution.py:109
  332.1 20.9 %fusion.139 = (f32[4,64,1024]{2,1,0:T(8,128)}, f32[4,64,1024]{2,1,0:T(8,128)}) fusion(f32[4,64,1024]{2,1,0:T(8,128)S(1)} %fusion.12, s32[1024]{0:T(1024)S(1)} %fusion.112, s32[1024]{0:T(1024)S(1)} %get-tuple-element.19, f32[4,64,2048]{2,1,0:T(8,128)S(1)} %fusion.41), kind=kOutput, calls=%fused_computation.157 | convolution fusion | flops 3231186944 | bytes 4202496 | tf_op jit(solution)/shard_map/mck,jk->mcj/dot_general | solution.py:108
  353.1 4.2 rev.15
  357.2 2.8 maximum_multiply_fusion
  360.0 4.8 copy.27
  364.8 6.7 %reshape.95 = f32[32,1,16384]{2,1,0:T(1,128)} reshape(f32[2048,4,64]{2,1,0:T(4,128)} %bitcast.86) | data formatting | bytes 4194304
  371.4 52.0 %all_to_all.109 = f32[32,1,16384]{2,1,0:T(1,128)} all-to-all(f32[32,1,16384]{2,1,0:T(1,128)} %reshape.95), channel_id=1, replica_groups=mesh['layer'=8,'row'=32] {'row'}, dimensions={0} | all-to-all | bytes 4194304 | tf_op jit(solution)/shard_map/all_to_all | solution.py:156
  423.5 8.7 %reduce.1 = f32[32,16384]{1,0:T(8,128)} reduce(f32[32,1,16384]{2,1,0:T(1,128)} %all_to_all.109, f32[]{:T(128)} %broadcast.260), dimensions={1}, to_apply=%all_to_all.90.reduce_sub_computation | reduce | bytes 4194308 | tf_op jit(solution)/shard_map/all_to_all | solution.py:156
  432.2 5.4 reshape.96
  437.6 6.6 %copy.43 = f32[4,64,32,64]{1,2,3,0:T(8,128)} copy(f32[4,64,32,64]{1,0,3,2:T(4,128)} %bitcast.88) | data formatting | bytes 4194304 | tf_op jit(solution)/shard_map/all_to_all | solution.py:156
  444.2 5.1 all_to_all.93
  449.3 21.0 %fusion.10 = f32[4,64,1024]{2,1,0:T(8,128)S(1)} fusion(s32[1024]{0:T(1024)S(1)} %get-tuple-element.18, s32[1024]{0:T(1024)S(1)} %get-tuple-element.19, f32[4,2048,64]{1,2,0:T(8,128)} %all_to_all.93), kind=kOutput, calls=%fused_computation.15 | convolution fusion | flops 3230662656 | bytes 2105344 | tf_op jit(solution)/shard_map/mkr,jk->mrj/dot_general | solution.py:119
  470.3 21.7 %fusion.138 = (f32[4,64,1024]{2,1,0:T(8,128)}, f32[4,64,1024]{2,1,0:T(8,128)}) fusion(f32[4,64,1024]{2,1,0:T(8,128)S(1)} %fusion.10, s32[1024]{0:T(1024)S(1)} %fusion.112, s32[1024]{0:T(1024)S(1)} %get-tuple-element.19, f32[4,2048,64]{1,2,0:T(8,128)S(1)} %copy-done.9), kind=kOutput, calls=%fused_computation.156 | convolution fusion | flops 3231186944 | bytes 4202496 | tf_op jit(solution)/shard_map/mkr,jk->mrj/dot_general | solution.py:118
  492.0 4.2 rev.16
  496.2 1.4 maximum_multiply_fusion.1
  497.6 1.4 copy.29
  499.0 41.9 %all_to_all.110 = f32[4,64,2048]{2,0,1:T(4,128)S(1)} all-to-all(f32[4,64,2048]{2,0,1:T(4,128)S(1)} %copy.29), channel_id=1, replica_groups=mesh['layer'=8,'row'=32] {'layer'}, dimensions={1} | all-to-all | bytes 4194304 | tf_op jit(solution)/shard_map/all_to_all | solution.py:158
  540.9 1.5 copy.45
  542.4 2.9 all_to_all.97
  545.3 3.6 convolution_bitcast_fusion
  548.9 2.5 copy.31
  551.4 5.4 all-to-all-start.5
  556.8 2.5 copy.33
  559.4 22.7 %all-to-all-done.5 = f32[32,8,2048]{2,1,0:T(8,128)} async-done(((f32[32,8,2048]{2,1,0:T(8,128)}), f32[32,8,2048]{2,1,0:T(8,128)}, u32[]{:S(2)}, u32[]{:S(2)}) %all-to-all-start.5) | async-done | bytes 2097184 | tf_op jit(solution)/shard_map/all_to_all | solution.py:160
  582.0 3.1 copy.44
  (49 shorter events, 2.3 us)
Async XLA Ops:
  0.6 80.9 %copy-start = (f32[32,32]{1,0:T(8,128)S(1)}, f32[32,32]{1,0:T(8,128)}, u32[]{:S(2)}) copy-start(f32[32,32]{1,0:T(8,128)} %param.9) | copy-start | bytes 12292
  0.6 6.2 %copy-start.11 = (f32[4,64,2048]{2,1,0:T(8,128)S(1)}, f32[4,64,2048]{2,1,0:T(8,128)}, u32[]{:S(2)}) copy-start(f32[4,64,2048]{2,1,0:T(8,128)} %param.7) | copy-start | bytes 6291460
  0.7 6.2 %copy-start.12 = (f32[4,64,2048]{2,1,0:T(8,128)S(1)}, f32[4,64,2048]{2,1,0:T(8,128)}, u32[]{:S(2)}) copy-start(f32[4,64,2048]{2,1,0:T(8,128)} %param.8) | copy-start | bytes 6291460
  3.8 1.8 copy-start.4
  3.8 17.5 %collective-permute-start.3 = (f32[4,2,2048]{2,0,1:T(4,128)S(1)}, f32[4,2,2048]{2,0,1:T(4,128)S(1)}, u32[]{:S(2)}, u32[]{:S(2)}) collective-permute-start(f32[4,2,2048]{2,0,1:T(4,128)S(1)} %get-tuple-element.13), channel_id=1, source_target_pairs={{0,1},{1,2},{2,3},{3,4},{4,5},{5,6},{6,7},{7,8},{8,9},{9,10},{10,1... | collective-permute-start | bytes 196616 | tf_op jit(solution)/shard_map/ppermute | solution.py:20
  5.6 17.9 %collective-permute-start.2 = (f32[4,2,2048]{2,0,1:T(4,128)S(1)}, f32[4,2,2048]{2,0,1:T(4,128)S(1)}, u32[]{:S(2)}, u32[]{:S(2)}) collective-permute-start(f32[4,2,2048]{2,0,1:T(4,128)S(1)} %get-tuple-element.12), channel_id=1, source_target_pairs={{1,0},{2,1},{3,2},{4,3},{5,4},{6,5},{7,6},{8,7},{9,8},{10,9},{11,1... | collective-permute-start | bytes 196616 | tf_op jit(solution)/shard_map/ppermute | solution.py:21
  9.6 1.3 copy-start.3
  10.9 6.3 %collective-permute-start.1 = (f32[2,4,1,2048]{3,1,2,0:T(4,128)S(1)}, f32[2,4,1,2048]{3,1,2,0:T(4,128)S(1)}, u32[]{:S(2)}, u32[]{:S(2)}) collective-permute-start(f32[2,4,1,2048]{3,1,2,0:T(4,128)S(1)} %get-tuple-element.7), channel_id=1, source_target_pairs={{1,0},{2,1},{3,2},{4,3},{5,4},{6,5},{7,6},{8,7},{9,8},{10,9},{11,1... | collective-permute-start | bytes 196616 | tf_op jit(solution)/shard_map/ppermute | solution.py:21
  12.2 5.8 collective-permute-start
  20.4 1.6 copy-start.2
  22.0 1.6 copy-start.5
  87.6 32.5 %all-to-all-start.1 = ((f32[32,8,2048]{2,1,0:T(8,128)}), f32[32,8,2048]{2,1,0:T(8,128)}, u32[]{:S(2)}, u32[]{:S(2)}) async-start(f32[32,8,2048]{2,1,0:T(8,128)} %copy.23), calls=%async_computation.1 | async-start | bytes 4194304 | tf_op jit(solution)/shard_map/all_to_all | solution.py:144
  121.8 1.3 copy-start.7
  126.5 21.6 %copy-start.8 = (f32[4,8,8,2048]{3,2,1,0:T(8,128)S(1)}, f32[4,8,8,2048]{3,2,1,0:T(8,128)}, u32[]{:S(2)}) copy-start(f32[4,8,8,2048]{3,2,1,0:T(8,128)} %copy-done.7) | copy-start | bytes 6291460
  126.5 21.6 %copy-start.13 = (f32[4,64,1024]{2,1,0:T(8,128)S(1)}, f32[4,64,1024]{2,1,0:T(8,128)}, u32[]{:S(2)}) copy-start(f32[4,64,1024]{2,1,0:T(8,128)} %rev.13) | copy-start | bytes 3145732
  181.1 13.5 %copy-start.16 = (f32[32]{0:T(128)S(1)}, f32[32]{0:T(128)}, u32[]{:S(2)}) copy-start(f32[32]{0:T(128)} %param.11) | copy-start | bytes 388
  181.1 58.1 %all-to-all-start.2 = ((f32[32,1,16384]{2,1,0:T(1,128)}), f32[32,1,16384]{2,1,0:T(1,128)}, u32[]{:S(2)}, u32[]{:S(2)}) async-start(f32[32,1,16384]{2,1,0:T(1,128)} %reshape.93), calls=%async_computation.2 | async-start | bytes 4194304 | tf_op jit(solution)/shard_map/all_to_all | solution.py:146
  265.4 1.2 slice-start
  270.0 21.6 %copy-start.6 = (f32[4,64,2048]{2,1,0:T(8,128)S(1)}, f32[4,64,2048]{2,1,0:T(8,128)}, u32[]{:S(2)}) copy-start(f32[4,64,2048]{2,1,0:T(8,128)} %all_to_all.89) | copy-start | bytes 6291460
  270.1 21.6 %copy-start.14 = (f32[4,64,1024]{2,1,0:T(8,128)S(1)}, f32[4,64,1024]{2,1,0:T(8,128)}, u32[]{:S(2)}) copy-start(f32[4,64,1024]{2,1,0:T(8,128)} %rev.14) | copy-start | bytes 3145732
  291.7 19.9 %copy-start.10 = (f32[64,2048]{1,0:T(8,128)S(1)}, f32[64,2048]{1,0:T(8,128)}, u32[]{:S(2)}) copy-start(f32[64,2048]{1,0:T(8,128)} %broadcast_add_fusion) | copy-start | bytes 1572868
  449.3 21.0 %copy-start.9 = (f32[4,2048,64]{1,2,0:T(8,128)S(1)}, f32[4,2048,64]{1,2,0:T(8,128)}, u32[]{:S(2)}) copy-start(f32[4,2048,64]{1,2,0:T(8,128)} %all_to_all.93) | copy-start | bytes 6291460
  542.4 2.9 copy-start.15
  551.4 30.6 %all-to-all-start.5 = ((f32[32,8,2048]{2,1,0:T(8,128)}), f32[32,8,2048]{2,1,0:T(8,128)}, u32[]{:S(2)}, u32[]{:S(2)}) async-start(f32[32,8,2048]{2,1,0:T(8,128)} %copy.31), calls=%async_computation.5 | async-start | bytes 4194304 | tf_op jit(solution)/shard_map/all_to_all | solution.py:160
  582.0 3.2 copy-start.1
where the time goes:
time: 597 us; the launch traced here: 585 us
  matrix products  174 us (29%)
  blocking collectives  126 us (21%)
  local copies, waits for them, and re-layouts  108 us (18%)
  waiting for transfers between devices  94 us (16%)
  other arithmetic  48.2 us (8%)
  starting transfers between devices  33.6 us (6%)
    all_to_all x1, blocking collectives, on_device(): lax.all_to_all(row_physical, 'row', split_axis=2, concat_axis=1, tiled=True)  52 us
    all_to_all x1, waiting for transfers between devices, on_device(): lax.all_to_all(column_spectra, 'row', split_axis=1, concat_axis=2, tiled=...  43.4 us
    all_to_all x1, blocking collectives, on_device(): lax.all_to_all(psi_modes, 'layer', split_axis=1, concat_axis=0, tiled=True)  41.9 us
    unnamed x42, local copies, waits for them, and re-layouts  34.2 us
    all_to_all x1, blocking collectives, on_device(): lax.all_to_all(q_next, 'layer', split_axis=1, concat_axis=0, tiled=True)  32.4 us
    all_to_all x1, waiting for transfers between devices, on_device(): lax.all_to_all(modal_rows, 'layer', split_axis=0, concat_axis=1, tiled=True)  27.1 us
    all_to_all x1, waiting for transfers between devices, on_device(): lax.all_to_all(layered, 'layer', split_axis=0, concat_axis=1, tiled=True)  22.7 us
    dot_general x1, matrix products, inverse_columns(): jnp.einsum('mkr,jk->mrj', source[:, :half_len], even_tab, precision=HIGHEST)  21.7 us
  transfers between devices with their start and end apart: 7, of which 4 were waited for; matrix products, arithmetic and copies ran while one was open for 2% of the time, Pallas kernels for 0%

commit v1 on v0

v1 whole, which is shorter than its diff:
```python
import functools
import math

import jax
import jax.numpy as jnp
import ml_dtypes
import numpy as np
from jax import lax
from jax.experimental import pallas as pl
from jax.experimental.pallas import tpu as pltpu
from jax.sharding import PartitionSpec as P

TIME_STEP = 0.1
VISCOSITY = 0.02
F32 = jnp.float32
BF16 = jnp.bfloat16
VMEM_LIMIT = 48 * 1024 * 1024
MARGIN = 128


def params():
    return pltpu.CompilerParams(vmem_limit_bytes=VMEM_LIMIT)


def half_table(length):
    positions = np.arange(1, length // 2 + 1, dtype=np.int64)
    product = (2 * positions[:, None] * positions[None, :]) % (2 * (length + 1))
    table = np.sin(product.astype(np.float64) * (math.pi / (length + 1)))
    high = table.astype(np.float32).astype(ml_dtypes.bfloat16)
    low = (table - high.astype(np.float64)).astype(np.float32).astype(ml_dtypes.bfloat16)
    return high, low


def column_eigen(length, shards):
    positions = np.arange(1, length // 2 + 1, dtype=np.float64)
    waves = np.stack([length + 1 - 2 * positions, 2 * positions])
    eigen = 4.0 * np.sin(waves * (math.pi / (2 * (length + 1)))) ** 2
    return eigen.astype(np.float32).reshape(2, shards, -1)


def split(value):
    high = value.astype(BF16)
    low = (value - high.astype(F32)).astype(BF16)
    return high, low


def dot(left, right):
    return jnp.dot(left, right, preferred_element_type=F32)


def flip_lanes(value):
    width = value.shape[1]
    order = 127 - lax.broadcasted_iota(jnp.int32, (value.shape[0], 128), 1)
    blocks = [
        jnp.take_along_axis(value[:, start : start + 128], order, axis=1)
        for start in range(width - 128, -1, -128)
    ]
    return jnp.concatenate(blocks, axis=1)


def alternating(width):
    lane = lax.broadcasted_iota(jnp.int32, (1, width), 1)
    return jnp.where(lane % 2 == 0, 1.0, -1.0).astype(F32)


def stencil_kernel(edge, prev, now, psi, top, bottom, q_out, fold, p_ext, z_ext, q_ext, l_ext):
    rows, cols = prev.shape[1], prev.shape[2]
    wide = cols + MARGIN

    def east(value):
        return pltpu.roll(value, wide - 1, 1)

    def west(value):
        return pltpu.roll(value, 1, 1)

    @pl.when(pl.program_id(0) == 0)
    def _():
        for ext in (p_ext, z_ext, q_ext, l_ext):
            ext[:, cols:] = jnp.zeros((rows + 16, MARGIN), F32)

    p_ext[8 : 8 + rows, :cols] = psi[0]
    z_ext[8 : 8 + rows, :cols] = now[0]
    q_ext[8 : 8 + rows, :cols] = prev[0]
    p_ext[7:8, :cols] = top[0, 0:1]
    z_ext[7:8, :cols] = top[0, 1:2]
    q_ext[6:8, :cols] = top[0, 2:4]
    p_ext[8 + rows : 9 + rows, :cols] = bottom[0, 0:1]
    z_ext[8 + rows : 9 + rows, :cols] = bottom[0, 1:2]
    q_ext[8 + rows : 10 + rows, :cols] = bottom[0, 2:4]

    def window(ext, tile):
        value = ext[pl.ds(pl.multiple_of(8 * tile, 8), 24), :]
        return value[7:15], value[8:16], value[9:17]

    def ghost(row):
        here = q_ext[row : row + 1, :]
        value = q_ext[row - 1 : row, :] + q_ext[row + 1 : row + 2, :] + east(here) + west(here) - 4.0 * here
        return value[:, :cols]

    l_ext[7:8, :cols] = ghost(7) * edge[0]
    l_ext[8 + rows : 9 + rows, :cols] = ghost(8 + rows) * edge[1]

    def inner(tile, carry):
        north, here, south = window(q_ext, tile)
        value = north + south + east(here) + west(here) - 4.0 * here
        l_ext[pl.ds(pl.multiple_of(8 * tile + 8, 8), 8), :cols] = value[:, :cols]
        return carry

    lax.fori_loop(0, rows // 8, inner, 0)

    def outer(tile, carry):
        zn, zc, zs = window(z_ext, tile)
        pn, pc, ps = window(p_ext, tile)
        zne, zce, zse = east(zn), east(zc), east(zs)
        znw, zcw, zsw = west(zn), west(zc), west(zs)
        down = zs - zn
        from_east = pc * ((zsw - znw) + down) + ps * (zsw - zc) + pn * (zc - znw)
        from_west = ps * (zc - zse) + pn * (zne - zc) - pc * ((zse - zne) + down)
        across = zce - zcw
        jacobian = pn * (across + (zne - znw)) - ps * (across + (zse - zsw))
        jacobian = jacobian + east(from_east) + west(from_west)
        ln, lc, ls = window(l_ext, tile)
        friction = ln + ls + east(lc) + west(lc) - 4.0 * lc
        here = q_ext[pl.ds(pl.multiple_of(8 * tile + 8, 8), 8), :]
        value = here - (2.0 * TIME_STEP / 12.0) * jacobian - (2.0 * TIME_STEP * VISCOSITY) * friction
        value = value[:, :cols]
        at = pl.ds(pl.multiple_of(8 * tile, 8), 8)
        q_out[0, at, :] = value
        lower, upper = value[:, : cols // 2], flip_lanes(value[:, cols // 2 :])
        fold[0, 0, at, :] = (lower + upper) * alternating(cols // 2)
        fold[1, 0, at, :] = lower - upper
        return carry

    lax.fori_loop(0, rows // 8, outer, 0)


def stencil(edge, q_prev, q_now, psi_now, top, bottom):
    layers, rows, cols = q_prev.shape
    block = pl.BlockSpec((1, rows, cols), lambda i: (i, 0, 0))
    rim = pl.BlockSpec((1, 4, cols), lambda i: (i, 0, 0))
    ext = pltpu.VMEM((rows + 16, cols + MARGIN), F32)
    return pl.pallas_call(
        stencil_kernel,
        grid=(layers,),
        in_specs=[pl.BlockSpec(memory_space=pltpu.SMEM), block, block, block, rim, rim],
        out_specs=[block, pl.BlockSpec((2, 1, rows, cols // 2), lambda i: (0, i, 0, 0))],
        out_shape=[
            jax.ShapeDtypeStruct(q_prev.shape, F32),
            jax.ShapeDtypeStruct((2, layers, rows, cols // 2), F32),
        ],
        scratch_shapes=[ext, ext, ext, ext],
        compiler_params=params(),
        name="stencil",
    )(edge, q_prev, q_now, psi_now, top, bottom)


def forward_kernel(source, table_high, table_low, result, high, low):
    @pl.when(pl.program_id(0) == 0)
    def _():
        high[...], low[...] = split(source[0])

    value = dot(high[...], table_high[...]) + dot(low[...], table_high[...]) + dot(high[...], table_low[...])
    width = result.shape[2]
    for part in range(result.shape[0]):
        result[part] = value[:, part * width : (part + 1) * width]


def forward(fold, parity, table_high, table_low, shards):
    depth = table_high.shape[0]
    lines = fold.shape[1] * fold.shape[2]
    width = depth // shards
    step = 2 * width
    column = pl.BlockSpec((depth, step), lambda i: (0, i))
    return pl.pallas_call(
        forward_kernel,
        grid=(depth // step,),
        in_specs=[pl.BlockSpec((1, lines, depth), lambda i: (parity, 0, 0)), column, column],
        out_specs=pl.BlockSpec((2, lines, width), lambda i: (i, 0, 0)),
        out_shape=jax.ShapeDtypeStruct((shards, lines, width), F32),
        scratch_shapes=[pltpu.VMEM((lines, depth), BF16)] * 2,
        compiler_params=params(),
        cost_estimate=pl.CostEstimate(flops=6 * lines * depth * depth, bytes_accessed=6 << 20, transcendentals=0),
        name="forward",
    )(fold.reshape(2, lines, depth), table_high, table_low)


def project_kernel(source, mix_high, mix_low, ratio, modal, ends, power):
    layers, rows, width = source.shape

    @pl.when(pl.program_id(0) == 0)
    def _():
        ends[...] = jnp.zeros(ends.shape, F32)
        power[...] = jnp.ones(power.shape, F32)

    tiles = [source[:, 8 * t : 8 * t + 8, :].reshape(8 * layers, width) for t in range(rows // 8)]
    high, low = split(jnp.concatenate(tiles, axis=1))
    mixed = dot(mix_high[...], high) + dot(mix_low[...], high) + dot(mix_high[...], low)
    decay = ratio[...]
    last, first, scale = ends[0], ends[1], power[...]
    for t in range(rows // 8):
        block = mixed[:, t * width : (t + 1) * width].reshape(8, layers, width)
        modal[8 * t : 8 * t + 8] = block
        for row in range(8):
            last = decay * last + block[row]
            first = first + scale * block[row]
            scale = scale * decay
    ends[0] = last
    ends[1] = first
    power[...] = scale


def project(stacked, mix_high, mix_low, ratio):
    layers, rows, width = stacked.shape
    step = 16
    whole = pl.BlockSpec(mix_high.shape, lambda i: (0, 0))
    return pl.pallas_call(
        project_kernel,
        grid=(rows // step,),
        in_specs=[
            pl.BlockSpec((layers, step, width), lambda i: (0, i, 0)),
            whole,
            whole,
            pl.BlockSpec((layers, width), lambda i: (0, 0)),
        ],
        out_specs=[
            pl.BlockSpec((step, layers, width), lambda i: (i, 0, 0)),
            pl.BlockSpec((2, layers, width), lambda i: (0, 0, 0)),
        ],
        out_shape=[
            jax.ShapeDtypeStruct((rows, layers, width), F32),
            jax.ShapeDtypeStruct((2, layers, width), F32),
        ],
        scratch_shapes=[pltpu.VMEM((layers, width), F32)],
        compiler_params=params(),
        name="project",
    )(stacked, mix_high, mix_low, ratio)


def solve_kernel(modal, carry, ratio, scale, mix_high, mix_low, result, down, up):
    rows, layers, width = modal.shape
    step = result.shape[1]
    decay = ratio[...]

    @pl.when(pl.program_id(0) == 0)
    def _():
        def forth(row, value):
            value = decay * value + modal[row]
            down[row] = value
            return value

        lax.fori_loop(0, rows, forth, carry[0], unroll=8)
        up[...] = carry[1]

    base = rows - step * (pl.program_id(0) + 1)
    beyond, factor = up[...], scale[...]
    solved = [None] * step
    for row in range(step - 1, -1, -1):
        value = decay * beyond
        beyond = modal[base + row] + value
        solved[row] = factor * (down[base + row] + value)
    up[...] = beyond
    tiles = [
        jnp.stack(solved[8 * t : 8 * t + 8]).reshape(8 * layers, width) for t in range(step // 8)
    ]
    high, low = split(jnp.concatenate(tiles, axis=1))
    mixed = dot(mix_high[...], high) + dot(mix_low[...], high) + dot(mix_high[...], low)
    for t in range(step // 8):
        result[:, 8 * t : 8 * t + 8, :] = mixed[:, t * width : (t + 1) * width].reshape(layers, 8, width)


def solve(modal, carry, ratio, scale, mix_high, mix_low):
    rows, layers, width = modal.shape
    step = 16
    whole = pl.BlockSpec(mix_high.shape, lambda i: (0, 0))
    field = pl.BlockSpec((layers, width), lambda i: (0, 0))
    return pl.pallas_call(
        solve_kernel,
        grid=(rows // step,),
        in_specs=[
            pl.BlockSpec((rows, layers, width), lambda i: (0, 0, 0)),
            pl.BlockSpec((2, layers, width), lambda i: (0, 0, 0)),
            field,
            field,
            whole,
            whole,
        ],
        out_specs=pl.BlockSpec((layers, step, width), lambda i: (0, rows // step - 1 - i, 0)),
        out_shape=jax.ShapeDtypeStruct((layers, rows, width), F32),
        scratch_shapes=[pltpu.VMEM((rows, layers, width), F32), pltpu.VMEM((layers, width), F32)],
        compiler_params=params(),
        name="solve",
    )(modal, carry, ratio, scale, mix_high, mix_low)


def gather_split(source, high, low):
    width = source.shape[2]
    for part in range(source.shape[0]):
        high[:, part * width : (part + 1) * width], low[:, part * width : (part + 1) * width] = split(source[part])


def inverse_odd_kernel(source, table_high, table_low, result, high, low):
    @pl.when(pl.program_id(0) == 0)
    def _():
        gather_split(source, high, low)

    value = dot(high[...], table_high[...]) + dot(low[...], table_high[...]) + dot(high[...], table_low[...])
    result[...] = value * alternating(value.shape[1])


def inverse_odd(source, table_high, table_low):
    shards, lines, width = source.shape
    depth = shards * width
    step = 256
    column = pl.BlockSpec((depth, step), lambda i: (0, i))
    return pl.pallas_call(
        inverse_odd_kernel,
        grid=(depth // step,),
        in_specs=[pl.BlockSpec(source.shape, lambda i: (0, 0, 0)), column, column],
        out_specs=pl.BlockSpec((lines, step), lambda i: (0, i)),
        out_shape=jax.ShapeDtypeStruct((lines, depth), F32),
        scratch_shapes=[pltpu.VMEM((lines, depth), BF16)] * 2,
        compiler_params=params(),
        name="inverse_odd",
    )(source, table_high, table_low)


def inverse_even_kernel(source, odd, table_high, table_low, result, high, low):
    @pl.when(pl.program_id(0) == 0)
    def _():
        gather_split(source, high, low)

    value = dot(high[...], table_high[...]) + dot(low[...], table_high[...]) + dot(high[...], table_low[...])
    step = value.shape[1]
    count = result.shape[1] // step
    index = pl.program_id(0)
    result[:, pl.ds(pl.multiple_of(index * step, step), step)] = odd[...] + value
    result[:, pl.ds(pl.multiple_of((count - 1 - index) * step, step), step)] = flip_lanes(odd[...] - value)


def inverse_even(source, odd, table_high, table_low):
    shards, lines, width = source.shape
    depth = shards * width
    step = 256
    column = pl.BlockSpec((depth, step), lambda i: (0, i))
    return pl.pallas_call(
        inverse_even_kernel,
        grid=(depth // step,),
        in_specs=[
            pl.BlockSpec(source.shape, lambda i: (0, 0, 0)),
            pl.BlockSpec((lines, step), lambda i: (0, i)),
            column,
            column,
        ],
        out_specs=pl.BlockSpec((lines, 2 * depth), lambda i: (0, 0)),
        out_shape=jax.ShapeDtypeStruct((lines, 2 * depth), F32),
        scratch_shapes=[pltpu.VMEM((lines, depth), BF16)] * 2,
        compiler_params=params(),
        name="inverse_even",
    )(source, odd, table_high, table_low)


def interface(ends, theta, rows):
    blocks = lax.axis_size("row")
    me = lax.axis_index("row")
    unit = rows * theta

    def decay(count):
        return jnp.exp(-unit * count.astype(F32))

    from_above = jnp.zeros_like(theta)
    from_below = jnp.zeros_like(theta)
    group = 1
    total = ends
    for radix in (2, 4, 4):
        place = (me // group) % radix
        inside = me % group
        parts = [total]
        for shift in range(1, radix):
            pairs = []
            for target in range(blocks):
                spot = (target // group) % radix
                pairs.append((target + ((spot + shift) % radix - spot) * group, target))
            parts.append(lax.ppermute(total, "row", pairs))
        last = jnp.zeros_like(theta)
        first = jnp.zeros_like(theta)
        for shift, part in enumerate(parts):
            spot = (place + shift) % radix
            last = last + decay(group * (radix - 1 - spot)) * part[0]
            first = first + decay(group * spot) * part[1]
            if shift:
                above = jnp.where(spot < place, decay(jnp.maximum(group * (place - 1 - spot), 0) + inside), 0.0)
                below = jnp.where(spot > place, decay(jnp.maximum(group * (spot - place - 1), 0) + group - 1 - inside), 0.0)
                from_above = from_above + above * part[0]
                from_below = from_below + below * part[1]
        total = jnp.stack([last, first])
        group *= radix
    span = jnp.exp(-theta * (rows * blocks + 1))
    wall = jnp.exp(-theta) / (1.0 - span * span)
    from_above = from_above + decay(me) * wall * (span * total[0] - total[1])
    from_below = from_below + decay(blocks - 1 - me) * wall * (span * total[1] - total[0])
    return jnp.stack([from_above, from_below])


def block_mix(weights, to_modes):
    count = weights.shape[0]
    eye = jnp.eye(8, dtype=F32)
    if to_modes:
        big = eye[:, None, None, :] * weights[None, :, :, None]
    else:
        big = weights[:, None, None, :] * eye[None, :, :, None]
    big = big.reshape(8 * count, 8 * count)
    high = lax.reduce_precision(big, 8, 7)
    return high.astype(BF16), (big - high).astype(BF16)


def on_device(q_prev, q_now, psi_now, layers_to_modes, modes_to_layers, stretch):
    layer_count, row_count, col_count = q_prev.shape
    blocks = lax.axis_size("row")
    shards = lax.axis_size("layer")
    me = lax.axis_index("row")
    table_high, table_low = (jnp.asarray(value) for value in half_table(col_count))

    last = jnp.concatenate([psi_now[:, -1:], q_now[:, -1:], q_prev[:, -2:]], axis=1)
    initial = jnp.concatenate([psi_now[:, :1], q_now[:, :1], q_prev[:, :2]], axis=1)
    up = [(i, i + 1) for i in range(blocks - 1)]
    down = [(j, i) for i, j in up]
    top = lax.ppermute(last, "row", up)
    bottom = lax.ppermute(initial, "row", down)
    edge = jnp.stack([me > 0, me < blocks - 1]).astype(F32)
    q_next, fold = stencil(edge, q_prev, q_now, psi_now, top, bottom)

    to_modes = block_mix(layers_to_modes, True)
    to_layers = block_mix(modes_to_layers, False)
    eigen = jnp.asarray(column_eigen(col_count, shards))
    eigen = lax.dynamic_index_in_dim(eigen, lax.axis_index("layer"), 1, keepdims=False)
    shift = eigen[:, None, :] + stretch[None, :, None]
    theta = 2.0 * jnp.arcsinh(0.5 * jnp.sqrt(shift))
    ratio = jnp.exp(-theta)
    scale = (-2.0 / (col_count + 1)) / jnp.sqrt(shift * (4.0 + shift))

    returned = []
    for chunk in range(2):
        spectrum = forward(fold, chunk, table_high, table_low, shards)
        stacked = lax.all_to_all(spectrum, "layer", split_axis=0, concat_axis=0, tiled=True)
        stacked = stacked.reshape(shards * layer_count, row_count, -1)
        modal, ends = project(stacked, *to_modes, ratio[chunk])
        carry = interface(ends, theta[chunk], row_count)
        layered = solve(modal, carry, ratio[chunk], scale[chunk], *to_layers)
        layered = layered.reshape(shards, layer_count * row_count, -1)
        returned.append(lax.all_to_all(layered, "layer", split_axis=0, concat_axis=0, tiled=True))
    odd = inverse_odd(returned[0], table_high, table_low)
    psi_next = inverse_even(returned[1], odd, table_high, table_low)
    return (q_next, psi_next.reshape(q_prev.shape))


def solution(mesh):
    return jax.shard_map(
        on_device,
        mesh=mesh,
        in_specs=(
            P("layer", "row", None),
            P("layer", "row", None),
            P("layer", "row", None),
            P(),
            P(),
            P(),
        ),
        out_specs=(P("layer", "row", None), P("layer", "row", None)),
        check_vma=False,
    )
```

time: 597 us -> 173 us (0.29); the launches traced: 585 us -> 171 us
  matrix products: 174 us -> 0 us
  blocking collectives: 126 us -> 0 us
  local copies, waits for them, and re-layouts: 108 us -> 21.9 us
  waiting for transfers between devices: 94 us -> 29.1 us
  Pallas kernels: 0 us -> 48.5 us
  other arithmetic: 48.2 us -> 12.9 us
  starting transfers between devices: 33.6 us -> 58 us
    dot_general x10 -> x0, matrix products: 174 us -> none  [the longest x1 21.7 us: inverse_columns(): jnp.einsum('mkr,jk->mrj', source[:, :half_len], even_tab, precision=HIGHEST)]
    all_to_all x3 -> x0, blocking collectives: 126 us -> none  [the longest x1 52 us: on_device(): lax.all_to_all(row_physical, 'row', split_axis=2, concat_axis=1, tiled=True)]
    all_to_all x3 -> x4, waiting for transfers between devices: 93.1 us -> 15.7 us  [the longest x2 10.6 us: on_device(): lax.all_to_all(spectrum, 'layer', split_axis=0, concat_axis=0, tiled=True)]
    pallas_call x0 -> x9, Pallas kernels: none -> 48.5 us  [the longest x1 20.1 us: stencil(): pl.pallas_call(stencil_kernel, grid=(layers,), in_specs=[pl.BlockSpec(mem...]
    all_to_all x11 -> x0, local copies, waits for them, and re-layouts: 37.5 us -> none  [the longest x3 12.2 us: on_device(): lax.all_to_all(column_spectra, 'row', split_axis=1, concat_axis=2, tiled=...]
    ppermute x4 -> x16, starting transfers between devices: 9.25 us -> 35.5 us  [the longest x14 32.5 us: interface(): parts.append(lax.ppermute(total, 'row', pairs))]
    unnamed x42 -> x43, local copies, waits for them, and re-layouts: 34.2 us -> 12.8 us
    all_to_all x2 -> x0, other arithmetic: 17.4 us -> none  [the longest x1 8.69 us: on_device(): lax.all_to_all(row_physical, 'row', split_axis=2, concat_axis=1, tiled=True)]
  transfers between devices with their start and end apart: 7 -> 20, of which waited for: 4 -> 12; matrix products, arithmetic and copies ran while one was open for 2% -> 8% of each run, Pallas kernels for 0% -> 8%
where the time goes in v1:
time: 173 us; the launch traced here: 171 us
  starting transfers between devices  58 us (34%)
  Pallas kernels  48.5 us (28%)
  waiting for transfers between devices  29.1 us (17%)
  local copies, waits for them, and re-layouts  21.9 us (13%)
  other arithmetic  12.9 us (7%)
    ppermute x14, starting transfers between devices, interface(): parts.append(lax.ppermute(total, 'row', pairs))  32.5 us
    pallas_call x1, Pallas kernels, stencil(): pl.pallas_call(stencil_kernel, grid=(layers,), in_specs=[pl.BlockSpec(mem...  20.1 us
    unnamed x43, local copies, waits for them, and re-layouts  12.8 us
    all_to_all x2, starting transfers between devices, on_device(): lax.all_to_all(spectrum, 'layer', split_axis=0, concat_axis=0, tiled=True)  11.6 us
    all_to_all x2, starting transfers between devices, on_device(): lax.all_to_all(layered, 'layer', split_axis=0, concat_axis=0, tiled=True)  10.9 us
    all_to_all x2, waiting for transfers between devices, on_device(): lax.all_to_all(spectrum, 'layer', split_axis=0, concat_axis=0, tiled=True)  10.6 us
    ppermute x14, waiting for transfers between devices, interface(): parts.append(lax.ppermute(total, 'row', pairs))  10.3 us
    pallas_call x2, Pallas kernels, forward(): pl.pallas_call(forward_kernel, grid=(depth // step,), in_specs=[pl.BlockS...  9.9 us
  transfers between devices with their start and end apart: 20, of which 12 were waited for; matrix products, arithmetic and copies ran while one was open for 8% of the time, Pallas kernels for 8%

profile of v1, /device:TPU:32, one launch (start us, length us, event | category | flops | bytes accessed | tf_op | source)
XLA Modules:
  0.0 171.4 jit_solution(984942849330666784)
XLA Ops:
  0.6 1.1 fusion.23
  1.7 1.3 fusion.21
  3.1 1.7 %collective-permute-start = (f32[4,4,2048]{2,1,0:T(4,128)S(1)}, f32[4,4,2048]{2,1,0:T(4,128)S(1)}, u32[]{:S(2)}, u32[]{:S(2)}) collective-permute-start(f32[4,4,2048]{2,1,0:T(4,128)S(1)} %pad_maximum_fusion), channel_id=1, source_target_pairs={{0,1},{1,2},{2,3},{3,4},{4,5},{5,6},{6,7},{7,8},{8,9},{9,10},{10,1... | collective-permute-start | bytes 393224 | tf_op jit(solution)/shard_map/ppermute | solution.py:427
  5.0 1.3 collective-permute-start.1
  6.3 3.1 %collective-permute-done.1.bottom = f32[4,4,2048]{2,1,0:T(4,128)S(1)} collective-permute-done((f32[4,4,2048]{2,1,0:T(4,128)S(1)}, f32[4,4,2048]{2,1,0:T(4,128)S(1)}, u32[]{:S(2)}, u32[]{:S(2)}) %collective-permute-start.1) | collective-permute-done | bytes 131104 | tf_op jit(solution)/shard_map/ppermute | solution.py:428
  9.5 1.6 copy-done.7
  11.1 20.1 %stencil.1 = (f32[4,64,2048]{2,1,0:T(8,128)}, f32[2,4,64,1024]{3,2,1,0:T(8,128)S(1)}) custom-call(f32[2]{0:T(128)S(1)} %add_convert_fusion.edge, f32[4,64,2048]{2,1,0:T(8,128)S(1)} %copy-done.7, f32[4,64,2048]{2,1,0:T(8,128)} %now.1, f32[4,64,2048]{2,1,0:T(8,128)} %psi.1, f32[4,4,2048]{2,1,0:T(4,128)S(1)} %collective-permute-done.top, ...), custom_call_target="tpu_custom_call" | custom-call | tf_op jit(solution)/shard_map/stencil/pallas_call | solution.py:142
  31.2 4.9 %forward.3 = f32[8,256,128]{2,1,0:T(8,128)} custom-call(f32[2,256,1024]{2,1,0:T(8,128)S(1)} %bitcast.24, bf16[1024,1024]{1,0:T(8,128)(2,1)S(1)} %copy-done, bf16[1024,1024]{1,0:T(8,128)(2,1)} %constant.223.clone.table_low), custom_call_target="tpu_custom_call" | custom-call | flops 1610612736 | bytes 6291456 | tf_op jit(solution)/shard_map/forward/pallas_call | solution.py:174
  36.1 1.3 copy-done.1
  37.4 5.9 %all-to-all-start.2 = ((f32[8,256,128]{2,1,0:T(8,128)}), f32[8,256,128]{2,1,0:T(8,128)S(1)}, u32[]{:S(2)}, u32[]{:S(2)}) async-start(f32[8,256,128]{2,1,0:T(8,128)} %forward.3), calls=%async_computation.2 | async-start | bytes 2097152 | tf_op jit(solution)/shard_map/all_to_all | solution.py:444
  43.4 1.6 copy-done.2
  45.0 5.0 %forward.2 = f32[8,256,128]{2,1,0:T(8,128)} custom-call(f32[2,256,1024]{2,1,0:T(8,128)S(1)} %bitcast.25, bf16[1024,1024]{1,0:T(8,128)(2,1)S(1)} %copy-done, bf16[1024,1024]{1,0:T(8,128)(2,1)} %constant.223.clone.table_low), custom_call_target="tpu_custom_call" | custom-call | flops 1610612736 | bytes 6291456 | tf_op jit(solution)/shard_map/forward/pallas_call | solution.py:174
  49.9 6.7 %all-to-all-done.2 = f32[8,256,128]{2,1,0:T(8,128)S(1)} async-done(((f32[8,256,128]{2,1,0:T(8,128)}), f32[8,256,128]{2,1,0:T(8,128)S(1)}, u32[]{:S(2)}, u32[]{:S(2)}) %all-to-all-start.2) | async-done | bytes 1048608 | tf_op jit(solution)/shard_map/all_to_all | solution.py:444
  56.6 1.0 copy-done.3
  57.6 5.7 %all-to-all-start = ((f32[8,256,128]{2,1,0:T(8,128)}), f32[8,256,128]{2,1,0:T(8,128)S(1)}, u32[]{:S(2)}, u32[]{:S(2)}) async-start(f32[8,256,128]{2,1,0:T(8,128)} %forward.2), calls=%async_computation | async-start | bytes 2097152 | tf_op jit(solution)/shard_map/all_to_all | solution.py:444
  63.3 0.7 copy.14
  64.0 1.2 broadcast_multiply_fusion.1
  65.2 1.5 mul.1098
  66.7 0.8 copy.12
  67.6 0.7 dynamic-slice_bitcast_fusion
  68.2 0.7 fusion.19
  69.0 1.0 fusion
  69.9 1.2 copy-done.4
  71.2 1.3 project.3
  72.5 1.0 copy-done.10
  73.5 1.3 collective-permute-start.9
  74.7 3.9 %all-to-all-done = f32[8,256,128]{2,1,0:T(8,128)S(1)} async-done(((f32[8,256,128]{2,1,0:T(8,128)}), f32[8,256,128]{2,1,0:T(8,128)S(1)}, u32[]{:S(2)}, u32[]{:S(2)}) %all-to-all-start) | async-done | bytes 1048608 | tf_op jit(solution)/shard_map/all_to_all | solution.py:444
  78.7 1.3 project.2
  80.0 1.0 copy-done.8
  81.3 1.8 %broadcast_multiply_fusion = f32[32,8,8,32]{3,2,1,0:T(8,128)} fusion(f32[8,8]{1,0:T(8,128)} %copy.14, f32[32,32]{1,0:T(8,128)S(1)} %copy-done.18), kind=kLoop, calls=%fused_computation | loop fusion | flops 65536 | bytes 266496 | tf_op jit(solution)/shard_map/mul | solution.py:410
  83.2 2.2 %mul.1250 = f32[256,256]{1,0:T(8,128)} reshape(f32[32,8,8,32]{3,2,1,0:T(8,128)} %broadcast_multiply_fusion) | data formatting | bytes 524288 | tf_op jit(solution)/shard_map/mul | solution.py:410
  85.4 1.4 multiply_add_fusion.7
  87.4 4.2 %collective-permute-start.12 = (f32[2,32,128]{2,1,0:T(8,128)}, f32[2,32,128]{2,1,0:T(8,128)S(1)}, u32[]{:S(2)}, u32[]{:S(2)}) collective-permute-start(f32[2,32,128]{2,1,0:T(8,128)} %pad_maximum_fusion.5), channel_id=1, source_target_pairs={{6,0},{7,1},{0,2},{1,3},{2,4},{3,5},{4,6},{5,7},{14,8},{15,9},{8,1... | collective-permute-start | bytes 98312 | tf_op jit(solution)/shard_map/ppermute | solution.py:383
  91.6 1.6 collective-permute-start.11
  93.2 2.7 %collective-permute-start.10 = (f32[2,32,128]{2,1,0:T(8,128)}, f32[2,32,128]{2,1,0:T(8,128)}, u32[]{:S(2)}, u32[]{:S(2)}) collective-permute-start(f32[2,32,128]{2,1,0:T(8,128)} %pad_maximum_fusion.5), channel_id=1, source_target_pairs={{2,0},{3,1},{4,2},{5,3},{6,4},{7,5},{0,6},{1,7},{10,8},{11,9},{12,... | collective-permute-start | bytes 98312 | tf_op jit(solution)/shard_map/ppermute | solution.py:383
  95.9 1.0 fusion.1
  97.8 0.8 multiply_add_fusion.5
  99.3 3.3 %collective-permute-start.15 = (f32[2,32,128]{2,1,0:T(8,128)}, f32[2,32,128]{2,1,0:T(8,128)}, u32[]{:S(2)}, u32[]{:S(2)}) collective-permute-start(f32[2,32,128]{2,1,0:T(8,128)} %pad_maximum_fusion.6), channel_id=1, source_target_pairs={{24,0},{25,1},{26,2},{27,3},{28,4},{29,5},{30,6},{31,7},{0,8},{1,9... | collective-permute-start | bytes 98312 | tf_op jit(solution)/shard_map/ppermute | solution.py:383
  102.6 4.5 %collective-permute-start.14 = (f32[2,32,128]{2,1,0:T(8,128)}, f32[2,32,128]{2,1,0:T(8,128)}, u32[]{:S(2)}, u32[]{:S(2)}) collective-permute-start(f32[2,32,128]{2,1,0:T(8,128)} %pad_maximum_fusion.6), channel_id=1, source_target_pairs={{16,0},{17,1},{18,2},{19,3},{20,4},{21,5},{22,6},{23,7},{24,8},{25... | collective-permute-start | bytes 98312 | tf_op jit(solution)/shard_map/ppermute | solution.py:383
  107.1 2.7 %collective-permute-start.13 = (f32[2,32,128]{2,1,0:T(8,128)}, f32[2,32,128]{2,1,0:T(8,128)}, u32[]{:S(2)}, u32[]{:S(2)}) collective-permute-start(f32[2,32,128]{2,1,0:T(8,128)} %pad_maximum_fusion.6), channel_id=1, source_target_pairs={{8,0},{9,1},{10,2},{11,3},{12,4},{13,5},{14,6},{15,7},{16,8},{17,9... | collective-permute-start | bytes 98312 | tf_op jit(solution)/shard_map/ppermute | solution.py:383
  109.7 0.7 slice_bitcast_fusion
  110.8 1.5 collective-permute-done.13
  112.3 0.9 multiply_add_fusion
  113.2 1.0 multiply_add_fusion.1
  114.2 2.7 %solve.3 = f32[32,64,128]{2,1,0:T(8,128)} custom-call(f32[64,32,128]{2,1,0:T(8,128)S(1)} %copy-done.11, f32[2,32,128]{2,1,0:T(8,128)S(1)} %pad_maximum_fusion.7.carry, f32[32,128]{1,0:T(8,128)S(1)} %get-tuple-element.36.ratio, f32[32,128]{1,0:T(8,128)S(1)} %get-tuple-element.32.scale, bf16[256,256]{1,0:T(8,128)(2,1)S(1)} %get-tuple-element.21.mix_high, ...), custom_call_target="tpu_custom_call" | custom-call | tf_op jit(solution)/shard_map/solve/pallas_call | solution.py:276
  116.9 4.9 %all-to-all-start.3 = ((f32[8,256,128]{2,1,0:T(8,128)}), f32[8,256,128]{2,1,0:T(8,128)S(1)}, u32[]{:S(2)}, u32[]{:S(2)}) async-start(f32[8,256,128]{2,1,0:T(8,128)} %bitcast.11), calls=%async_computation.3 | async-start | bytes 2097152 | tf_op jit(solution)/shard_map/all_to_all | solution.py:450
  121.8 1.7 collective-permute-start.5
  123.5 3.4 %collective-permute-start.4 = (f32[2,32,128]{2,1,0:T(8,128)S(1)}, f32[2,32,128]{2,1,0:T(8,128)S(1)}, u32[]{:S(2)}, u32[]{:S(2)}) collective-permute-start(f32[2,32,128]{2,1,0:T(8,128)S(1)} %pad_maximum_fusion.2), channel_id=1, source_target_pairs={{4,0},{5,1},{6,2},{7,3},{0,4},{1,5},{2,6},{3,7},{12,8},{13,9},{14,... | collective-permute-start | bytes 98312 | tf_op jit(solution)/shard_map/ppermute | solution.py:383
  127.3 1.8 %collective-permute-done.4 = f32[2,32,128]{2,1,0:T(8,128)S(1)} collective-permute-done((f32[2,32,128]{2,1,0:T(8,128)S(1)}, f32[2,32,128]{2,1,0:T(8,128)S(1)}, u32[]{:S(2)}, u32[]{:S(2)}) %collective-permute-start.4) | collective-permute-done | bytes 32800 | tf_op jit(solution)/shard_map/ppermute | solution.py:383
  129.2 1.7 collective-permute-done.3
  130.9 1.8 %collective-permute-start.8 = (f32[2,32,128]{2,1,0:T(8,128)S(1)}, f32[2,32,128]{2,1,0:T(8,128)S(1)}, u32[]{:S(2)}, u32[]{:S(2)}) collective-permute-start(f32[2,32,128]{2,1,0:T(8,128)S(1)} %pad_maximum_fusion.3), channel_id=1, source_target_pairs={{24,0},{25,1},{26,2},{27,3},{28,4},{29,5},{30,6},{31,7},{0,8},{1,9... | collective-permute-start | bytes 98312 | tf_op jit(solution)/shard_map/ppermute | solution.py:383
  132.7 4.5 %collective-permute-start.7 = (f32[2,32,128]{2,1,0:T(8,128)S(1)}, f32[2,32,128]{2,1,0:T(8,128)S(1)}, u32[]{:S(2)}, u32[]{:S(2)}) collective-permute-start(f32[2,32,128]{2,1,0:T(8,128)S(1)} %pad_maximum_fusion.3), channel_id=1, source_target_pairs={{16,0},{17,1},{18,2},{19,3},{20,4},{21,5},{22,6},{23,7},{24,8},{25... | collective-permute-start | bytes 98312 | tf_op jit(solution)/shard_map/ppermute | solution.py:383
  137.8 2.8 %collective-permute-done.7 = f32[2,32,128]{2,1,0:T(8,128)S(1)} collective-permute-done((f32[2,32,128]{2,1,0:T(8,128)S(1)}, f32[2,32,128]{2,1,0:T(8,128)S(1)}, u32[]{:S(2)}, u32[]{:S(2)}) %collective-permute-start.7) | collective-permute-done | bytes 32800 | tf_op jit(solution)/shard_map/ppermute | solution.py:383
  140.6 1.6 collective-permute-done.6
  142.1 0.8 multiply_add_fusion.8
  142.9 0.8 multiply_add_fusion.9
  143.8 1.2 copy-done.9
  145.0 2.5 %solve.2 = f32[32,64,128]{2,1,0:T(8,128)} custom-call(f32[64,32,128]{2,1,0:T(8,128)S(1)} %copy-done.9, f32[2,32,128]{2,1,0:T(8,128)S(1)} %pad_maximum_fusion.4.carry, f32[32,128]{1,0:T(8,128)S(1)} %get-tuple-element.37.ratio, f32[32,128]{1,0:T(8,128)S(1)} %get-tuple-element.33.scale, bf16[256,256]{1,0:T(8,128)(2,1)S(1)} %get-tuple-element.21.mix_high, ...), custom_call_target="tpu_custom_call" | custom-call | tf_op jit(solution)/shard_map/solve/pallas_call | solution.py:276
  147.5 5.9 %all-to-all-start.1 = ((f32[8,256,128]{2,1,0:T(8,128)}), f32[8,256,128]{2,1,0:T(8,128)}, u32[]{:S(2)}, u32[]{:S(2)}) async-start(f32[8,256,128]{2,1,0:T(8,128)} %bitcast.7), calls=%async_computation.1 | async-start | bytes 2097152 | tf_op jit(solution)/shard_map/all_to_all | solution.py:450
  153.5 4.4 %inverse_odd.1.odd = f32[256,1024]{1,0:T(8,128)S(1)} custom-call(f32[8,256,128]{2,1,0:T(8,128)S(1)} %all-to-all-done.3.source, bf16[1024,1024]{1,0:T(8,128)(2,1)S(1)} %copy-done, bf16[1024,1024]{1,0:T(8,128)(2,1)} %constant.223.clone.table_low), custom_call_target="tpu_custom_call" | custom-call | tf_op jit(solution)/shard_map/inverse_odd/pallas_call | solution.py:315
  157.9 1.0 copy-done.5
  158.8 5.1 %all-to-all-done.1.source = f32[8,256,128]{2,1,0:T(8,128)} async-done(((f32[8,256,128]{2,1,0:T(8,128)}), f32[8,256,128]{2,1,0:T(8,128)}, u32[]{:S(2)}, u32[]{:S(2)}) %all-to-all-start.1) | async-done | bytes 1048608 | tf_op jit(solution)/shard_map/all_to_all | solution.py:450
  163.9 1.2 copy-done.6
  165.1 6.3 %inverse_even.1 = f32[256,2048]{1,0:T(8,128)} custom-call(f32[8,256,128]{2,1,0:T(8,128)} %all-to-all-done.1.source, f32[256,1024]{1,0:T(8,128)S(1)} %copy-done.6, bf16[1024,1024]{1,0:T(8,128)(2,1)S(1)} %copy-done, bf16[1024,1024]{1,0:T(8,128)(2,1)} %constant.223.clone.table_low), custom_call_target="tpu_custom_call" | custom-call | tf_op jit(solution)/shard_map/inverse_even/pallas_call | solution.py:345
  (59 shorter events, 4.2 us)
Async XLA Ops:
  3.1 3.2 %collective-permute-start = (f32[4,4,2048]{2,1,0:T(4,128)S(1)}, f32[4,4,2048]{2,1,0:T(4,128)S(1)}, u32[]{:S(2)}, u32[]{:S(2)}) collective-permute-start(f32[4,4,2048]{2,1,0:T(4,128)S(1)} %pad_maximum_fusion), channel_id=1, source_target_pairs={{0,1},{1,2},{2,3},{3,4},{4,5},{5,6},{6,7},{7,8},{8,9},{9,10},{10,1... | collective-permute-start | bytes 393224 | tf_op jit(solution)/shard_map/ppermute | solution.py:427
  5.0 4.5 %collective-permute-start.1 = (f32[4,4,2048]{2,1,0:T(4,128)S(1)}, f32[4,4,2048]{2,1,0:T(4,128)S(1)}, u32[]{:S(2)}, u32[]{:S(2)}) collective-permute-start(f32[4,4,2048]{2,1,0:T(4,128)S(1)} %pad_maximum_fusion.1), channel_id=1, source_target_pairs={{1,0},{2,1},{3,2},{4,3},{5,4},{6,5},{7,6},{8,7},{9,8},{10,9},{11,1... | collective-permute-start | bytes 393224 | tf_op jit(solution)/shard_map/ppermute | solution.py:428
  6.3 24.8 %copy-start = (bf16[1024,1024]{1,0:T(8,128)(2,1)S(1)}, bf16[1024,1024]{1,0:T(8,128)(2,1)}, u32[]{:S(2)}) copy-start(bf16[1024,1024]{1,0:T(8,128)(2,1)} %constant.222.clone.table_high) | copy-start | bytes 6291460
  9.5 1.6 copy-start.7
  36.1 1.3 copy-start.1
  37.4 19.2 %all-to-all-start.2 = ((f32[8,256,128]{2,1,0:T(8,128)}), f32[8,256,128]{2,1,0:T(8,128)S(1)}, u32[]{:S(2)}, u32[]{:S(2)}) async-start(f32[8,256,128]{2,1,0:T(8,128)} %forward.3), calls=%async_computation.2 | async-start | bytes 2097152 | tf_op jit(solution)/shard_map/all_to_all | solution.py:444
  43.4 1.6 copy-start.2
  49.9 13.4 %copy-start.19 = (f32[32,32]{1,0:T(8,128)S(1)}, f32[32,32]{1,0:T(8,128)}, u32[]{:S(2)}) copy-start(f32[32,32]{1,0:T(8,128)} %param.12) | copy-start | bytes 12292
  49.9 18.3 %copy-start.20 = (f32[32]{0:T(128)S(1)}, f32[32]{0:T(128)}, u32[]{:S(2)}) copy-start(f32[32]{0:T(128)} %param.14) | copy-start | bytes 388
  56.6 1.0 copy-start.3
  57.6 21.1 %all-to-all-start = ((f32[8,256,128]{2,1,0:T(8,128)}), f32[8,256,128]{2,1,0:T(8,128)S(1)}, u32[]{:S(2)}, u32[]{:S(2)}) async-start(f32[8,256,128]{2,1,0:T(8,128)} %forward.2), calls=%async_computation | async-start | bytes 2097152 | tf_op jit(solution)/shard_map/all_to_all | solution.py:444
  66.7 14.6 %copy-start.18 = (f32[32,32]{1,0:T(8,128)S(1)}, f32[32,32]{1,0:T(8,128)}, u32[]{:S(2)}) copy-start(f32[32,32]{1,0:T(8,128)} %param.13) | copy-start | bytes 12292
  69.9 1.2 copy-start.4
  72.5 1.0 copy-start.10
  73.5 11.9 %collective-permute-start.9 = (f32[2,32,128]{2,1,0:T(8,128)S(1)}, f32[2,32,128]{2,1,0:T(8,128)}, u32[]{:S(2)}, u32[]{:S(2)}) collective-permute-start(f32[2,32,128]{2,1,0:T(8,128)S(1)} %get-tuple-element.13), channel_id=1, source_target_pairs={{1,0},{0,1},{3,2},{2,3},{5,4},{4,5},{7,6},{6,7},{9,8},{8,9},{11,10... | collective-permute-start | bytes 98312 | tf_op jit(solution)/shard_map/ppermute | solution.py:383
  80.0 1.0 copy-start.8
  81.0 33.3 %copy-start.11 = (f32[64,32,128]{2,1,0:T(8,128)S(1)}, f32[64,32,128]{2,1,0:T(8,128)}, u32[]{:S(2)}) copy-start(f32[64,32,128]{2,1,0:T(8,128)} %copy-done.10) | copy-start | bytes 3145732
  81.0 4.5 %collective-permute-start.2 = (f32[2,32,128]{2,1,0:T(8,128)S(1)}, f32[2,32,128]{2,1,0:T(8,128)S(1)}, u32[]{:S(2)}, u32[]{:S(2)}) collective-permute-start(f32[2,32,128]{2,1,0:T(8,128)S(1)} %get-tuple-element.11), channel_id=1, source_target_pairs={{1,0},{0,1},{3,2},{2,3},{5,4},{4,5},{7,6},{6,7},{9,8},{8,9},{11,10... | collective-permute-start | bytes 98312 | tf_op jit(solution)/shard_map/ppermute | solution.py:383
  85.4 7.8 %copy-start.15 = (f32[2,32,128]{2,1,0:T(8,128)}, f32[2,32,128]{2,1,0:T(8,128)S(1)}, u32[]{:S(2)}) copy-start(f32[2,32,128]{2,1,0:T(8,128)S(1)} %collective-permute-done.2) | copy-start | bytes 98308
  86.8 6.4 %copy-start.13 = (f32[1,32,128]{2,1,0:T(8,128)}, f32[1,32,128]{2,1,0:T(8,128)S(1)}, u32[]{:S(2)}) copy-start(f32[1,32,128]{2,1,0:T(8,128)S(1)} %get-tuple-element.28) | copy-start | bytes 49156
  86.8 6.4 %copy-start.14 = (f32[1,32,128]{2,1,0:T(8,128)}, f32[1,32,128]{2,1,0:T(8,128)S(1)}, u32[]{:S(2)}) copy-start(f32[1,32,128]{2,1,0:T(8,128)S(1)} %get-tuple-element.29) | copy-start | bytes 49156
  87.4 9.6 %collective-permute-start.12 = (f32[2,32,128]{2,1,0:T(8,128)}, f32[2,32,128]{2,1,0:T(8,128)S(1)}, u32[]{:S(2)}, u32[]{:S(2)}) collective-permute-start(f32[2,32,128]{2,1,0:T(8,128)} %pad_maximum_fusion.5), channel_id=1, source_target_pairs={{6,0},{7,1},{0,2},{1,3},{2,4},{3,5},{4,6},{5,7},{14,8},{15,9},{8,1... | collective-permute-start | bytes 98312 | tf_op jit(solution)/shard_map/ppermute | solution.py:383
  91.6 5.6 %collective-permute-start.11 = (f32[2,32,128]{2,1,0:T(8,128)}, f32[2,32,128]{2,1,0:T(8,128)S(1)}, u32[]{:S(2)}, u32[]{:S(2)}) collective-permute-start(f32[2,32,128]{2,1,0:T(8,128)} %pad_maximum_fusion.5), channel_id=1, source_target_pairs={{4,0},{5,1},{6,2},{7,3},{0,4},{1,5},{2,6},{3,7},{12,8},{13,9},{14,... | collective-permute-start | bytes 98312 | tf_op jit(solution)/shard_map/ppermute | solution.py:383
  93.2 4.6 %collective-permute-start.10 = (f32[2,32,128]{2,1,0:T(8,128)}, f32[2,32,128]{2,1,0:T(8,128)}, u32[]{:S(2)}, u32[]{:S(2)}) collective-permute-start(f32[2,32,128]{2,1,0:T(8,128)} %pad_maximum_fusion.5), channel_id=1, source_target_pairs={{2,0},{3,1},{4,2},{5,3},{6,4},{7,5},{0,6},{1,7},{10,8},{11,9},{12,... | collective-permute-start | bytes 98312 | tf_op jit(solution)/shard_map/ppermute | solution.py:383
  97.0 12.7 %copy-start.16 = (f32[2,32,128]{2,1,0:T(8,128)}, f32[2,32,128]{2,1,0:T(8,128)S(1)}, u32[]{:S(2)}) copy-start(f32[2,32,128]{2,1,0:T(8,128)S(1)} %collective-permute-done.12) | copy-start | bytes 98308
  97.2 0.6 copy-start.17
  99.3 11.2 %collective-permute-start.15 = (f32[2,32,128]{2,1,0:T(8,128)}, f32[2,32,128]{2,1,0:T(8,128)}, u32[]{:S(2)}, u32[]{:S(2)}) collective-permute-start(f32[2,32,128]{2,1,0:T(8,128)} %pad_maximum_fusion.6), channel_id=1, source_target_pairs={{24,0},{25,1},{26,2},{27,3},{28,4},{29,5},{30,6},{31,7},{0,8},{1,9... | collective-permute-start | bytes 98312 | tf_op jit(solution)/shard_map/ppermute | solution.py:383
  102.6 8.2 %collective-permute-start.14 = (f32[2,32,128]{2,1,0:T(8,128)}, f32[2,32,128]{2,1,0:T(8,128)}, u32[]{:S(2)}, u32[]{:S(2)}) collective-permute-start(f32[2,32,128]{2,1,0:T(8,128)} %pad_maximum_fusion.6), channel_id=1, source_target_pairs={{16,0},{17,1},{18,2},{19,3},{20,4},{21,5},{22,6},{23,7},{24,8},{25... | collective-permute-start | bytes 98312 | tf_op jit(solution)/shard_map/ppermute | solution.py:383
  107.1 5.2 %collective-permute-start.13 = (f32[2,32,128]{2,1,0:T(8,128)}, f32[2,32,128]{2,1,0:T(8,128)}, u32[]{:S(2)}, u32[]{:S(2)}) collective-permute-start(f32[2,32,128]{2,1,0:T(8,128)} %pad_maximum_fusion.6), channel_id=1, source_target_pairs={{8,0},{9,1},{10,2},{11,3},{12,4},{13,5},{14,6},{15,7},{16,8},{17,9... | collective-permute-start | bytes 98312 | tf_op jit(solution)/shard_map/ppermute | solution.py:383
  114.2 7.6 %copy-start.12 = (f32[1,32,128]{2,1,0:T(8,128)S(1)}, f32[1,32,128]{2,1,0:T(8,128)}, u32[]{:S(2)}) copy-start(f32[1,32,128]{2,1,0:T(8,128)} %get-tuple-element.35) | copy-start | bytes 49156
  116.9 30.6 %all-to-all-start.3 = ((f32[8,256,128]{2,1,0:T(8,128)}), f32[8,256,128]{2,1,0:T(8,128)S(1)}, u32[]{:S(2)}, u32[]{:S(2)}) async-start(f32[8,256,128]{2,1,0:T(8,128)} %bitcast.11), calls=%async_computation.3 | async-start | bytes 2097152 | tf_op jit(solution)/shard_map/all_to_all | solution.py:450
  121.8 5.5 %collective-permute-start.5 = (f32[2,32,128]{2,1,0:T(8,128)S(1)}, f32[2,32,128]{2,1,0:T(8,128)S(1)}, u32[]{:S(2)}, u32[]{:S(2)}) collective-permute-start(f32[2,32,128]{2,1,0:T(8,128)S(1)} %pad_maximum_fusion.2), channel_id=1, source_target_pairs={{6,0},{7,1},{0,2},{1,3},{2,4},{3,5},{4,6},{5,7},{14,8},{15,9},{8,1... | collective-permute-start | bytes 98312 | tf_op jit(solution)/shard_map/ppermute | solution.py:383
  123.5 5.7 %collective-permute-start.4 = (f32[2,32,128]{2,1,0:T(8,128)S(1)}, f32[2,32,128]{2,1,0:T(8,128)S(1)}, u32[]{:S(2)}, u32[]{:S(2)}) collective-permute-start(f32[2,32,128]{2,1,0:T(8,128)S(1)} %pad_maximum_fusion.2), channel_id=1, source_target_pairs={{4,0},{5,1},{6,2},{7,3},{0,4},{1,5},{2,6},{3,7},{12,8},{13,9},{14,... | collective-permute-start | bytes 98312 | tf_op jit(solution)/shard_map/ppermute | solution.py:383
  126.9 3.9 %collective-permute-start.3 = (f32[2,32,128]{2,1,0:T(8,128)S(1)}, f32[2,32,128]{2,1,0:T(8,128)S(1)}, u32[]{:S(2)}, u32[]{:S(2)}) collective-permute-start(f32[2,32,128]{2,1,0:T(8,128)S(1)} %pad_maximum_fusion.2), channel_id=1, source_target_pairs={{2,0},{3,1},{4,2},{5,3},{6,4},{7,5},{0,6},{1,7},{10,8},{11,9},{12,... | collective-permute-start | bytes 98312 | tf_op jit(solution)/shard_map/ppermute | solution.py:383
  130.9 6.9 %collective-permute-start.8 = (f32[2,32,128]{2,1,0:T(8,128)S(1)}, f32[2,32,128]{2,1,0:T(8,128)S(1)}, u32[]{:S(2)}, u32[]{:S(2)}) collective-permute-start(f32[2,32,128]{2,1,0:T(8,128)S(1)} %pad_maximum_fusion.3), channel_id=1, source_target_pairs={{24,0},{25,1},{26,2},{27,3},{28,4},{29,5},{30,6},{31,7},{0,8},{1,9... | collective-permute-start | bytes 98312 | tf_op jit(solution)/shard_map/ppermute | solution.py:383
  132.7 7.8 %collective-permute-start.7 = (f32[2,32,128]{2,1,0:T(8,128)S(1)}, f32[2,32,128]{2,1,0:T(8,128)S(1)}, u32[]{:S(2)}, u32[]{:S(2)}) collective-permute-start(f32[2,32,128]{2,1,0:T(8,128)S(1)} %pad_maximum_fusion.3), channel_id=1, source_target_pairs={{16,0},{17,1},{18,2},{19,3},{20,4},{21,5},{22,6},{23,7},{24,8},{25... | collective-permute-start | bytes 98312 | tf_op jit(solution)/shard_map/ppermute | solution.py:383
  137.2 5.0 %collective-permute-start.6 = (f32[2,32,128]{2,1,0:T(8,128)S(1)}, f32[2,32,128]{2,1,0:T(8,128)S(1)}, u32[]{:S(2)}, u32[]{:S(2)}) collective-permute-start(f32[2,32,128]{2,1,0:T(8,128)S(1)} %pad_maximum_fusion.3), channel_id=1, source_target_pairs={{8,0},{9,1},{10,2},{11,3},{12,4},{13,5},{14,6},{15,7},{16,8},{17,9... | collective-permute-start | bytes 98312 | tf_op jit(solution)/shard_map/ppermute | solution.py:383
  143.8 1.2 copy-start.9
  147.5 16.4 %all-to-all-start.1 = ((f32[8,256,128]{2,1,0:T(8,128)}), f32[8,256,128]{2,1,0:T(8,128)}, u32[]{:S(2)}, u32[]{:S(2)}) async-start(f32[8,256,128]{2,1,0:T(8,128)} %bitcast.7), calls=%async_computation.1 | async-start | bytes 2097152 | tf_op jit(solution)/shard_map/all_to_all | solution.py:450
  157.9 1.0 copy-start.5
  163.9 1.2 copy-start.6

commit v2 on v1

v2 whole, which is shorter than its diff:
```python
import functools
import math

import jax
import jax.numpy as jnp
import ml_dtypes
import numpy as np
from jax import lax
from jax.experimental import pallas as pl
from jax.experimental.pallas import tpu as pltpu
from jax.sharding import PartitionSpec as P

TIME_STEP = 0.1
VISCOSITY = 0.02
F32 = jnp.float32
BF16 = jnp.bfloat16
LANES = 128
LAG = 2


def params(megabytes):
    return pltpu.CompilerParams(vmem_limit_bytes=megabytes << 20)


def half_table(length):
    positions = np.arange(1, length // 2 + 1, dtype=np.int64)
    product = (2 * positions[:, None] * positions[None, :]) % (2 * (length + 1))
    table = np.sin(product.astype(np.float64) * (math.pi / (length + 1)))
    high = table.astype(np.float32).astype(ml_dtypes.bfloat16)
    low = (table - high.astype(np.float64)).astype(np.float32).astype(ml_dtypes.bfloat16)
    return high, low


def column_eigen(length, shards):
    positions = np.arange(1, length // 2 + 1, dtype=np.float64)
    waves = np.stack([length + 1 - 2 * positions, 2 * positions])
    eigen = 4.0 * np.sin(waves * (math.pi / (2 * (length + 1)))) ** 2
    eigen = eigen.astype(np.float32).reshape(2, shards, -1)
    return np.concatenate([eigen[0], eigen[1]], axis=1)


def split(value):
    high = value.astype(BF16)
    low = (value - high.astype(F32)).astype(BF16)
    return high, low


def dot(left, right):
    return jnp.dot(left, right, preferred_element_type=F32)


def three_dots(high, low, table_high, table_low):
    return dot(high, table_high) + dot(low, table_high) + dot(high, table_low)


def alternating(shape):
    lane = lax.broadcasted_iota(jnp.int32, shape, 1)
    return jnp.where(lane % 2 == 0, 1.0, -1.0).astype(F32)


def rim_kernel(prev_first, now_first, psi_first, prev_last, now_last, psi_last, initial, last):
    rows = prev_last.shape[1]
    initial[:, 0:1] = psi_first[:, 0:1]
    initial[:, 1:2] = now_first[:, 0:1]
    initial[:, 2:4] = prev_first[:, 0:2]
    last[:, 0:1] = psi_last[:, rows - 1 :]
    last[:, 1:2] = now_last[:, rows - 1 :]
    last[:, 2:4] = prev_last[:, rows - 2 :]


def rims(q_prev, q_now, psi_now):
    layers, rows, cols = q_prev.shape
    first = pl.BlockSpec((layers, 8, cols), lambda i: (0, 0, 0))
    final = pl.BlockSpec((layers, 8, cols), lambda i: (0, rows // 8 - 1, 0))
    rim = jax.ShapeDtypeStruct((layers, 4, cols), F32)
    whole = pl.BlockSpec(rim.shape, lambda i: (0, 0, 0))
    return pl.pallas_call(
        rim_kernel,
        grid=(1,),
        in_specs=[first, first, first, final, final, final],
        out_specs=[whole, whole],
        out_shape=[rim, rim],
        compiler_params=params(62),
        name="rims",
    )(q_prev, q_now, psi_now, q_prev, q_now, psi_now)


def fill(ext, start, source, index, first, rows):
    for c in range(ext.shape[0]):
        ext[c, start : start + rows, :] = source[(*index, slice(first, first + rows), slice(LANES * c, LANES * (c + 1)))]


def shift_columns(source, to_east, to_west):
    count, rows, width = source.shape
    lane = lax.broadcasted_iota(jnp.int32, (rows, width), 1)
    east, west = {count: 0.0}, {-1: 0.0}

    def store(c):
        to_east[c] = jnp.where(lane == width - 1, east[c + 1], east[c])
        to_west[c] = jnp.where(lane == 0, west[c - 1], west[c])

    for c in range(count + LAG):
        if c < count:
            value = source[c]
            east[c] = pltpu.roll(value, width - 1, 1)
            west[c] = pltpu.roll(value, 1, 1)
        if c >= LAG:
            store(c - LAG)


def advance(fields, q_held, high, low, layer, wall):
    p, z, ze, zw, q, qe, qw = fields
    count, _, width = p.shape
    rows = q_held.shape[1]
    lane = lax.broadcasted_iota(jnp.int32, (rows, width), 1)
    third = -2.0 * TIME_STEP / 12.0
    drag = -2.0 * TIME_STEP * VISCOSITY
    middle, east, west = {}, {count: 0.0}, {-1: 0.0}

    def tendency(c):
        def here(ext, row=0):
            return ext[c, 8 + row : 8 + row + rows, :]

        pn, pc, ps = here(p, -1), here(p), here(p, 1)
        zn, zc, zs = here(z, -1), here(z), here(z, 1)
        zne, zce, zse = here(ze, -1), here(ze), here(ze, 1)
        znw, zcw, zsw = here(zw, -1), here(zw), here(zw, 1)
        qc = here(q)
        near = here(q, -1) + here(q, 1)
        far = here(q, -2) + here(q, 2)
        down = zs - zn
        beside = 2.0 * near - 8.0 * qc
        from_east = pc * ((zsw - znw) + down) + ps * (zsw - zc) + pn * (zc - znw)
        from_west = ps * (zc - zse) + pn * (zne - zc) - pc * ((zse - zne) + down)
        from_east = third * from_east + drag * (beside + here(qe))
        from_west = third * from_west + drag * (beside + here(qw))
        east[c] = pltpu.roll(from_east, width - 1, 1)
        west[c] = pltpu.roll(from_west, 1, 1)
        across = zce - zcw
        own = pn * (across + (zne - znw)) - ps * (across + (zse - zsw))
        bulk = far - 8.0 * near + 20.0 * qc - wall * qc
        if c == 0:
            bulk = bulk - jnp.where(lane == 0, qc, 0.0)
        if c == count - 1:
            bulk = bulk - jnp.where(lane == width - 1, qc, 0.0)
        middle[c] = qc + third * own + drag * bulk

    def finish(c):
        value = middle[c] + jnp.where(lane == width - 1, east[c + 1], east[c])
        value = value + jnp.where(lane == 0, west[c - 1], west[c])
        q_held[layer, :, width * c : width * (c + 1)] = value

    for c in range(count + LAG):
        if c < count:
            tendency(c)
        if c >= LAG:
            finish(c - LAG)

    order = width - 1 - lane
    sign = alternating((rows, width))
    pairs = {}

    def load(c):
        upper = q_held[layer, :, width * (count - 1 - c) : width * (count - c)]
        pairs[c] = q_held[layer, :, width * c : width * (c + 1)], jnp.take_along_axis(upper, order, axis=1)

    def store(c):
        lower, upper = pairs[c]
        column = slice(width * c, width * (c + 1))
        for parity, value in enumerate(((lower + upper) * sign, lower - upper)):
            line = pl.ds(pl.multiple_of((parity * q_held.shape[0] + layer) * rows, rows), rows)
            high[line, column], low[line, column] = split(value)

    for c in range(count // 2 + LAG):
        if c < count // 2:
            load(c)
        if c >= LAG:
            store(c - LAG)


def step_kernel(blocks, place, prev, now, psi, top, bottom, table_high, table_low, q_out, spectrum, *scratch):
    fields, q_held, p, z, ze, zw, q, qe, qw, high, low, held, sems, q_sems, sems_out = scratch
    layers, rows, _ = prev.shape
    shards, lines, width = held.shape
    width //= 2
    count = table_high.shape[1] // width
    index = pl.program_id(0)

    def load(layer, which):
        source = (psi, now, prev)[which]
        return pltpu.make_async_copy(source.at[layer], fields.at[layer, which], sems.at[layer, which])

    def save(layer):
        return pltpu.make_async_copy(q_held.at[layer], q_out.at[layer], q_sems.at[layer])

    def send(step):
        block = pl.ds(step * count, count)
        return pltpu.make_async_copy(held.at[block], spectrum.at[block], sems_out.at[step])

    @pl.when(index == 0)
    def _():
        for layer in range(2):
            for which in range(3):
                load(layer, which).start()

    @pl.when(index < layers)
    def _():
        for which in range(3):
            load(index, which).wait()

        @pl.when(index + 2 < layers)
        def _():
            for which in range(3):
                load(index + 2, which).start()

        for which, ext in enumerate((p, z, q)):
            fill(ext, 8, fields, (index, which), 0, rows)
            first, size = ((0, 1), (1, 1), (2, 2))[which]
            fill(ext, 8 - size, top, (index,), first, size)
            fill(ext, 8 + rows, bottom, (index,), first, size)
        shift_columns(z, ze, zw)
        shift_columns(q, qe, qw)
        row = lax.broadcasted_iota(jnp.int32, (rows, LANES), 0)
        wall_above = jnp.where(place[0] == 0, 0, -1)
        wall_below = jnp.where(place[0] == blocks - 1, rows - 1, -1)
        wall = jnp.where((row == wall_above) | (row == wall_below), 1.0, 0.0).astype(F32)
        advance((p, z, ze, zw, q, qe, qw), q_held, high, low, index, wall)
        save(index).start()

    @pl.when(index >= layers)
    def _():
        step = index - layers
        value = three_dots(high[...], low[...], table_high[...], table_low[...])
        for part in range(count):
            column = slice(part * width, (part + 1) * width)
            held[step * count + part, :, :width] = value[:lines, column]
            held[step * count + part, :, width:] = value[lines:, column]
        send(step).start()

    @pl.when(index == pl.num_programs(0) - 1)
    def _():
        for layer in range(layers):
            save(layer).wait()
        for step in range(shards // count):
            send(step).wait()


def step_forward(place, q_prev, q_now, psi_now, top, bottom, table_high, table_low, shards, blocks):
    layers, rows, cols = q_prev.shape
    depth = cols // 2
    lines = layers * rows
    width = depth // shards
    step = 2 * width
    steps = depth // step
    hbm = pl.BlockSpec(memory_space=pltpu.HBM)
    rim = pl.BlockSpec((layers, 4, cols), lambda i: (0, 0, 0))
    column = pl.BlockSpec((depth, step), lambda i: (0, jnp.maximum(i - layers, 0)))
    return pl.pallas_call(
        functools.partial(step_kernel, blocks),
        grid=(layers + steps,),
        in_specs=[pl.BlockSpec(memory_space=pltpu.SMEM), hbm, hbm, hbm, rim, rim, column, column],
        out_specs=[hbm, hbm],
        out_shape=[
            jax.ShapeDtypeStruct(q_prev.shape, F32),
            jax.ShapeDtypeStruct((shards, lines, 2 * width), F32),
        ],
        scratch_shapes=[
            pltpu.VMEM((layers, 3, rows, cols), F32),
            pltpu.VMEM((layers, rows, cols), F32),
        ]
        + [pltpu.VMEM((cols // LANES, rows + 16, LANES), F32)] * 7
        + [pltpu.VMEM((2 * lines, depth), BF16)] * 2
        + [
            pltpu.VMEM((shards, lines, 2 * width), F32),
            pltpu.SemaphoreType.DMA((layers, 3)),
            pltpu.SemaphoreType.DMA((layers,)),
            pltpu.SemaphoreType.DMA((steps,)),
        ],
        compiler_params=params(62),
        cost_estimate=pl.CostEstimate(flops=12 * lines * depth * depth, bytes_accessed=16 << 20, transcendentals=0),
        name="step_forward",
    )(place, q_prev, q_now, psi_now, top, bottom, table_high, table_low)


def prepare_kernel(shard, eigen, stretch, to_modes, to_layers, theta, ratio, scale, in_high, in_low, out_high, out_low):
    modes, width = theta.shape
    wave = eigen[pl.ds(shard[0], 1), :]
    for mode in range(modes):
        theta[mode : mode + 1, :] = wave + stretch[mode]
    shift = theta[...]
    half = 0.5 * jnp.sqrt(shift)
    angle = 2.0 * jnp.log1p(half + half * half / (1.0 + jnp.sqrt(1.0 + half * half)))
    theta[...] = angle
    ratio[...] = jnp.exp(-angle)
    scale[...] = (-2.0 / (width * eigen.shape[0] + 1)) / jnp.sqrt(shift * (4.0 + shift))

    size = 8 * modes
    line = lax.broadcasted_iota(jnp.int32, (size, modes), 0)
    index = lax.broadcasted_iota(jnp.int32, (size, modes), 1)
    by_layer = (line // 8 == index).astype(F32)
    by_mode = (line % modes == index).astype(F32)
    down = lax.broadcasted_iota(jnp.int32, (size, size), 0)
    along = lax.broadcasted_iota(jnp.int32, (size, size), 1)

    def exact(left, right, sides):
        return lax.dot_general(
            left, right, ((sides, ((), ()))), precision=lax.Precision.HIGHEST, preferred_element_type=F32
        )

    spread = exact(exact(by_mode, to_modes[...], ((1,), (0,))), by_layer, ((1,), (1,)))
    in_high[...], in_low[...] = split(jnp.where(down // modes == along % 8, spread, 0.0))
    spread = exact(exact(by_layer, to_layers[...], ((1,), (0,))), by_mode, ((1,), (1,)))
    out_high[...], out_low[...] = split(jnp.where(down % 8 == along // modes, spread, 0.0))


def prepare(shard, eigen, stretch, to_modes, to_layers):
    modes, width = stretch.shape[0], eigen.shape[1]
    field = jax.ShapeDtypeStruct((modes, width), F32)
    mix = jax.ShapeDtypeStruct((8 * modes, 8 * modes), BF16)
    vmem, smem = pl.BlockSpec(memory_space=pltpu.VMEM), pl.BlockSpec(memory_space=pltpu.SMEM)
    return pl.pallas_call(
        prepare_kernel,
        in_specs=[smem, vmem, smem, vmem, vmem],
        out_specs=[vmem] * 7,
        out_shape=[field, field, field, mix, mix, mix, mix],
        compiler_params=params(8),
        name="prepare",
    )(shard, eigen, stretch, to_modes, to_layers)


def project_kernel(source, mix_high, mix_low, ratio, modal, ends, power):
    layers, rows, width = source.shape

    @pl.when(pl.program_id(0) == 0)
    def _():
        ends[...] = jnp.zeros(ends.shape, F32)
        power[...] = jnp.ones(power.shape, F32)

    decay = ratio[...]
    last, first, scale = ends[0], ends[1], power[...]
    for t in range(rows // 8):
        high, low = split(source[:, 8 * t : 8 * t + 8, :].reshape(8 * layers, width))
        mixed = dot(mix_high[...], high) + dot(mix_low[...], high) + dot(mix_high[...], low)
        block = mixed.reshape(8, layers, width)
        modal[8 * t : 8 * t + 8] = block
        for row in range(8):
            last = decay * last + block[row]
            first = first + scale * block[row]
            scale = scale * decay
    ends[0] = last
    ends[1] = first
    power[...] = scale


def project(stacked, mix_high, mix_low, ratio):
    layers, rows, width = stacked.shape
    step = 16
    whole = pl.BlockSpec(mix_high.shape, lambda i: (0, 0))
    return pl.pallas_call(
        project_kernel,
        grid=(rows // step,),
        in_specs=[
            pl.BlockSpec((layers, step, width), lambda i: (0, i, 0)),
            whole,
            whole,
            pl.BlockSpec((layers, width), lambda i: (0, 0)),
        ],
        out_specs=[
            pl.BlockSpec((step, layers, width), lambda i: (i, 0, 0)),
            pl.BlockSpec((2, layers, width), lambda i: (0, 0, 0)),
        ],
        out_shape=[
            jax.ShapeDtypeStruct((rows, layers, width), F32),
            jax.ShapeDtypeStruct((2, layers, width), F32),
        ],
        scratch_shapes=[pltpu.VMEM((layers, width), F32)],
        compiler_params=params(12),
        name="project",
    )(stacked, mix_high, mix_low, ratio)


RADICES = (2, 4, 4)


def exchange(total, level, blocks):
    radix, group = RADICES[level], math.prod(RADICES[:level])
    parts = []
    for shift in range(1, radix):
        pairs = []
        for target in range(blocks):
            spot = (target // group) % radix
            pairs.append((target + ((spot + shift) % radix - spot) * group, target))
        parts.append(lax.ppermute(total, "row", pairs))
    return parts


def decayed(unit, count):
    return jnp.exp(-unit * count.astype(F32))


def join(unit, me, parts, level):
    radix, group = RADICES[level], math.prod(RADICES[:level])
    place = (me // group) % radix
    last = jnp.zeros_like(unit)
    first = jnp.zeros_like(unit)
    for shift, part in enumerate(parts):
        spot = (place + shift) % radix
        last = last + decayed(unit, group * (radix - 1 - spot)) * part[0]
        first = first + decayed(unit, group * spot) * part[1]
    return last, first


def join_kernel(level, rows, place, theta, *refs):
    parts, result = refs[:-1], refs[-1]
    last, first = join(rows * theta[...], place[0], parts, level)
    result[0] = last
    result[1] = first


def join_level(level, rows, place, theta, parts):
    vmem, smem = pl.BlockSpec(memory_space=pltpu.VMEM), pl.BlockSpec(memory_space=pltpu.SMEM)
    return pl.pallas_call(
        functools.partial(join_kernel, level, rows),
        in_specs=[smem, vmem] + [vmem] * len(parts),
        out_specs=vmem,
        out_shape=jax.ShapeDtypeStruct(parts[0].shape, F32),
        compiler_params=params(8),
        name="join",
    )(place, theta, *parts)


def entering(theta, rows, me, blocks, levels):
    unit = rows * theta
    above = jnp.zeros_like(theta)
    below = jnp.zeros_like(theta)
    for level, parts in enumerate(levels):
        radix, group = RADICES[level], math.prod(RADICES[:level])
        spot_here, inside = (me // group) % radix, me % group
        for shift in range(1, radix):
            spot = (spot_here + shift) % radix
            over = jnp.maximum(group * (spot_here - 1 - spot), 0) + inside
            under = jnp.maximum(group * (spot - spot_here - 1), 0) + group - 1 - inside
            above = above + jnp.where(spot < spot_here, decayed(unit, over), 0.0) * parts[shift][0]
            below = below + jnp.where(spot > spot_here, decayed(unit, under), 0.0) * parts[shift][1]
    last, first = join(unit, me, levels[-1], len(levels) - 1)
    span = jnp.exp(-theta * (rows * blocks + 1))
    wall = jnp.exp(-theta) / (1.0 - span * span)
    above = above + decayed(unit, me) * wall * (span * last - first)
    below = below + decayed(unit, blocks - 1 - me) * wall * (span * first - last)
    return above, below


def solve_kernel(blocks, place, theta, modal, ratio, scale, mix_high, mix_low, *refs):
    count = sum(RADICES)
    parts, (result, down, up) = refs[:count], refs[count:]
    rows, layers, width = modal.shape
    step = result.shape[1]
    decay = ratio[...]

    @pl.when(pl.program_id(0) == 0)
    def _():
        levels, at = [], 0
        for radix in RADICES:
            levels.append(parts[at : at + radix])
            at += radix
        above, below = entering(theta[...], rows, place[0], blocks, levels)
        up[...] = below

        def forth(row, value):
            value = decay * value + modal[row]
            down[row] = value
            return value

        lax.fori_loop(0, rows, forth, above, unroll=8)

    base = rows - step * (pl.program_id(0) + 1)
    beyond, factor = up[...], scale[...]
    solved = [None] * step
    for row in range(step - 1, -1, -1):
        value = decay * beyond
        beyond = modal[base + row] + value
        solved[row] = factor * (down[base + row] + value)
    up[...] = beyond
    for t in range(step // 8):
        high, low = split(jnp.stack(solved[8 * t : 8 * t + 8]).reshape(8 * layers, width))
        mixed = dot(mix_high[...], high) + dot(mix_low[...], high) + dot(mix_high[...], low)
        result[:, 8 * t : 8 * t + 8, :] = mixed.reshape(layers, 8, width)


def solve(place, theta, modal, ratio, scale, mix_high, mix_low, parts, blocks):
    rows, layers, width = modal.shape
    step = 16
    whole = pl.BlockSpec(mix_high.shape, lambda i: (0, 0))
    field = pl.BlockSpec((layers, width), lambda i: (0, 0))
    return pl.pallas_call(
        functools.partial(solve_kernel, blocks),
        grid=(rows // step,),
        in_specs=[
            pl.BlockSpec(memory_space=pltpu.SMEM),
            field,
            pl.BlockSpec((rows, layers, width), lambda i: (0, 0, 0)),
            field,
            field,
            whole,
            whole,
        ]
        + [pl.BlockSpec((2, layers, width), lambda i: (0, 0, 0))] * len(parts),
        out_specs=pl.BlockSpec((layers, step, width), lambda i: (0, rows // step - 1 - i, 0)),
        out_shape=jax.ShapeDtypeStruct((layers, rows, width), F32),
        scratch_shapes=[pltpu.VMEM((rows, layers, width), F32), pltpu.VMEM((layers, width), F32)],
        compiler_params=params(16),
        name="solve",
    )(place, theta, modal, ratio, scale, mix_high, mix_low, *parts)


def inverse_kernel(source, table_high, table_low, result, high, low, held, sems):
    shards, lines, width = source.shape
    width //= 2
    index = pl.program_id(0)

    @pl.when(index == 0)
    def _():
        for part in range(shards):
            column = slice(part * width, (part + 1) * width)
            for parity in range(2):
                line = slice(parity * lines, (parity + 1) * lines)
                high[line, column], low[line, column] = split(source[part, :, parity * width : (parity + 1) * width])

    value = three_dots(high[...], low[...], table_high[...], table_low[...])
    step = value.shape[1]
    count = result.shape[1] // step
    odd, even = value[:lines] * alternating((1, step)), value[lines:]
    held[index] = odd + even
    mirror = odd - even
    order = LANES - 1 - lax.broadcasted_iota(jnp.int32, (lines, LANES), 1)
    for part in range(step // LANES):
        block = mirror[:, step - LANES * (part + 1) : step - LANES * part]
        held[count - 1 - index, :, LANES * part : LANES * (part + 1)] = jnp.take_along_axis(block, order, axis=1)

    def copy(block):
        column = pl.ds(pl.multiple_of(block * step, step), step)
        return pltpu.make_async_copy(held.at[block], result.at[:, column], sems.at[block])

    copy(index).start()
    copy(count - 1 - index).start()

    @pl.when(index == pl.num_programs(0) - 1)
    def _():
        for block in range(count):
            copy(block).wait()


def inverse(source, table_high, table_low):
    shards, lines, width = source.shape
    depth = shards * width // 2
    step = 256
    count = 2 * depth // step
    column = pl.BlockSpec((depth, step), lambda i: (0, i))
    return pl.pallas_call(
        inverse_kernel,
        grid=(depth // step,),
        in_specs=[pl.BlockSpec(source.shape, lambda i: (0, 0, 0)), column, column],
        out_specs=pl.BlockSpec(memory_space=pltpu.HBM),
        out_shape=jax.ShapeDtypeStruct((lines, 2 * depth), F32),
        scratch_shapes=[pltpu.VMEM((2 * lines, depth), BF16)] * 2
        + [pltpu.VMEM((count, lines, step), F32), pltpu.SemaphoreType.DMA((count,))],
        compiler_params=params(24),
        name="inverse",
    )(source, table_high, table_low)


def on_device(q_prev, q_now, psi_now, layers_to_modes, modes_to_layers, stretch):
    layer_count, row_count, col_count = q_prev.shape
    blocks = lax.axis_size("row")
    shards = lax.axis_size("layer")
    me = lax.axis_index("row")
    table_high, table_low = (jnp.asarray(value) for value in half_table(col_count))
    eigen = jnp.asarray(column_eigen(col_count, shards))
    place = me.astype(jnp.int32).reshape(1)
    shard = lax.axis_index("layer").astype(jnp.int32).reshape(1)

    initial, last = rims(q_prev, q_now, psi_now)
    pairs = [(i, i + 1) for i in range(blocks - 1)]
    top = lax.ppermute(last, "row", pairs)
    bottom = lax.ppermute(initial, "row", [(j, i) for i, j in pairs])
    theta, ratio, scale, *mixes = prepare(shard, eigen, stretch, layers_to_modes, modes_to_layers)
    q_next, spectrum = step_forward(place, q_prev, q_now, psi_now, top, bottom, table_high, table_low, shards, blocks)
    stacked = lax.all_to_all(spectrum, "layer", split_axis=0, concat_axis=0, tiled=True)
    stacked = stacked.reshape(shards * layer_count, row_count, -1)
    modal, total = project(stacked, mixes[0], mixes[1], ratio)
    parts = []
    for level in range(len(RADICES)):
        group = [total] + exchange(total, level, blocks)
        parts.extend(group)
        if level + 1 < len(RADICES):
            total = join_level(level, row_count, place, theta, group)
    layered = solve(place, theta, modal, ratio, scale, mixes[2], mixes[3], parts, blocks)
    layered = layered.reshape(shards, layer_count * row_count, -1)
    returned = lax.all_to_all(layered, "layer", split_axis=0, concat_axis=0, tiled=True)
    psi_next = inverse(returned, table_high, table_low)
    return (q_next, psi_next.reshape(q_prev.shape))


def solution(mesh):
    return jax.shard_map(
        on_device,
        mesh=mesh,
        in_specs=(
            P("layer", "row", None),
            P("layer", "row", None),
            P("layer", "row", None),
            P(),
            P(),
            P(),
        ),
        out_specs=(P("layer", "row", None), P("layer", "row", None)),
        check_vma=False,
    )
```

time: 173 us -> 126 us (0.73)
  blocking collectives: 0 us -> 30.6 us
  starting transfers between devices: 58 us -> 30.2 us
  local copies, waits for them, and re-layouts: 21.9 us -> 0.69 us
  Pallas kernels: 48.5 us -> 29.1 us
  other arithmetic: 12.9 us -> 0 us
  waiting for transfers between devices: 29.1 us -> 32.5 us
    all_to_all x0 -> x1, blocking collectives: none -> 30.6 us  [on_device(): lax.all_to_all(layered, 'layer', split_axis=0, concat_axis=0, tiled=True)]
    pallas_call x7, Pallas kernels: 45.9 us -> 27.1 us  [the longest x1 14.7 us: step_forward(): pl.pallas_call(functools.partial(step_kernel, blocks), grid=(layers + ste...]
    all_to_all x2 -> x1, waiting for transfers between devices: 10.6 us -> 23.2 us  [on_device(): lax.all_to_all(spectrum, 'layer', split_axis=0, concat_axis=0, tiled=True)]
    unnamed x43 -> x16, local copies, waits for them, and re-layouts: 12.8 us -> 0.69 us
    ppermute x16 -> x9, starting transfers between devices: 35.5 us -> 24.1 us  [the longest x7 21.1 us: exchange(): parts.append(lax.ppermute(total, 'row', pairs))]
    all_to_all x2 -> x0, starting transfers between devices: 10.9 us -> none  [on_device(): lax.all_to_all(layered, 'layer', split_axis=0, concat_axis=0, tiled=True)]
    add x7 -> x0, other arithmetic: 5.77 us -> none  [the longest x3 2.24 us: interface(): last = last + decay(group * (radix - 1 - spot)) * part[0]]
    all_to_all x2 -> x1, starting transfers between devices: 11.6 us -> 6.07 us  [on_device(): lax.all_to_all(spectrum, 'layer', split_axis=0, concat_axis=0, tiled=True)]
  transfers between devices with their start and end apart: 20 -> 10, of which waited for: 12 -> 6; matrix products, arithmetic and copies ran while one was open for 8% -> 0% of each run, Pallas kernels for 8% -> 1%
where the time goes in v2:
time: 126 us; the launch traced here: 124 us
  waiting for transfers between devices  32.5 us (26%)
  blocking collectives  30.6 us (24%)
  starting transfers between devices  30.2 us (24%)
  Pallas kernels  29.1 us (23%)
    all_to_all x1, blocking collectives, on_device(): lax.all_to_all(layered, 'layer', split_axis=0, concat_axis=0, tiled=True)  30.6 us
    all_to_all x1, waiting for transfers between devices, on_device(): lax.all_to_all(spectrum, 'layer', split_axis=0, concat_axis=0, tiled=True)  23.2 us
    ppermute x7, starting transfers between devices, exchange(): parts.append(lax.ppermute(total, 'row', pairs))  21.1 us
    pallas_call x1, Pallas kernels, step_forward(): pl.pallas_call(functools.partial(step_kernel, blocks), grid=(layers + ste...  14.7 us
    pallas_call x1, Pallas kernels, inverse(): pl.pallas_call(inverse_kernel, grid=(depth // step,), in_specs=[pl.BlockS...  6.26 us
    all_to_all x1, starting transfers between devices, on_device(): lax.all_to_all(spectrum, 'layer', split_axis=0, concat_axis=0, tiled=True)  6.07 us
    ppermute x7, waiting for transfers between devices, exchange(): parts.append(lax.ppermute(total, 'row', pairs))  5.97 us
    ppermute x1, waiting for transfers between devices, on_device(): bottom = lax.ppermute(initial, 'row', [(j, i) for i, j in pairs])  3.4 us
  transfers between devices with their start and end apart: 10, of which 6 were waited for; matrix products, arithmetic and copies ran while one was open for 0% of the time, Pallas kernels for 1%

profile of v2, /device:TPU:32, one launch (start us, length us, event | category | flops | bytes accessed | tf_op | source)
XLA Modules:
  0.0 123.8 jit_solution(10233493443770274700)
XLA Ops:
  0.6 2.1 %rims.1 = (f32[4,4,2048]{2,1,0:T(4,128)}, f32[4,4,2048]{2,1,0:T(4,128)}) custom-call(f32[4,64,2048]{2,1,0:T(8,128)} %prev.1, f32[4,64,2048]{2,1,0:T(8,128)} %now.1, f32[4,64,2048]{2,1,0:T(8,128)} %psi.1, f32[4,64,2048]{2,1,0:T(8,128)} %prev.1, f32[4,64,2048]{2,1,0:T(8,128)} %now.1, f32[4,64,2048]{2,1,0:T(8,128)} %psi.1), custom_call_target="tpu_custom_call" | custom-call | tf_op jit(solution)/shard_map/rims/pallas_call | solution.py:77
  2.7 1.7 %collective-permute-start = (f32[4,4,2048]{2,1,0:T(4,128)}, f32[4,4,2048]{2,1,0:T(4,128)S(1)}, u32[]{:S(2)}, u32[]{:S(2)}) collective-permute-start(f32[4,4,2048]{2,1,0:T(4,128)} %get-tuple-element.15), channel_id=1, source_target_pairs={{0,1},{1,2},{2,3},{3,4},{4,5},{5,6},{6,7},{7,8},{8,9},{9,10},{10,1... | collective-permute-start | bytes 393224 | tf_op jit(solution)/shard_map/ppermute | solution.py:584
  4.5 1.3 %collective-permute-start.1 = (f32[4,4,2048]{2,1,0:T(4,128)}, f32[4,4,2048]{2,1,0:T(4,128)S(1)}, u32[]{:S(2)}, u32[]{:S(2)}) collective-permute-start(f32[4,4,2048]{2,1,0:T(4,128)} %get-tuple-element.16), channel_id=1, source_target_pairs={{1,0},{2,1},{3,2},{4,3},{5,4},{6,5},{7,6},{8,7},{9,8},{10,9},{11,1... | collective-permute-start | bytes 393224 | tf_op jit(solution)/shard_map/ppermute | solution.py:585
  5.8 0.0 collective-permute-done.top
  5.8 0.0 copy-start.6
  5.8 3.4 %collective-permute-done.1.bottom = f32[4,4,2048]{2,1,0:T(4,128)S(1)} collective-permute-done((f32[4,4,2048]{2,1,0:T(4,128)}, f32[4,4,2048]{2,1,0:T(4,128)S(1)}, u32[]{:S(2)}, u32[]{:S(2)}) %collective-permute-start.1) | collective-permute-done | bytes 131104 | tf_op jit(solution)/shard_map/ppermute | solution.py:585
  9.2 0.0 copy-start.7
  9.2 0.0 copy-done.6
  9.2 0.6 copy-done.7
  9.8 14.7 %step_forward.1 = (f32[4,64,2048]{2,1,0:T(8,128)}, f32[8,256,256]{2,1,0:T(8,128)}) custom-call(s32[1]{0:T(128)} %bitcast.place, f32[4,64,2048]{2,1,0:T(8,128)} %prev.1, f32[4,64,2048]{2,1,0:T(8,128)} %now.1, f32[4,64,2048]{2,1,0:T(8,128)} %psi.1, f32[4,4,2048]{2,1,0:T(4,128)} %copy-done.6, f32[4,4,2048]{2,1,0:T(4,128)} %copy-done.7, ...), custom_call_target="tpu_custom_call" | custom-call | flops 3221225472 | bytes 16777216 | tf_op jit(solution)/shard_map/step_forward/pallas_call | solution.py:258
  24.6 0.0 copy-start.2
  24.6 0.0 copy-start.3
  24.6 0.0 copy-start.4
  24.6 0.0 copy-start.5
  24.6 6.1 %all-to-all-start = ((f32[8,256,256]{2,1,0:T(8,128)}), f32[8,256,256]{2,1,0:T(8,128)S(1)}, u32[]{:S(2)}, u32[]{:S(2)}) async-start(f32[8,256,256]{2,1,0:T(8,128)} %get-tuple-element.19), calls=%async_computation | async-start | bytes 4194304 | tf_op jit(solution)/shard_map/all_to_all | solution.py:588
  30.7 0.0 copy-done.2
  30.7 0.0 copy-done.3
  30.7 0.0 copy-done.4
  30.7 0.0 copy-done.5
  30.7 1.6 %prepare.1 = (f32[32,256]{1,0:T(8,128)S(1)}, f32[32,256]{1,0:T(8,128)S(1)}, f32[32,256]{1,0:T(8,128)S(1)}, bf16[256,256]{1,0:T(8,128)(2,1)S(1)}, bf16[256,256]{1...) custom-call(s32[1]{0:T(128)} %bitcast.1.shard, f32[8,256]{1,0:T(8,128)S(1)} %copy-done.4, ...), custom_call_target="tpu_custom_call" | custom-call | tf_op jit(solution)/shard_map/prepare/pallas_call | solution.py:321
  32.4 23.2 %all-to-all-done = f32[8,256,256]{2,1,0:T(8,128)S(1)} async-done(((f32[8,256,256]{2,1,0:T(8,128)}), f32[8,256,256]{2,1,0:T(8,128)S(1)}, u32[]{:S(2)}, u32[]{:S(2)}) %all-to-all-start) | async-done | bytes 2097184 | tf_op jit(solution)/shard_map/all_to_all | solution.py:588
  55.5 1.9 %project.1 = (f32[64,32,256]{2,1,0:T(8,128)S(1)}, f32[2,32,256]{2,1,0:T(8,128)S(1)}) custom-call(f32[32,64,256]{2,1,0:T(8,128)S(1)} %bitcast.5, bf16[256,256]{1,0:T(8,128)(2,1)S(1)} %get-tuple-element.20.mix_high, bf16[256,256]{1,0:T(8,128)(2,1)S(1)} %get-tuple-element.21.mix_low, f32[32,256]{1,0:T(8,128)S(1)} %get-tuple-element.22.ratio), custom_call_target="tpu_custom_call" | custom-call | tf_op jit(solution)/shard_map/project/pallas_call | solution.py:359
  57.4 2.3 %collective-permute-start.2 = (f32[2,32,256]{2,1,0:T(8,128)S(1)}, f32[2,32,256]{2,1,0:T(8,128)S(1)}, u32[]{:S(2)}, u32[]{:S(2)}) collective-permute-start(f32[2,32,256]{2,1,0:T(8,128)S(1)} %get-tuple-element.27.refs_0_), channel_id=1, source_target_pairs={{1,0},{0,1},{3,2},{2,3},{5,4},{4,5},{7,6},{6,7},{9,8},{8,9},{11,10... | collective-permute-start | bytes 196616 | tf_op jit(solution)/shard_map/ppermute | solution.py:393
  59.7 0.9 collective-permute-done.2.refs_1_
  60.6 3.7 %collective-permute-start.5 = (f32[2,32,256]{2,1,0:T(8,128)S(1)}, f32[2,32,256]{2,1,0:T(8,128)S(1)}, u32[]{:S(2)}, u32[]{:S(2)}) collective-permute-start(f32[2,32,256]{2,1,0:T(8,128)S(1)} %join.2.refs_0_.refs_2_), channel_id=1, source_target_pairs={{6,0},{7,1},{0,2},{1,3},{2,4},{3,5},{4,6},{5,7},{14,8},{15,9},{8,1... | collective-permute-start | bytes 196616 | tf_op jit(solution)/shard_map/ppermute | solution.py:393
  64.4 2.5 %collective-permute-start.4 = (f32[2,32,256]{2,1,0:T(8,128)S(1)}, f32[2,32,256]{2,1,0:T(8,128)S(1)}, u32[]{:S(2)}, u32[]{:S(2)}) collective-permute-start(f32[2,32,256]{2,1,0:T(8,128)S(1)} %join.2.refs_0_.refs_2_), channel_id=1, source_target_pairs={{4,0},{5,1},{6,2},{7,3},{0,4},{1,5},{2,6},{3,7},{12,8},{13,9},{14,... | collective-permute-start | bytes 196616 | tf_op jit(solution)/shard_map/ppermute | solution.py:393
  66.8 1.9 %collective-permute-start.3 = (f32[2,32,256]{2,1,0:T(8,128)S(1)}, f32[2,32,256]{2,1,0:T(8,128)S(1)}, u32[]{:S(2)}, u32[]{:S(2)}) collective-permute-start(f32[2,32,256]{2,1,0:T(8,128)S(1)} %join.2.refs_0_.refs_2_), channel_id=1, source_target_pairs={{2,0},{3,1},{4,2},{5,3},{6,4},{7,5},{0,6},{1,7},{10,8},{11,9},{12,... | collective-permute-start | bytes 196616 | tf_op jit(solution)/shard_map/ppermute | solution.py:393
  68.7 0.0 collective-permute-done.5.refs_3_.refs_5_
  68.7 1.8 %collective-permute-done.4.refs_2_.refs_4_ = f32[2,32,256]{2,1,0:T(8,128)S(1)} collective-permute-done((f32[2,32,256]{2,1,0:T(8,128)S(1)}, f32[2,32,256]{2,1,0:T(8,128)S(1)}, u32[]{:S(2)}, u32[]{:S(2)}) %collective-permute-start.4) | collective-permute-done | bytes 65568 | tf_op jit(solution)/shard_map/ppermute | solution.py:393
  70.6 0.5 collective-permute-done.3.refs_1_.refs_3_
  71.1 0.1 join.3.refs_6_
  71.2 3.7 %collective-permute-start.8 = (f32[2,32,256]{2,1,0:T(8,128)S(1)}, f32[2,32,256]{2,1,0:T(8,128)S(1)}, u32[]{:S(2)}, u32[]{:S(2)}) collective-permute-start(f32[2,32,256]{2,1,0:T(8,128)S(1)} %join.3.refs_6_), channel_id=1, source_target_pairs={{24,0},{25,1},{26,2},{27,3},{28,4},{29,5},{30,6},{31,7},{0,8},{1,9... | collective-permute-start | bytes 196616 | tf_op jit(solution)/shard_map/ppermute | solution.py:393
  74.8 4.2 %collective-permute-start.7 = (f32[2,32,256]{2,1,0:T(8,128)S(1)}, f32[2,32,256]{2,1,0:T(8,128)S(1)}, u32[]{:S(2)}, u32[]{:S(2)}) collective-permute-start(f32[2,32,256]{2,1,0:T(8,128)S(1)} %join.3.refs_6_), channel_id=1, source_target_pairs={{16,0},{17,1},{18,2},{19,3},{20,4},{21,5},{22,6},{23,7},{24,8},{25... | collective-permute-start | bytes 196616 | tf_op jit(solution)/shard_map/ppermute | solution.py:393
  79.1 2.8 %collective-permute-start.6 = (f32[2,32,256]{2,1,0:T(8,128)S(1)}, f32[2,32,256]{2,1,0:T(8,128)S(1)}, u32[]{:S(2)}, u32[]{:S(2)}) collective-permute-start(f32[2,32,256]{2,1,0:T(8,128)S(1)} %join.3.refs_6_), channel_id=1, source_target_pairs={{8,0},{9,1},{10,2},{11,3},{12,4},{13,5},{14,6},{15,7},{16,8},{17,9... | collective-permute-start | bytes 196616 | tf_op jit(solution)/shard_map/ppermute | solution.py:393
  81.9 0.0 collective-permute-done.8.refs_9_
  81.9 2.7 %collective-permute-done.7.refs_8_ = f32[2,32,256]{2,1,0:T(8,128)S(1)} collective-permute-done((f32[2,32,256]{2,1,0:T(8,128)S(1)}, f32[2,32,256]{2,1,0:T(8,128)S(1)}, u32[]{:S(2)}, u32[]{:S(2)}) %collective-permute-start.7) | collective-permute-done | bytes 65568 | tf_op jit(solution)/shard_map/ppermute | solution.py:393
  84.6 0.0 collective-permute-done.6.refs_7_
  84.6 2.4 %solve.1 = f32[32,64,256]{2,1,0:T(8,128)S(1)} custom-call(s32[1]{0:T(128)} %bitcast.place, f32[32,256]{1,0:T(8,128)S(1)} %get-tuple-element.18.theta, f32[64,32,256]{2,1,0:T(8,128)S(1)} %get-tuple-element.23.modal, f32[32,256]{1,0:T(8,128)S(1)} %get-tuple-element.22.ratio, f32[32,256]{1,0:T(8,128)S(1)} %get-tuple-element.24.scale, ...), custom_call_target="tpu_custom_call" | custom-call | tf_op jit(solution)/shard_map/solve/pallas_call | solution.py:495
  87.0 0.0 copy-start
  87.0 0.0 copy-start.1
  87.0 30.6 %all_to_all.10.source = f32[8,256,256]{2,1,0:T(8,128)S(1)} all-to-all(f32[8,256,256]{2,1,0:T(8,128)S(1)} %bitcast.6), channel_id=1, replica_groups=mesh['layer'=8,'row'=32] {'layer'}, dimensions={0} | all-to-all | bytes 4194304 | tf_op jit(solution)/shard_map/all_to_all | solution.py:599
  117.6 0.0 copy-done
  117.6 0.0 copy-done.1
  117.6 6.3 %inverse.1 = f32[256,2048]{1,0:T(8,128)} custom-call(f32[8,256,256]{2,1,0:T(8,128)S(1)} %all_to_all.10.source, bf16[1024,1024]{1,0:T(8,128)(2,1)S(1)} %copy-done.1, bf16[1024,1024]{1,0:T(8,128)(2,1)S(1)} %copy-done), custom_call_target="tpu_custom_call" | custom-call | tf_op jit(solution)/shard_map/inverse/pallas_call | solution.py:559
  (1 shorter events, 0.0 us)
Async XLA Ops:
  2.7 3.0 %collective-permute-start = (f32[4,4,2048]{2,1,0:T(4,128)}, f32[4,4,2048]{2,1,0:T(4,128)S(1)}, u32[]{:S(2)}, u32[]{:S(2)}) collective-permute-start(f32[4,4,2048]{2,1,0:T(4,128)} %get-tuple-element.15), channel_id=1, source_target_pairs={{0,1},{1,2},{2,3},{3,4},{4,5},{5,6},{6,7},{7,8},{8,9},{9,10},{10,1... | collective-permute-start | bytes 393224 | tf_op jit(solution)/shard_map/ppermute | solution.py:584
  4.5 4.7 %collective-permute-start.1 = (f32[4,4,2048]{2,1,0:T(4,128)}, f32[4,4,2048]{2,1,0:T(4,128)S(1)}, u32[]{:S(2)}, u32[]{:S(2)}) collective-permute-start(f32[4,4,2048]{2,1,0:T(4,128)} %get-tuple-element.16), channel_id=1, source_target_pairs={{1,0},{2,1},{3,2},{4,3},{5,4},{6,5},{7,6},{8,7},{9,8},{10,9},{11,1... | collective-permute-start | bytes 393224 | tf_op jit(solution)/shard_map/ppermute | solution.py:585
  5.8 3.4 %copy-start.6 = (f32[4,4,2048]{2,1,0:T(4,128)}, f32[4,4,2048]{2,1,0:T(4,128)S(1)}, u32[]{:S(2)}) copy-start(f32[4,4,2048]{2,1,0:T(4,128)S(1)} %collective-permute-done.top) | copy-start | bytes 393220
  9.2 0.7 copy-start.7
  24.6 6.1 %copy-start.2 = (f32[32,32]{1,0:T(8,128)S(1)}, f32[32,32]{1,0:T(8,128)}, u32[]{:S(2)}) copy-start(f32[32,32]{1,0:T(8,128)} %to_modes.1) | copy-start | bytes 12292
  24.6 6.1 %copy-start.3 = (f32[32,32]{1,0:T(8,128)S(1)}, f32[32,32]{1,0:T(8,128)}, u32[]{:S(2)}) copy-start(f32[32,32]{1,0:T(8,128)} %to_layers.1) | copy-start | bytes 12292
  24.6 6.1 %copy-start.4 = (f32[8,256]{1,0:T(8,128)S(1)}, f32[8,256]{1,0:T(8,128)}, u32[]{:S(2)}) copy-start(f32[8,256]{1,0:T(8,128)} %constant.17.clone.eigen) | copy-start | bytes 24580
  24.6 6.1 %copy-start.5 = (f32[32]{0:T(128)S(1)}, f32[32]{0:T(128)}, u32[]{:S(2)}) copy-start(f32[32]{0:T(128)} %stretch.1) | copy-start | bytes 388
  24.6 30.9 %all-to-all-start = ((f32[8,256,256]{2,1,0:T(8,128)}), f32[8,256,256]{2,1,0:T(8,128)S(1)}, u32[]{:S(2)}, u32[]{:S(2)}) async-start(f32[8,256,256]{2,1,0:T(8,128)} %get-tuple-element.19), calls=%async_computation | async-start | bytes 4194304 | tf_op jit(solution)/shard_map/all_to_all | solution.py:588
  57.4 3.2 %collective-permute-start.2 = (f32[2,32,256]{2,1,0:T(8,128)S(1)}, f32[2,32,256]{2,1,0:T(8,128)S(1)}, u32[]{:S(2)}, u32[]{:S(2)}) collective-permute-start(f32[2,32,256]{2,1,0:T(8,128)S(1)} %get-tuple-element.27.refs_0_), channel_id=1, source_target_pairs={{1,0},{0,1},{3,2},{2,3},{5,4},{4,5},{7,6},{6,7},{9,8},{8,9},{11,10... | collective-permute-start | bytes 196616 | tf_op jit(solution)/shard_map/ppermute | solution.py:393
  60.6 8.1 %collective-permute-start.5 = (f32[2,32,256]{2,1,0:T(8,128)S(1)}, f32[2,32,256]{2,1,0:T(8,128)S(1)}, u32[]{:S(2)}, u32[]{:S(2)}) collective-permute-start(f32[2,32,256]{2,1,0:T(8,128)S(1)} %join.2.refs_0_.refs_2_), channel_id=1, source_target_pairs={{6,0},{7,1},{0,2},{1,3},{2,4},{3,5},{4,6},{5,7},{14,8},{15,9},{8,1... | collective-permute-start | bytes 196616 | tf_op jit(solution)/shard_map/ppermute | solution.py:393
  64.4 6.2 %collective-permute-start.4 = (f32[2,32,256]{2,1,0:T(8,128)S(1)}, f32[2,32,256]{2,1,0:T(8,128)S(1)}, u32[]{:S(2)}, u32[]{:S(2)}) collective-permute-start(f32[2,32,256]{2,1,0:T(8,128)S(1)} %join.2.refs_0_.refs_2_), channel_id=1, source_target_pairs={{4,0},{5,1},{6,2},{7,3},{0,4},{1,5},{2,6},{3,7},{12,8},{13,9},{14,... | collective-permute-start | bytes 196616 | tf_op jit(solution)/shard_map/ppermute | solution.py:393
  66.8 4.3 %collective-permute-start.3 = (f32[2,32,256]{2,1,0:T(8,128)S(1)}, f32[2,32,256]{2,1,0:T(8,128)S(1)}, u32[]{:S(2)}, u32[]{:S(2)}) collective-permute-start(f32[2,32,256]{2,1,0:T(8,128)S(1)} %join.2.refs_0_.refs_2_), channel_id=1, source_target_pairs={{2,0},{3,1},{4,2},{5,3},{6,4},{7,5},{0,6},{1,7},{10,8},{11,9},{12,... | collective-permute-start | bytes 196616 | tf_op jit(solution)/shard_map/ppermute | solution.py:393
  71.2 10.7 %collective-permute-start.8 = (f32[2,32,256]{2,1,0:T(8,128)S(1)}, f32[2,32,256]{2,1,0:T(8,128)S(1)}, u32[]{:S(2)}, u32[]{:S(2)}) collective-permute-start(f32[2,32,256]{2,1,0:T(8,128)S(1)} %join.3.refs_6_), channel_id=1, source_target_pairs={{24,0},{25,1},{26,2},{27,3},{28,4},{29,5},{30,6},{31,7},{0,8},{1,9... | collective-permute-start | bytes 196616 | tf_op jit(solution)/shard_map/ppermute | solution.py:393
  74.8 9.8 %collective-permute-start.7 = (f32[2,32,256]{2,1,0:T(8,128)S(1)}, f32[2,32,256]{2,1,0:T(8,128)S(1)}, u32[]{:S(2)}, u32[]{:S(2)}) collective-permute-start(f32[2,32,256]{2,1,0:T(8,128)S(1)} %join.3.refs_6_), channel_id=1, source_target_pairs={{16,0},{17,1},{18,2},{19,3},{20,4},{21,5},{22,6},{23,7},{24,8},{25... | collective-permute-start | bytes 196616 | tf_op jit(solution)/shard_map/ppermute | solution.py:393
  79.1 5.5 %collective-permute-start.6 = (f32[2,32,256]{2,1,0:T(8,128)S(1)}, f32[2,32,256]{2,1,0:T(8,128)S(1)}, u32[]{:S(2)}, u32[]{:S(2)}) collective-permute-start(f32[2,32,256]{2,1,0:T(8,128)S(1)} %join.3.refs_6_), channel_id=1, source_target_pairs={{8,0},{9,1},{10,2},{11,3},{12,4},{13,5},{14,6},{15,7},{16,8},{17,9... | collective-permute-start | bytes 196616 | tf_op jit(solution)/shard_map/ppermute | solution.py:393
  87.0 30.6 %copy-start = (bf16[1024,1024]{1,0:T(8,128)(2,1)S(1)}, bf16[1024,1024]{1,0:T(8,128)(2,1)}, u32[]{:S(2)}) copy-start(bf16[1024,1024]{1,0:T(8,128)(2,1)} %constant.16.clone.table_low) | copy-start | bytes 6291460
  87.0 30.6 %copy-start.1 = (bf16[1024,1024]{1,0:T(8,128)(2,1)S(1)}, bf16[1024,1024]{1,0:T(8,128)(2,1)}, u32[]{:S(2)}) copy-start(bf16[1024,1024]{1,0:T(8,128)(2,1)} %constant.15.clone.table_high) | copy-start | bytes 6291460

commit v3 on v2

v3 whole, which is shorter than its diff:
```python
import functools
import math

import jax
import jax.numpy as jnp
import ml_dtypes
import numpy as np
from jax import lax
from jax.experimental import pallas as pl
from jax.experimental.pallas import tpu as pltpu
from jax.sharding import PartitionSpec as P

TIME_STEP = 0.1
VISCOSITY = 0.02
F32 = jnp.float32
BF16 = jnp.bfloat16
LANES = 128
LAG = 2
INNER_LIMIT = 46
OUTER_LIMIT = 24


def params(megabytes):
    return pltpu.CompilerParams(vmem_limit_bytes=megabytes << 20)


def half_table(length):
    positions = np.arange(1, length // 2 + 1, dtype=np.int64)
    product = (2 * positions[:, None] * positions[None, :]) % (2 * (length + 1))
    table = np.sin(product.astype(np.float64) * (math.pi / (length + 1)))
    high = table.astype(np.float32).astype(ml_dtypes.bfloat16)
    low = (table - high.astype(np.float64)).astype(np.float32).astype(ml_dtypes.bfloat16)
    return high, low


def column_eigen(length, shards):
    positions = np.arange(1, length // 2 + 1, dtype=np.float64)
    waves = np.stack([length + 1 - 2 * positions, 2 * positions])
    eigen = 4.0 * np.sin(waves * (math.pi / (2 * (length + 1)))) ** 2
    eigen = eigen.astype(np.float32).reshape(2, shards, -1)
    return np.concatenate([eigen[0], eigen[1]], axis=1)


def split(value):
    high = value.astype(BF16)
    low = (value - high.astype(F32)).astype(BF16)
    return high, low


def dot(left, right):
    return jnp.dot(left, right, preferred_element_type=F32)


def three_dots(high, low, table_high, table_low):
    return dot(high, table_high) + dot(low, table_high) + dot(high, table_low)


def alternating(shape):
    lane = lax.broadcasted_iota(jnp.int32, shape, 1)
    return jnp.where(lane % 2 == 0, 1.0, -1.0).astype(F32)


def vmem():
    return pl.BlockSpec(memory_space=pltpu.VMEM)


def smem():
    return pl.BlockSpec(memory_space=pltpu.SMEM)


def rim_kernel(prev_first, now_first, psi_first, prev_last, now_last, psi_last, initial, last):
    rows = prev_last.shape[1]
    initial[:, 0:1] = psi_first[:, 0:1]
    initial[:, 1:2] = now_first[:, 0:1]
    initial[:, 2:4] = prev_first[:, 0:2]
    last[:, 0:1] = psi_last[:, rows - 1 :]
    last[:, 1:2] = now_last[:, rows - 1 :]
    last[:, 2:4] = prev_last[:, rows - 2 :]


def rims(q_prev, q_now, psi_now):
    layers, rows, cols = q_prev.shape
    first = pl.BlockSpec((layers, 8, cols), lambda i: (0, 0, 0))
    final = pl.BlockSpec((layers, 8, cols), lambda i: (0, rows // 8 - 1, 0))
    rim = jax.ShapeDtypeStruct((layers, 4, cols), F32)
    whole = pl.BlockSpec(rim.shape, lambda i: (0, 0, 0))
    return pl.pallas_call(
        rim_kernel,
        grid=(1,),
        in_specs=[first, first, first, final, final, final],
        out_specs=[whole, whole],
        out_shape=[rim, rim],
        compiler_params=params(62),
        name="rims",
    )(q_prev, q_now, psi_now, q_prev, q_now, psi_now)


def shift_columns(source, to_east, to_west):
    count, rows, width = source.shape
    lane = lax.broadcasted_iota(jnp.int32, (rows, width), 1)
    east, west = {count: 0.0}, {-1: 0.0}

    def store(c):
        to_east[c] = jnp.where(lane == width - 1, east[c + 1], east[c])
        to_west[c] = jnp.where(lane == 0, west[c - 1], west[c])

    for c in range(count + LAG):
        if c < count:
            value = source[c]
            east[c] = pltpu.roll(value, width - 1, 1)
            west[c] = pltpu.roll(value, 1, 1)
        if c >= LAG:
            store(c - LAG)


def advance(fields, segments, rows, store):
    p, z, ze, zw, q, qe, qw = fields
    count, _, width = p.shape
    lane = lax.broadcasted_iota(jnp.int32, (rows, width), 1)
    third = -2.0 * TIME_STEP / 12.0
    drag = -2.0 * TIME_STEP * VISCOSITY
    middle = {}
    east = {(n, count): 0.0 for n in range(len(segments))}
    west = {(n, -1): 0.0 for n in range(len(segments))}

    def tendency(n, c):
        start, wall = segments[n]

        def here(ext, row=0):
            return ext[c, start + row : start + row + rows, :]

        pn, pc, ps = here(p, -1), here(p), here(p, 1)
        zn, zc, zs = here(z, -1), here(z), here(z, 1)
        zne, zce, zse = here(ze, -1), here(ze), here(ze, 1)
        znw, zcw, zsw = here(zw, -1), here(zw), here(zw, 1)
        qc = here(q)
        near = here(q, -1) + here(q, 1)
        far = here(q, -2) + here(q, 2)
        down = zs - zn
        beside = 2.0 * near - 8.0 * qc
        from_east = pc * ((zsw - znw) + down) + ps * (zsw - zc) + pn * (zc - znw)
        from_west = ps * (zc - zse) + pn * (zne - zc) - pc * ((zse - zne) + down)
        from_east = third * from_east + drag * (beside + here(qe))
        from_west = third * from_west + drag * (beside + here(qw))
        east[n, c] = pltpu.roll(from_east, width - 1, 1)
        west[n, c] = pltpu.roll(from_west, 1, 1)
        across = zce - zcw
        own = pn * (across + (zne - znw)) - ps * (across + (zse - zsw))
        bulk = far - 8.0 * near + 20.0 * qc
        if wall is not None:
            bulk = bulk - wall * qc
        if c == 0:
            bulk = bulk - jnp.where(lane == 0, qc, 0.0)
        if c == count - 1:
            bulk = bulk - jnp.where(lane == width - 1, qc, 0.0)
        middle[n, c] = qc + third * own + drag * bulk

    def finish(n, c):
        value = middle[n, c] + jnp.where(lane == width - 1, east[n, c + 1], east[n, c])
        store(n, c, value + jnp.where(lane == 0, west[n, c - 1], west[n, c]))

    for c in range(count + LAG):
        for n in range(len(segments)):
            if c < count:
                tendency(n, c)
            if c >= LAG:
                finish(n, c - LAG)


def fold_columns(count, rows, read, write):
    lane = lax.broadcasted_iota(jnp.int32, (rows, LANES), 1)
    order = LANES - 1 - lane
    sign = alternating((rows, LANES))
    pairs = {}
    for c in range(count // 2 + LAG):
        if c < count // 2:
            pairs[c] = read(c), jnp.take_along_axis(read(count - 1 - c), order, axis=1)
        if c >= LAG:
            lower, upper = pairs[c - LAG]
            write(c - LAG, (lower + upper) * sign, lower - upper)


def inner_kernel(prev, now, psi, table_high_in, table_low_in, q_out, high, low, rim, near, table_high, table_low, *scratch):
    fields, q_held, p, z, ze, zw, q, qe, qw, sems, q_sems, table_sems = scratch
    layers, rows, cols = prev.shape
    inner = rows - 16
    layer = pl.program_id(0)

    def load(index, which):
        source = (psi, now, prev)[which]
        slot = index % 2
        return pltpu.make_async_copy(source.at[index], fields.at[slot, which], sems.at[slot, which])

    def save(index):
        return pltpu.make_async_copy(
            q_held.at[index, pl.ds(8, inner)], q_out.at[index, pl.ds(8, inner)], q_sems.at[index]
        )

    tables = [
        pltpu.make_async_copy(table_high_in, table_high, table_sems.at[0]),
        pltpu.make_async_copy(table_low_in, table_low, table_sems.at[1]),
    ]

    @pl.when(layer == 0)
    def _():
        for index in range(2):
            for which in range(3):
                load(index, which).start()

    for which in range(3):
        load(layer, which).wait()
    for which, ext in enumerate((p, z, q)):
        for c in range(ext.shape[0]):
            ext[c, 8 : 8 + rows, :] = fields[layer % 2, which, :, LANES * c : LANES * (c + 1)]
        near[which, layer, 0:4] = fields[layer % 2, which, 0:4]
        near[which, layer, 4:8] = fields[layer % 2, which, rows - 4 :]

    @pl.when(layer + 2 < layers)
    def _():
        for which in range(3):
            load(layer + 2, which).start()

    @pl.when(layer == layers - 2)
    def _():
        for table in tables:
            table.start()

    shift_columns(z, ze, zw)
    shift_columns(q, qe, qw)

    def store(n, c, value):
        q_held[layer, :, LANES * c : LANES * (c + 1)] = value

    advance((p, z, ze, zw, q, qe, qw), [(8, None)], rows, store)
    save(layer).start()
    rim[layer, 0:8] = q_held[layer, 0:8]
    rim[layer, 8:16] = q_held[layer, rows - 8 :]

    def read(c):
        return q_held[layer, 8 : 8 + inner, LANES * c : LANES * (c + 1)]

    def write(c, *folds):
        for parity, value in enumerate(folds):
            line = pl.ds(pl.multiple_of((parity * layers + layer) * inner, inner), inner)
            column = slice(LANES * c, LANES * (c + 1))
            high[line, column], low[line, column] = split(value)

    fold_columns(cols // LANES, inner, read, write)

    @pl.when(layer == layers - 1)
    def _():
        for index in range(layers):
            save(index).wait()
        for table in tables:
            table.wait()


def inner_step(q_prev, q_now, psi_now, table_high, table_low):
    layers, rows, cols = q_prev.shape
    depth = cols // 2
    hbm = pl.BlockSpec(memory_space=pltpu.HBM)
    lines = jax.ShapeDtypeStruct((2 * layers * (rows - 16), depth), BF16)
    table = jax.ShapeDtypeStruct((depth, depth), BF16)
    return pl.pallas_call(
        inner_kernel,
        grid=(layers,),
        in_specs=[hbm] * 5,
        out_specs=[hbm] + [vmem()] * 6,
        out_shape=[
            jax.ShapeDtypeStruct(q_prev.shape, F32),
            lines,
            lines,
            jax.ShapeDtypeStruct((layers, 16, cols), F32),
            jax.ShapeDtypeStruct((3, layers, 8, cols), F32),
            table,
            table,
        ],
        scratch_shapes=[pltpu.VMEM((2, 3, rows, cols), F32), pltpu.VMEM((layers, rows, cols), F32)]
        + [pltpu.VMEM((cols // LANES, rows + 16, LANES), F32)] * 7
        + [
            pltpu.SemaphoreType.DMA((2, 3)),
            pltpu.SemaphoreType.DMA((layers,)),
            pltpu.SemaphoreType.DMA((2,)),
        ],
        compiler_params=params(INNER_LIMIT),
        cost_estimate=pl.CostEstimate(flops=60 * layers * rows * cols, bytes_accessed=12 << 20, transcendentals=0),
        name="inner_step",
    )(q_prev, q_now, psi_now, table_high, table_low)


def outer_kernel(blocks, place, top, bottom, high_in, low_in, rim, near, table_high, table_low, q_in, q_out, spectrum, *scratch):
    q_rim, p, z, ze, zw, q, qe, qw, high, low, held, q_sems, sems = scratch
    layers, _, cols = rim.shape
    shards, lines, width = held.shape
    width //= 2
    rows = lines // layers
    inner = rows - 16

    for n in range(layers):
        first, last = 8 + 32 * n, 24 + 32 * n
        for which, (ext, row, size) in enumerate(((p, 0, 1), (z, 1, 1), (q, 2, 2))):
            for c in range(cols // LANES):
                column = slice(LANES * c, LANES * (c + 1))
                ext[c, first - size : first, :] = top[n, row : row + size, column]
                ext[c, first : first + 4, :] = near[which, n, 0:4, column]
                ext[c, last + 4 : last + 8, :] = near[which, n, 4:8, column]
                ext[c, last + 8 : last + 8 + size, :] = bottom[n, row : row + size, column]
    shift_columns(z, ze, zw)
    shift_columns(q, qe, qw)
    row = lax.broadcasted_iota(jnp.int32, (8, LANES), 0)
    wall_above = jnp.where(row == jnp.where(place[0] == 0, 0, -1), 1.0, 0.0).astype(F32)
    wall_below = jnp.where(row == jnp.where(place[0] == blocks - 1, 7, -1), 1.0, 0.0).astype(F32)
    segments = []
    for n in range(layers):
        segments += [(8 + 32 * n, wall_above), (24 + 32 * n, wall_below)]

    def store(n, c, value):
        at, column = slice(8 * (n % 2), 8 * (n % 2) + 8), slice(LANES * c, LANES * (c + 1))
        fresh = row >= 6 if n % 2 else row < 2
        q_rim[n // 2, at, column] = jnp.where(fresh, value, rim[n // 2, at, column])

    advance((p, z, ze, zw, q, qe, qw), segments, 8, store)

    def save(n, edge):
        source = q_rim.at[n, pl.ds(8 * edge, 8)]
        return pltpu.make_async_copy(source, q_out.at[n, pl.ds((rows - 8) * edge, 8)], q_sems.at[n, edge])

    for n in range(layers):
        for edge in range(2):
            save(n, edge).start()

    for block in range(2 * layers):
        line = slice(block * rows, block * rows + inner)
        high[line, :] = high_in[block * inner : (block + 1) * inner, :]
        low[line, :] = low_in[block * inner : (block + 1) * inner, :]
    for n in range(layers):

        def read(c):
            return q_rim[n, :, LANES * c : LANES * (c + 1)]

        def write(c, *folds):
            for parity, value in enumerate(folds):
                start = (parity * layers + n) * rows + inner
                column = slice(LANES * c, LANES * (c + 1))
                high[start : start + 16, column], low[start : start + 16, column] = split(value)

        fold_columns(cols // LANES, 16, read, write)

    def send(step):
        block = pl.ds(2 * step, 2)
        return pltpu.make_async_copy(held.at[block], spectrum.at[block], sems.at[step])

    def columns(step, carry):
        span = pl.ds(pl.multiple_of(step * 2 * width, 2 * width), 2 * width)
        value = three_dots(high[...], low[...], table_high[:, span], table_low[:, span])
        for part in range(2):
            column = slice(part * width, (part + 1) * width)
            for parity in range(2):
                lane = slice(parity * width, (parity + 1) * width)
                for n in range(layers):
                    start, to = (parity * layers + n) * rows, n * rows
                    held[2 * step + part, to + 8 : to + 8 + inner, lane] = value[start : start + inner, column]
                    held[2 * step + part, to : to + 8, lane] = value[start + inner : start + inner + 8, column]
                    held[2 * step + part, to + rows - 8 : to + rows, lane] = value[start + rows - 8 : start + rows, column]
        send(step).start()
        return carry

    lax.fori_loop(0, shards // 2, columns, 0)
    for n in range(layers):
        for edge in range(2):
            save(n, edge).wait()
    for step in range(shards // 2):
        send(step).wait()


def outer_step(place, top, bottom, high, low, rim, near, table_high, table_low, q_next, shards, blocks):
    layers, rows, cols = q_next.shape
    depth = cols // 2
    lines = layers * rows
    width = depth // shards
    hbm = pl.BlockSpec(memory_space=pltpu.HBM)
    return pl.pallas_call(
        functools.partial(outer_kernel, blocks),
        in_specs=[smem()] + [vmem()] * 8 + [hbm],
        out_specs=[hbm, hbm],
        out_shape=[
            jax.ShapeDtypeStruct(q_next.shape, F32),
            jax.ShapeDtypeStruct((shards, lines, 2 * width), F32),
        ],
        input_output_aliases={9: 0},
        scratch_shapes=[pltpu.VMEM((layers, 16, cols), F32)]
        + [pltpu.VMEM((cols // LANES, 32 * layers + 8, LANES), F32)] * 7
        + [pltpu.VMEM((2 * lines, depth), BF16)] * 2
        + [
            pltpu.VMEM((shards, lines, 2 * width), F32),
            pltpu.SemaphoreType.DMA((layers, 2)),
            pltpu.SemaphoreType.DMA((shards // 2,)),
        ],
        compiler_params=params(OUTER_LIMIT),
        cost_estimate=pl.CostEstimate(flops=12 * lines * depth * depth, bytes_accessed=4 << 20, transcendentals=0),
        name="outer_step",
    )(place, top, bottom, high, low, rim, near, table_high, table_low, q_next)


def prepare_kernel(shard, eigen, stretch, to_modes, to_layers, theta, ratio, scale, in_high, in_low, out_high, out_low):
    modes, width = theta.shape
    wave = eigen[pl.ds(shard[0], 1), :]
    for mode in range(modes):
        theta[mode : mode + 1, :] = wave + stretch[mode]
    shift = theta[...]
    half = 0.5 * jnp.sqrt(shift)
    angle = 2.0 * jnp.log1p(half + half * half / (1.0 + jnp.sqrt(1.0 + half * half)))
    theta[...] = angle
    ratio[...] = jnp.exp(-angle)
    scale[...] = (-2.0 / (width * eigen.shape[0] + 1)) / jnp.sqrt(shift * (4.0 + shift))

    size = 8 * modes
    line = lax.broadcasted_iota(jnp.int32, (size, modes), 0)
    index = lax.broadcasted_iota(jnp.int32, (size, modes), 1)
    by_layer = (line // 8 == index).astype(F32)
    by_mode = (line % modes == index).astype(F32)
    down = lax.broadcasted_iota(jnp.int32, (size, size), 0)
    along = lax.broadcasted_iota(jnp.int32, (size, size), 1)

    def exact(left, right, sides):
        return lax.dot_general(
            left, right, ((sides, ((), ()))), precision=lax.Precision.HIGHEST, preferred_element_type=F32
        )

    spread = exact(exact(by_mode, to_modes[...], ((1,), (0,))), by_layer, ((1,), (1,)))
    in_high[...], in_low[...] = split(jnp.where(down // modes == along % 8, spread, 0.0))
    spread = exact(exact(by_layer, to_layers[...], ((1,), (0,))), by_mode, ((1,), (1,)))
    out_high[...], out_low[...] = split(jnp.where(down % 8 == along // modes, spread, 0.0))


def prepare(shard, eigen, stretch, to_modes, to_layers):
    modes, width = stretch.shape[0], eigen.shape[1]
    field = jax.ShapeDtypeStruct((modes, width), F32)
    mix = jax.ShapeDtypeStruct((8 * modes, 8 * modes), BF16)
    return pl.pallas_call(
        prepare_kernel,
        in_specs=[smem(), vmem(), smem(), vmem(), vmem()],
        out_specs=[vmem()] * 7,
        out_shape=[field, field, field, mix, mix, mix, mix],
        compiler_params=params(8),
        name="prepare",
    )(shard, eigen, stretch, to_modes, to_layers)


def project_kernel(source, mix_high, mix_low, ratio, modal, ends):
    layers, rows, width = source.shape
    decay = ratio[...]

    def tile(t, sums):
        last, first, scale = sums
        at = pl.ds(pl.multiple_of(8 * t, 8), 8)
        high, low = split(source[:, at, :].reshape(8 * layers, width))
        mixed = dot(mix_high[...], high) + dot(mix_low[...], high) + dot(mix_high[...], low)
        block = mixed.reshape(8, layers, width)
        modal[at] = block
        for row in range(8):
            last = decay * last + block[row]
            first = first + scale * block[row]
            scale = scale * decay
        return last, first, scale

    zeros = jnp.zeros((layers, width), F32)
    last, first, _ = lax.fori_loop(0, rows // 8, tile, (zeros, zeros, zeros + 1.0), unroll=2)
    ends[0] = last
    ends[1] = first


def project(stacked, mix_high, mix_low, ratio):
    layers, rows, width = stacked.shape
    return pl.pallas_call(
        project_kernel,
        in_specs=[vmem()] * 4,
        out_specs=[vmem()] * 2,
        out_shape=[
            jax.ShapeDtypeStruct((rows, layers, width), F32),
            jax.ShapeDtypeStruct((2, layers, width), F32),
        ],
        compiler_params=params(8),
        name="project",
    )(stacked, mix_high, mix_low, ratio)


RADICES = (2, 4, 4)


def exchange(total, level, blocks):
    radix, group = RADICES[level], math.prod(RADICES[:level])
    parts = []
    for shift in range(1, radix):
        pairs = []
        for target in range(blocks):
            spot = (target // group) % radix
            pairs.append((target + ((spot + shift) % radix - spot) * group, target))
        parts.append(lax.ppermute(total, "row", pairs))
    return parts


def decayed(unit, count):
    return jnp.exp(-unit * count.astype(F32))


def join(unit, me, parts, level):
    radix, group = RADICES[level], math.prod(RADICES[:level])
    place = (me // group) % radix
    last = jnp.zeros_like(unit)
    first = jnp.zeros_like(unit)
    for shift, part in enumerate(parts):
        spot = (place + shift) % radix
        last = last + decayed(unit, group * (radix - 1 - spot)) * part[0]
        first = first + decayed(unit, group * spot) * part[1]
    return last, first


def join_kernel(level, rows, place, theta, *refs):
    parts, result = refs[:-1], refs[-1]
    last, first = join(rows * theta[...], place[0], parts, level)
    result[0] = last
    result[1] = first


def join_level(level, rows, place, theta, parts):
    return pl.pallas_call(
        functools.partial(join_kernel, level, rows),
        in_specs=[smem(), vmem()] + [vmem()] * len(parts),
        out_specs=vmem(),
        out_shape=jax.ShapeDtypeStruct(parts[0].shape, F32),
        compiler_params=params(8),
        name="join",
    )(place, theta, *parts)


def entering(theta, rows, me, blocks, levels):
    unit = rows * theta
    above = jnp.zeros_like(theta)
    below = jnp.zeros_like(theta)
    for level, parts in enumerate(levels):
        radix, group = RADICES[level], math.prod(RADICES[:level])
        spot_here, inside = (me // group) % radix, me % group
        for shift in range(1, radix):
            spot = (spot_here + shift) % radix
            over = jnp.maximum(group * (spot_here - 1 - spot), 0) + inside
            under = jnp.maximum(group * (spot - spot_here - 1), 0) + group - 1 - inside
            above = above + jnp.where(spot < spot_here, decayed(unit, over), 0.0) * parts[shift][0]
            below = below + jnp.where(spot > spot_here, decayed(unit, under), 0.0) * parts[shift][1]
    last, first = join(unit, me, levels[-1], len(levels) - 1)
    span = jnp.exp(-theta * (rows * blocks + 1))
    wall = jnp.exp(-theta) / (1.0 - span * span)
    above = above + decayed(unit, me) * wall * (span * last - first)
    below = below + decayed(unit, blocks - 1 - me) * wall * (span * first - last)
    return above, below


def solve_kernel(blocks, place, theta, modal, ratio, scale, mix_high, mix_low, *refs):
    count = sum(RADICES)
    parts, (result, down) = refs[:count], refs[count:]
    rows, layers, width = modal.shape
    decay, factor = ratio[...], scale[...]
    levels, at = [], 0
    for radix in RADICES:
        levels.append(parts[at : at + radix])
        at += radix
    above, below = entering(theta[...], rows, place[0], blocks, levels)

    def forth(row, value):
        value = decay * value + modal[row]
        down[row] = value
        return value

    lax.fori_loop(0, rows, forth, above, unroll=8)

    def tile(step, beyond):
        base = pl.multiple_of(rows - 8 * (step + 1), 8)
        solved = [None] * 8
        for row in range(7, -1, -1):
            value = decay * beyond
            beyond = modal[base + row] + value
            solved[row] = factor * (down[base + row] + value)
        high, low = split(jnp.stack(solved).reshape(8 * layers, width))
        mixed = dot(mix_high[...], high) + dot(mix_low[...], high) + dot(mix_high[...], low)
        result[:, pl.ds(base, 8), :] = mixed.reshape(layers, 8, width)
        return beyond

    lax.fori_loop(0, rows // 8, tile, below, unroll=2)


def solve(place, theta, modal, ratio, scale, mix_high, mix_low, parts, blocks):
    rows, layers, width = modal.shape
    return pl.pallas_call(
        functools.partial(solve_kernel, blocks),
        in_specs=[smem()] + [vmem()] * (6 + len(parts)),
        out_specs=vmem(),
        out_shape=jax.ShapeDtypeStruct((layers, rows, width), F32),
        scratch_shapes=[pltpu.VMEM((rows, layers, width), F32)],
        compiler_params=params(12),
        name="solve",
    )(place, theta, modal, ratio, scale, mix_high, mix_low, *parts)


def inverse_kernel(source, table_high, table_low, result, high, low, held, sems):
    shards, lines, width = source.shape
    width //= 2
    for part in range(shards):
        column = slice(part * width, (part + 1) * width)
        for parity in range(2):
            line = slice(parity * lines, (parity + 1) * lines)
            high[line, column], low[line, column] = split(source[part, :, parity * width : (parity + 1) * width])

    count, _, step = held.shape
    order = LANES - 1 - lax.broadcasted_iota(jnp.int32, (lines, LANES), 1)
    sign = alternating((1, step))

    def copy(block):
        column = pl.ds(block * step, step)
        return pltpu.make_async_copy(held.at[block], result.at[:, column], sems.at[block])

    def columns(index):
        span = slice(index * step, (index + 1) * step)
        value = three_dots(high[...], low[...], table_high[:, span], table_low[:, span])
        odd, even = value[:lines] * sign, value[lines:]
        held[index] = odd + even
        copy(index).start()
        mirror = odd - even
        for part in range(step // LANES):
            block = mirror[:, step - LANES * (part + 1) : step - LANES * part]
            held[count - 1 - index, :, LANES * part : LANES * (part + 1)] = jnp.take_along_axis(block, order, axis=1)
        copy(count - 1 - index).start()

    for index in range(count // 2):
        columns(index)
    for block in range(count):
        copy(block).wait()


def inverse(source, table_high, table_low):
    shards, lines, width = source.shape
    depth = shards * width // 2
    step = 256
    count = 2 * depth // step
    return pl.pallas_call(
        inverse_kernel,
        in_specs=[vmem()] * 3,
        out_specs=pl.BlockSpec(memory_space=pltpu.HBM),
        out_shape=jax.ShapeDtypeStruct((lines, 2 * depth), F32),
        scratch_shapes=[pltpu.VMEM((2 * lines, depth), BF16)] * 2
        + [pltpu.VMEM((count, lines, step), F32), pltpu.SemaphoreType.DMA((count,))],
        compiler_params=params(14),
        name="inverse",
    )(source, table_high, table_low)


def on_device(q_prev, q_now, psi_now, layers_to_modes, modes_to_layers, stretch):
    layer_count, row_count, col_count = q_prev.shape
    blocks = lax.axis_size("row")
    shards = lax.axis_size("layer")
    me = lax.axis_index("row")
    table_high, table_low = (jnp.asarray(value) for value in half_table(col_count))
    eigen = jnp.asarray(column_eigen(col_count, shards))
    place = me.astype(jnp.int32).reshape(1)
    shard = lax.axis_index("layer").astype(jnp.int32).reshape(1)

    initial, last = rims(q_prev, q_now, psi_now)
    pairs = [(i, i + 1) for i in range(blocks - 1)]
    top = lax.ppermute(last, "row", pairs)
    bottom = lax.ppermute(initial, "row", [(j, i) for i, j in pairs])
    theta, ratio, scale, *mixes = prepare(shard, eigen, stretch, layers_to_modes, modes_to_layers)
    q_next, *folded, table_high, table_low = inner_step(q_prev, q_now, psi_now, table_high, table_low)
    q_next, spectrum = outer_step(place, top, bottom, *folded, table_high, table_low, q_next, shards, blocks)
    stacked = lax.all_to_all(spectrum, "layer", split_axis=0, concat_axis=0, tiled=True)
    stacked = stacked.reshape(shards * layer_count, row_count, -1)
    modal, total = project(stacked, mixes[0], mixes[1], ratio)
    parts = []
    for level in range(len(RADICES)):
        group = [total] + exchange(total, level, blocks)
        parts.extend(group)
        if level + 1 < len(RADICES):
            total = join_level(level, row_count, place, theta, group)
    layered = solve(place, theta, modal, ratio, scale, mixes[2], mixes[3], parts, blocks)
    layered = layered.reshape(shards, layer_count * row_count, -1)
    returned = lax.all_to_all(layered, "layer", split_axis=0, concat_axis=0, tiled=True)
    psi_next = inverse(returned, table_high, table_low)
    return (q_next, psi_next.reshape(q_prev.shape))


def solution(mesh):
    return jax.shard_map(
        on_device,
        mesh=mesh,
        in_specs=(
            P("layer", "row", None),
            P("layer", "row", None),
            P("layer", "row", None),
            P(),
            P(),
            P(),
        ),
        out_specs=(P("layer", "row", None), P("layer", "row", None)),
        check_vma=False,
    )
```

time: 126 us -> 121 us (0.960)
  starting transfers between devices: 30.2 us -> 25.4 us
  waiting for transfers between devices: 32.5 us -> 36.9 us
  blocking collectives: 30.6 us -> 28.1 us
  Pallas kernels: 29.1 us -> 26.7 us
    ppermute x7, waiting for transfers between devices: 5.97 us -> 12.5 us  [exchange(): parts.append(lax.ppermute(total, 'row', pairs))]
    ppermute x7, starting transfers between devices: 21.1 us -> 16.3 us  [exchange(): parts.append(lax.ppermute(total, 'row', pairs))]
    ppermute x1, waiting for transfers between devices: 3.4 us -> 0.01 us  [on_device(): bottom = lax.ppermute(initial, 'row', [(j, i) for i, j in pairs])]
    all_to_all x1, blocking collectives: 30.6 us -> 28.1 us  [on_device(): lax.all_to_all(layered, 'layer', split_axis=0, concat_axis=0, tiled=True)]
    pallas_call x5 -> x6, Pallas kernels: 26.9 us -> 24.5 us  [the longest x1 8.23 us: inner_step(): pl.pallas_call(inner_kernel, grid=(layers,), in_specs=[hbm] * 5, out_spec...]
  transfers between devices with their start and end apart: 10 -> 10, of which waited for: 6 -> 7; matrix products, arithmetic and copies ran while one was open for 0% -> 0% of each run, Pallas kernels for 1% -> 8%
where the time goes in v3:
time: 121 us; the launch traced here: 119 us
  waiting for transfers between devices  36.9 us (30%)
  blocking collectives  28.1 us (23%)
  Pallas kernels  26.7 us (22%)
  starting transfers between devices  25.4 us (21%)
  local copies, waits for them, and re-layouts  1.35 us (1%)
    all_to_all x1, blocking collectives, on_device(): lax.all_to_all(layered, 'layer', split_axis=0, concat_axis=0, tiled=True)  28.1 us
    all_to_all x1, waiting for transfers between devices, on_device(): lax.all_to_all(spectrum, 'layer', split_axis=0, concat_axis=0, tiled=True)  24.4 us
    ppermute x7, starting transfers between devices, exchange(): parts.append(lax.ppermute(total, 'row', pairs))  16.3 us
    ppermute x7, waiting for transfers between devices, exchange(): parts.append(lax.ppermute(total, 'row', pairs))  12.5 us
    pallas_call x1, Pallas kernels, inner_step(): pl.pallas_call(inner_kernel, grid=(layers,), in_specs=[hbm] * 5, out_spec...  8.23 us
    pallas_call x1, Pallas kernels, outer_step(): pl.pallas_call(functools.partial(outer_kernel, blocks), in_specs=[smem()]...  6.26 us
    all_to_all x1, starting transfers between devices, on_device(): lax.all_to_all(spectrum, 'layer', split_axis=0, concat_axis=0, tiled=True)  6.08 us
    pallas_call x1, Pallas kernels, inverse(): pl.pallas_call(inverse_kernel, in_specs=[vmem()] * 3, out_specs=pl.BlockS...  4.58 us
  transfers between devices with their start and end apart: 10, of which 7 were waited for; matrix products, arithmetic and copies ran while one was open for 0% of the time, Pallas kernels for 8%

profile of v3, /device:TPU:32, one launch (start us, length us, event | category | flops | bytes accessed | tf_op | source)
XLA Modules:
  0.0 119.4 jit_solution(10734283224505034258)
XLA Ops:
  0.6 2.1 %rims.1 = (f32[4,4,2048]{2,1,0:T(4,128)}, f32[4,4,2048]{2,1,0:T(4,128)}) custom-call(f32[4,64,2048]{2,1,0:T(8,128)} %prev.1, f32[4,64,2048]{2,1,0:T(8,128)} %now.1, f32[4,64,2048]{2,1,0:T(8,128)} %psi.1, f32[4,64,2048]{2,1,0:T(8,128)} %prev.1, f32[4,64,2048]{2,1,0:T(8,128)} %now.1, f32[4,64,2048]{2,1,0:T(8,128)} %psi.1), custom_call_target="tpu_custom_call" | custom-call | tf_op jit(solution)/shard_map/rims/pallas_call | solution.py:87
  2.7 1.7 %collective-permute-start = (f32[4,4,2048]{2,1,0:T(4,128)}, f32[4,4,2048]{2,1,0:T(4,128)S(1)}, u32[]{:S(2)}, u32[]{:S(2)}) collective-permute-start(f32[4,4,2048]{2,1,0:T(4,128)} %get-tuple-element.22), channel_id=1, source_target_pairs={{0,1},{1,2},{2,3},{3,4},{4,5},{5,6},{6,7},{7,8},{8,9},{9,10},{10,1... | collective-permute-start | bytes 393224 | tf_op jit(solution)/shard_map/ppermute | solution.py:668
  4.5 1.3 %collective-permute-start.1 = (f32[4,4,2048]{2,1,0:T(4,128)}, f32[4,4,2048]{2,1,0:T(4,128)S(1)}, u32[]{:S(2)}, u32[]{:S(2)}) collective-permute-start(f32[4,4,2048]{2,1,0:T(4,128)} %get-tuple-element.23), channel_id=1, source_target_pairs={{1,0},{2,1},{3,2},{4,3},{5,4},{6,5},{7,6},{8,7},{9,8},{10,9},{11,1... | collective-permute-start | bytes 393224 | tf_op jit(solution)/shard_map/ppermute | solution.py:669
  5.8 8.2 %inner_step.1 = (f32[4,64,2048]{2,1,0:T(8,128)}, bf16[384,1024]{1,0:T(8,128)(2,1)S(1)}, bf16[384,1024]{1,0:T(8,128)(2,1)S(1)}, f32[4,16,2048]{2,1,0:T(8,128)S(1)...) custom-call(f32[4,64,2048]{2,1,0:T(8,128)} %prev.1, ...), custom_call_target="tpu_custom_call" | custom-call | flops 31457280 | bytes 12582912 | tf_op jit(solution)/shard_map/inner_step/pallas_call | solution.py:264
  14.0 0.0 copy-start.1
  14.0 0.0 copy-start.3
  14.0 0.0 collective-permute-done.top
  14.0 0.0 collective-permute-done.1.bottom
  14.1 6.3 %outer_step.1 = (f32[4,64,2048]{2,1,0:T(8,128)}, f32[8,256,256]{2,1,0:T(8,128)S(1)}) custom-call(s32[1]{0:T(128)} %bitcast.place, f32[4,4,2048]{2,1,0:T(4,128)S(1)} %collective-permute-done.top, f32[4,4,2048]{2,1,0:T(4,128)S(1)} %collective-permute-done.1.bottom, bf16[384,1024]{1,0:T(8,128)(2,1)S(1)} %get-tuple-element.24.high_in, ...), custom_call_target="tpu_custom_call", output_to_operand_aliasing={{0}: (9, {})} | custom-call | flops 3221225472 | bytes 4194304 | tf_op jit(solution)/shard_map/outer_step/pallas_call | solution.py:382
  20.3 0.0 copy-done.1
  20.3 0.0 copy-done.3
  20.3 0.0 copy-start
  20.3 1.3 %copy-done = f32[8,256,256]{2,1,0:T(8,128)} copy-done((f32[8,256,256]{2,1,0:T(8,128)}, f32[8,256,256]{2,1,0:T(8,128)S(1)}, u32[]{:S(2)}) %copy-start) | copy-done | bytes 2097176
  21.7 0.0 copy-start.5
  21.7 0.0 copy-start.6
  21.7 0.0 copy-start.7
  21.7 0.0 copy-start.8
  21.7 6.1 %all-to-all-start = ((f32[8,256,256]{2,1,0:T(8,128)}), f32[8,256,256]{2,1,0:T(8,128)S(1)}, u32[]{:S(2)}, u32[]{:S(2)}) async-start(f32[8,256,256]{2,1,0:T(8,128)} %copy-done), calls=%async_computation | async-start | bytes 4194304 | tf_op jit(solution)/shard_map/all_to_all | solution.py:673
  27.8 0.0 copy-done.5
  27.8 0.0 copy-done.6
  27.8 0.0 copy-done.7
  27.8 0.0 copy-done.8
  27.8 1.6 %prepare.1 = (f32[32,256]{1,0:T(8,128)S(1)}, f32[32,256]{1,0:T(8,128)S(1)}, f32[32,256]{1,0:T(8,128)S(1)}, bf16[256,256]{1,0:T(8,128)(2,1)S(1)}, bf16[256,256]{1...) custom-call(s32[1]{0:T(128)} %bitcast.1.shard, f32[8,256]{1,0:T(8,128)S(1)} %copy-done.7, ...), custom_call_target="tpu_custom_call" | custom-call | tf_op jit(solution)/shard_map/prepare/pallas_call | solution.py:440
  29.4 24.4 %all-to-all-done = f32[8,256,256]{2,1,0:T(8,128)S(1)} async-done(((f32[8,256,256]{2,1,0:T(8,128)}), f32[8,256,256]{2,1,0:T(8,128)S(1)}, u32[]{:S(2)}, u32[]{:S(2)}) %all-to-all-start) | async-done | bytes 2097184 | tf_op jit(solution)/shard_map/all_to_all | solution.py:673
  53.8 1.7 %project.1 = (f32[64,32,256]{2,1,0:T(8,128)S(1)}, f32[2,32,256]{2,1,0:T(8,128)S(1)}) custom-call(f32[32,64,256]{2,1,0:T(8,128)S(1)} %bitcast.5, bf16[256,256]{1,0:T(8,128)(2,1)S(1)} %get-tuple-element.34.mix_high, bf16[256,256]{1,0:T(8,128)(2,1)S(1)} %get-tuple-element.35.mix_low, f32[32,256]{1,0:T(8,128)S(1)} %get-tuple-element.36.ratio), custom_call_target="tpu_custom_call" | custom-call | tf_op jit(solution)/shard_map/project/pallas_call | solution.py:475
  55.5 1.1 collective-permute-start.2
  56.6 0.9 collective-permute-done.2.refs_1_
  57.5 5.6 %collective-permute-start.3 = (f32[2,32,256]{2,1,0:T(8,128)S(1)}, f32[2,32,256]{2,1,0:T(8,128)S(1)}, u32[]{:S(2)}, u32[]{:S(2)}) collective-permute-start(f32[2,32,256]{2,1,0:T(8,128)S(1)} %join.2.refs_0_.refs_2_), channel_id=1, source_target_pairs={{2,0},{3,1},{4,2},{5,3},{6,4},{7,5},{0,6},{1,7},{10,8},{11,9},{12,... | collective-permute-start | bytes 196616 | tf_op jit(solution)/shard_map/ppermute | solution.py:499
  63.1 0.0 collective-permute-start.4
  63.1 1.0 collective-permute-start.5
  64.0 2.2 %collective-permute-done.3.refs_1_.refs_3_ = f32[2,32,256]{2,1,0:T(8,128)S(1)} collective-permute-done((f32[2,32,256]{2,1,0:T(8,128)S(1)}, f32[2,32,256]{2,1,0:T(8,128)S(1)}, u32[]{:S(2)}, u32[]{:S(2)}) %collective-permute-start.3) | collective-permute-done | bytes 65568 | tf_op jit(solution)/shard_map/ppermute | solution.py:499
  66.2 3.0 %collective-permute-done.4.refs_2_.refs_4_ = f32[2,32,256]{2,1,0:T(8,128)S(1)} collective-permute-done((f32[2,32,256]{2,1,0:T(8,128)S(1)}, f32[2,32,256]{2,1,0:T(8,128)S(1)}, u32[]{:S(2)}, u32[]{:S(2)}) %collective-permute-start.4) | collective-permute-done | bytes 65568 | tf_op jit(solution)/shard_map/ppermute | solution.py:499
  69.2 0.4 collective-permute-done.5.refs_3_.refs_5_
  69.6 0.1 join.3.refs_6_
  69.6 4.2 %collective-permute-start.6 = (f32[2,32,256]{2,1,0:T(8,128)S(1)}, f32[2,32,256]{2,1,0:T(8,128)S(1)}, u32[]{:S(2)}, u32[]{:S(2)}) collective-permute-start(f32[2,32,256]{2,1,0:T(8,128)S(1)} %join.3.refs_6_), channel_id=1, source_target_pairs={{8,0},{9,1},{10,2},{11,3},{12,4},{13,5},{14,6},{15,7},{16,8},{17,9... | collective-permute-start | bytes 196616 | tf_op jit(solution)/shard_map/ppermute | solution.py:499
  73.8 2.7 %collective-permute-start.7 = (f32[2,32,256]{2,1,0:T(8,128)S(1)}, f32[2,32,256]{2,1,0:T(8,128)S(1)}, u32[]{:S(2)}, u32[]{:S(2)}) collective-permute-start(f32[2,32,256]{2,1,0:T(8,128)S(1)} %join.3.refs_6_), channel_id=1, source_target_pairs={{16,0},{17,1},{18,2},{19,3},{20,4},{21,5},{22,6},{23,7},{24,8},{25... | collective-permute-start | bytes 196616 | tf_op jit(solution)/shard_map/ppermute | solution.py:499
  76.5 1.8 %collective-permute-start.8 = (f32[2,32,256]{2,1,0:T(8,128)S(1)}, f32[2,32,256]{2,1,0:T(8,128)S(1)}, u32[]{:S(2)}, u32[]{:S(2)}) collective-permute-start(f32[2,32,256]{2,1,0:T(8,128)S(1)} %join.3.refs_6_), channel_id=1, source_target_pairs={{24,0},{25,1},{26,2},{27,3},{28,4},{29,5},{30,6},{31,7},{0,8},{1,9... | collective-permute-start | bytes 196616 | tf_op jit(solution)/shard_map/ppermute | solution.py:499
  78.4 0.0 collective-permute-done.6.refs_7_
  78.4 4.1 %collective-permute-done.7.refs_8_ = f32[2,32,256]{2,1,0:T(8,128)S(1)} collective-permute-done((f32[2,32,256]{2,1,0:T(8,128)S(1)}, f32[2,32,256]{2,1,0:T(8,128)S(1)}, u32[]{:S(2)}, u32[]{:S(2)}) %collective-permute-start.7) | collective-permute-done | bytes 65568 | tf_op jit(solution)/shard_map/ppermute | solution.py:499
  82.5 2.0 %collective-permute-done.8.refs_9_ = f32[2,32,256]{2,1,0:T(8,128)S(1)} collective-permute-done((f32[2,32,256]{2,1,0:T(8,128)S(1)}, f32[2,32,256]{2,1,0:T(8,128)S(1)}, u32[]{:S(2)}, u32[]{:S(2)}) %collective-permute-start.8) | collective-permute-done | bytes 65568 | tf_op jit(solution)/shard_map/ppermute | solution.py:499
  84.5 2.1 %solve.1 = f32[32,64,256]{2,1,0:T(8,128)S(1)} custom-call(s32[1]{0:T(128)} %bitcast.place, f32[32,256]{1,0:T(8,128)S(1)} %get-tuple-element.32.theta, f32[64,32,256]{2,1,0:T(8,128)S(1)} %get-tuple-element.37.modal, f32[32,256]{1,0:T(8,128)S(1)} %get-tuple-element.36.ratio, f32[32,256]{1,0:T(8,128)S(1)} %get-tuple-element.38.scale, ...), custom_call_target="tpu_custom_call" | custom-call | tf_op jit(solution)/shard_map/solve/pallas_call | solution.py:593
  86.6 0.0 copy-start.2
  86.6 0.0 copy-start.4
  86.6 28.1 %all_to_all.10.source = f32[8,256,256]{2,1,0:T(8,128)S(1)} all-to-all(f32[8,256,256]{2,1,0:T(8,128)S(1)} %bitcast.6), channel_id=1, replica_groups=mesh['layer'=8,'row'=32] {'layer'}, dimensions={0} | all-to-all | bytes 4194304 | tf_op jit(solution)/shard_map/all_to_all | solution.py:684
  114.7 0.0 copy-done.2
  114.7 0.0 copy-done.4
  114.7 4.6 %inverse.1 = f32[256,2048]{1,0:T(8,128)} custom-call(f32[8,256,256]{2,1,0:T(8,128)S(1)} %all_to_all.10.source, bf16[1024,1024]{1,0:T(8,128)(2,1)S(1)} %copy-done.2, bf16[1024,1024]{1,0:T(8,128)(2,1)S(1)} %copy-done.4), custom_call_target="tpu_custom_call" | custom-call | tf_op jit(solution)/shard_map/inverse/pallas_call | solution.py:644
  (1 shorter events, 0.0 us)
Async XLA Ops:
  2.7 11.3 %collective-permute-start = (f32[4,4,2048]{2,1,0:T(4,128)}, f32[4,4,2048]{2,1,0:T(4,128)S(1)}, u32[]{:S(2)}, u32[]{:S(2)}) collective-permute-start(f32[4,4,2048]{2,1,0:T(4,128)} %get-tuple-element.22), channel_id=1, source_target_pairs={{0,1},{1,2},{2,3},{3,4},{4,5},{5,6},{6,7},{7,8},{8,9},{9,10},{10,1... | collective-permute-start | bytes 393224 | tf_op jit(solution)/shard_map/ppermute | solution.py:668
  4.5 9.6 %collective-permute-start.1 = (f32[4,4,2048]{2,1,0:T(4,128)}, f32[4,4,2048]{2,1,0:T(4,128)S(1)}, u32[]{:S(2)}, u32[]{:S(2)}) collective-permute-start(f32[4,4,2048]{2,1,0:T(4,128)} %get-tuple-element.23), channel_id=1, source_target_pairs={{1,0},{2,1},{3,2},{4,3},{5,4},{6,5},{7,6},{8,7},{9,8},{10,9},{11,1... | collective-permute-start | bytes 393224 | tf_op jit(solution)/shard_map/ppermute | solution.py:669
  14.0 6.3 %copy-start.1 = (bf16[1024,1024]{1,0:T(8,128)(2,1)}, bf16[1024,1024]{1,0:T(8,128)(2,1)S(1)}, u32[]{:S(2)}) copy-start(bf16[1024,1024]{1,0:T(8,128)(2,1)S(1)} %get-tuple-element.28.table_high) | copy-start | bytes 6291460
  14.0 6.3 %copy-start.3 = (bf16[1024,1024]{1,0:T(8,128)(2,1)}, bf16[1024,1024]{1,0:T(8,128)(2,1)S(1)}, u32[]{:S(2)}) copy-start(bf16[1024,1024]{1,0:T(8,128)(2,1)S(1)} %get-tuple-element.29.table_low) | copy-start | bytes 6291460
  20.3 1.3 %copy-start = (f32[8,256,256]{2,1,0:T(8,128)}, f32[8,256,256]{2,1,0:T(8,128)S(1)}, u32[]{:S(2)}) copy-start(f32[8,256,256]{2,1,0:T(8,128)S(1)} %get-tuple-element.33) | copy-start | bytes 6291460
  21.7 6.1 %copy-start.5 = (f32[32,32]{1,0:T(8,128)S(1)}, f32[32,32]{1,0:T(8,128)}, u32[]{:S(2)}) copy-start(f32[32,32]{1,0:T(8,128)} %to_modes.1) | copy-start | bytes 12292
  21.7 6.1 %copy-start.6 = (f32[32,32]{1,0:T(8,128)S(1)}, f32[32,32]{1,0:T(8,128)}, u32[]{:S(2)}) copy-start(f32[32,32]{1,0:T(8,128)} %to_layers.1) | copy-start | bytes 12292
  21.7 6.1 %copy-start.7 = (f32[8,256]{1,0:T(8,128)S(1)}, f32[8,256]{1,0:T(8,128)}, u32[]{:S(2)}) copy-start(f32[8,256]{1,0:T(8,128)} %constant.17.clone.eigen) | copy-start | bytes 24580
  21.7 6.1 %copy-start.8 = (f32[32]{0:T(128)S(1)}, f32[32]{0:T(128)}, u32[]{:S(2)}) copy-start(f32[32]{0:T(128)} %stretch.1) | copy-start | bytes 388
  21.7 32.1 %all-to-all-start = ((f32[8,256,256]{2,1,0:T(8,128)}), f32[8,256,256]{2,1,0:T(8,128)S(1)}, u32[]{:S(2)}, u32[]{:S(2)}) async-start(f32[8,256,256]{2,1,0:T(8,128)} %copy-done), calls=%async_computation | async-start | bytes 4194304 | tf_op jit(solution)/shard_map/all_to_all | solution.py:673
  55.5 2.0 %collective-permute-start.2 = (f32[2,32,256]{2,1,0:T(8,128)S(1)}, f32[2,32,256]{2,1,0:T(8,128)S(1)}, u32[]{:S(2)}, u32[]{:S(2)}) collective-permute-start(f32[2,32,256]{2,1,0:T(8,128)S(1)} %get-tuple-element.41.refs_0_), channel_id=1, source_target_pairs={{1,0},{0,1},{3,2},{2,3},{5,4},{4,5},{7,6},{6,7},{9,8},{8,9},{11,10... | collective-permute-start | bytes 196616 | tf_op jit(solution)/shard_map/ppermute | solution.py:499
  57.5 8.7 %collective-permute-start.3 = (f32[2,32,256]{2,1,0:T(8,128)S(1)}, f32[2,32,256]{2,1,0:T(8,128)S(1)}, u32[]{:S(2)}, u32[]{:S(2)}) collective-permute-start(f32[2,32,256]{2,1,0:T(8,128)S(1)} %join.2.refs_0_.refs_2_), channel_id=1, source_target_pairs={{2,0},{3,1},{4,2},{5,3},{6,4},{7,5},{0,6},{1,7},{10,8},{11,9},{12,... | collective-permute-start | bytes 196616 | tf_op jit(solution)/shard_map/ppermute | solution.py:499
  63.1 6.1 %collective-permute-start.4 = (f32[2,32,256]{2,1,0:T(8,128)S(1)}, f32[2,32,256]{2,1,0:T(8,128)S(1)}, u32[]{:S(2)}, u32[]{:S(2)}) collective-permute-start(f32[2,32,256]{2,1,0:T(8,128)S(1)} %join.2.refs_0_.refs_2_), channel_id=1, source_target_pairs={{4,0},{5,1},{6,2},{7,3},{0,4},{1,5},{2,6},{3,7},{12,8},{13,9},{14,... | collective-permute-start | bytes 196616 | tf_op jit(solution)/shard_map/ppermute | solution.py:499
  63.1 6.5 %collective-permute-start.5 = (f32[2,32,256]{2,1,0:T(8,128)S(1)}, f32[2,32,256]{2,1,0:T(8,128)S(1)}, u32[]{:S(2)}, u32[]{:S(2)}) collective-permute-start(f32[2,32,256]{2,1,0:T(8,128)S(1)} %join.2.refs_0_.refs_2_), channel_id=1, source_target_pairs={{6,0},{7,1},{0,2},{1,3},{2,4},{3,5},{4,6},{5,7},{14,8},{15,9},{8,1... | collective-permute-start | bytes 196616 | tf_op jit(solution)/shard_map/ppermute | solution.py:499
  69.6 8.7 %collective-permute-start.6 = (f32[2,32,256]{2,1,0:T(8,128)S(1)}, f32[2,32,256]{2,1,0:T(8,128)S(1)}, u32[]{:S(2)}, u32[]{:S(2)}) collective-permute-start(f32[2,32,256]{2,1,0:T(8,128)S(1)} %join.3.refs_6_), channel_id=1, source_target_pairs={{8,0},{9,1},{10,2},{11,3},{12,4},{13,5},{14,6},{15,7},{16,8},{17,9... | collective-permute-start | bytes 196616 | tf_op jit(solution)/shard_map/ppermute | solution.py:499
  73.8 8.7 %collective-permute-start.7 = (f32[2,32,256]{2,1,0:T(8,128)S(1)}, f32[2,32,256]{2,1,0:T(8,128)S(1)}, u32[]{:S(2)}, u32[]{:S(2)}) collective-permute-start(f32[2,32,256]{2,1,0:T(8,128)S(1)} %join.3.refs_6_), channel_id=1, source_target_pairs={{16,0},{17,1},{18,2},{19,3},{20,4},{21,5},{22,6},{23,7},{24,8},{25... | collective-permute-start | bytes 196616 | tf_op jit(solution)/shard_map/ppermute | solution.py:499
  76.5 8.0 %collective-permute-start.8 = (f32[2,32,256]{2,1,0:T(8,128)S(1)}, f32[2,32,256]{2,1,0:T(8,128)S(1)}, u32[]{:S(2)}, u32[]{:S(2)}) collective-permute-start(f32[2,32,256]{2,1,0:T(8,128)S(1)} %join.3.refs_6_), channel_id=1, source_target_pairs={{24,0},{25,1},{26,2},{27,3},{28,4},{29,5},{30,6},{31,7},{0,8},{1,9... | collective-permute-start | bytes 196616 | tf_op jit(solution)/shard_map/ppermute | solution.py:499
  86.6 28.1 %copy-start.2 = (bf16[1024,1024]{1,0:T(8,128)(2,1)S(1)}, bf16[1024,1024]{1,0:T(8,128)(2,1)}, u32[]{:S(2)}) copy-start(bf16[1024,1024]{1,0:T(8,128)(2,1)} %copy-done.1) | copy-start | bytes 6291460
  86.6 28.1 %copy-start.4 = (bf16[1024,1024]{1,0:T(8,128)(2,1)S(1)}, bf16[1024,1024]{1,0:T(8,128)(2,1)}, u32[]{:S(2)}) copy-start(bf16[1024,1024]{1,0:T(8,128)(2,1)} %copy-done.3) | copy-start | bytes 6291460

commit v4 on v3

--- a/solution.py
+++ b/solution.py
@@ -66,6 +66,17 @@
 
 def smem():
     return pl.BlockSpec(memory_space=pltpu.SMEM)
+
+
+MOVES = ((0, 0), (2, 1), (2, 0), (1, 1), (3, 1), (1, 0), (3, 0), (0, 1))
+
+
+def target_shard(shard, move):
+    return lax.rem(shard // 2 + move[0], 4) * 2 + lax.rem(shard % 2 + move[1], 2)
+
+
+def source_shard(shard, move):
+    return lax.rem(shard // 2 + 4 - move[0], 4) * 2 + lax.rem(shard % 2 + move[1], 2)
 
 
 def rim_kernel(prev_first, now_first, psi_first, prev_last, now_last, psi_last, initial, last):
@@ -288,8 +299,9 @@
     )(q_prev, q_now, psi_now, table_high, table_low)
 
 
-def outer_kernel(blocks, place, top, bottom, high_in, low_in, rim, near, table_high, table_low, q_in, q_out, spectrum, *scratch):
-    q_rim, p, z, ze, zw, q, qe, qw, high, low, held, q_sems, sems = scratch
+def outer_kernel(blocks, place, shard, top, bottom, high_in, low_in, rim, near, table_high, table_low, q_in, q_out, *refs):
+    leaving, scratch = refs[: len(MOVES)], refs[len(MOVES) :]
+    q_rim, p, z, ze, zw, q, qe, qw, high, low, held, q_sems = scratch
     layers, _, cols = rim.shape
     shards, lines, width = held.shape
     width //= 2
@@ -346,10 +358,6 @@
 
         fold_columns(cols // LANES, 16, read, write)
 
-    def send(step):
-        block = pl.ds(2 * step, 2)
-        return pltpu.make_async_copy(held.at[block], spectrum.at[block], sems.at[step])
-
     def columns(step, carry):
         span = pl.ds(pl.multiple_of(step * 2 * width, 2 * width), 2 * width)
         value = three_dots(high[...], low[...], table_high[:, span], table_low[:, span])
@@ -362,18 +370,17 @@
                     held[2 * step + part, to + 8 : to + 8 + inner, lane] = value[start : start + inner, column]
                     held[2 * step + part, to : to + 8, lane] = value[start + inner : start + inner + 8, column]
                     held[2 * step + part, to + rows - 8 : to + rows, lane] = value[start + rows - 8 : start + rows, column]
-        send(step).start()
         return carry
 
     lax.fori_loop(0, shards // 2, columns, 0)
+    for move, piece in zip(MOVES, leaving):
+        piece[...] = held[target_shard(shard[0], move)]
     for n in range(layers):
         for edge in range(2):
             save(n, edge).wait()
-    for step in range(shards // 2):
-        send(step).wait()
-
-
-def outer_step(place, top, bottom, high, low, rim, near, table_high, table_low, q_next, shards, blocks):
+
+
+def outer_step(place, shard, top, bottom, high, low, rim, near, table_high, table_low, q_next, shards, blocks):
     layers, rows, cols = q_next.shape
     depth = cols // 2
     lines = layers * rows
@@ -381,25 +388,29 @@
     hbm = pl.BlockSpec(memory_space=pltpu.HBM)
     return pl.pallas_call(
         functools.partial(outer_kernel, blocks),
-        in_specs=[smem()] + [vmem()] * 8 + [hbm],
-        out_specs=[hbm, hbm],
-        out_shape=[
-            jax.ShapeDtypeStruct(q_next.shape, F32),
-            jax.ShapeDtypeStruct((shards, lines, 2 * width), F32),
-        ],
-        input_output_aliases={9: 0},
+        in_specs=[smem()] * 2 + [vmem()] * 8 + [hbm],
+        out_specs=[hbm] + [vmem()] * len(MOVES),
+        out_shape=[jax.ShapeDtypeStruct(q_next.shape, F32)]
+        + [jax.ShapeDtypeStruct((lines, 2 * width), F32)] * len(MOVES),
+        input_output_aliases={10: 0},
         scratch_shapes=[pltpu.VMEM((layers, 16, cols), F32)]
         + [pltpu.VMEM((cols // LANES, 32 * layers + 8, LANES), F32)] * 7
         + [pltpu.VMEM((2 * lines, depth), BF16)] * 2
         + [
             pltpu.VMEM((shards, lines, 2 * width), F32),
             pltpu.SemaphoreType.DMA((layers, 2)),
-            pltpu.SemaphoreType.DMA((shards // 2,)),
         ],
         compiler_params=params(OUTER_LIMIT),
         cost_estimate=pl.CostEstimate(flops=12 * lines * depth * depth, bytes_accessed=4 << 20, transcendentals=0),
         name="outer_step",
-    )(place, top, bottom, high, low, rim, near, table_high, table_low, q_next)
+    )(place, shard, top, bottom, high, low, rim, near, table_high, table_low, q_next)
+
+
+def choose(which, piece):
+    total = 0
+    for number, move in enumerate(MOVES):
+        total = total + jnp.where(piece == number, move[which], 0)
+    return total
 
 
 def prepare_kernel(shard, eigen, stretch, to_modes, to_layers, theta, ratio, scale, in_high, in_low, out_high, out_low):
@@ -417,7 +428,16 @@
     size = 8 * modes
     line = lax.broadcasted_iota(jnp.int32, (size, modes), 0)
     index = lax.broadcasted_iota(jnp.int32, (size, modes), 1)
-    by_layer = (line // 8 == index).astype(F32)
+
+    piece = line // (size // len(MOVES))
+    share = modes // len(MOVES)
+
+    def layer_of(around, across):
+        other = lax.rem(shard[0] // 2 + around, 4) * 2 + lax.rem(shard[0] % 2 + across, 2)
+        return (other * share + (line // 8) % share == index).astype(F32)
+
+    arriving = layer_of(4 - choose(0, piece), choose(1, piece))
+    leaving = layer_of(choose(0, piece), choose(1, piece))
     by_mode = (line % modes == index).astype(F32)
     down = lax.broadcasted_iota(jnp.int32, (size, size), 0)
     along = lax.broadcasted_iota(jnp.int32, (size, size), 1)
@@ -427,9 +447,9 @@
             left, right, ((sides, ((), ()))), precision=lax.Precision.HIGHEST, preferred_element_type=F32
         )
 
-    spread = exact(exact(by_mode, to_modes[...], ((1,), (0,))), by_layer, ((1,), (1,)))
+    spread = exact(exact(by_mode, to_modes[...], ((1,), (0,))), arriving, ((1,), (1,)))
     in_high[...], in_low[...] = split(jnp.where(down // modes == along % 8, spread, 0.0))
-    spread = exact(exact(by_layer, to_layers[...], ((1,), (0,))), by_mode, ((1,), (1,)))
+    spread = exact(exact(leaving, to_layers[...], ((1,), (0,))), by_mode, ((1,), (1,)))
     out_high[...], out_low[...] = split(jnp.where(down % 8 == along // modes, spread, 0.0))
 
 
@@ -447,14 +467,17 @@
     )(shard, eigen, stretch, to_modes, to_layers)
 
 
-def project_kernel(source, mix_high, mix_low, ratio, modal, ends):
-    layers, rows, width = source.shape
+def project_kernel(mix_high, mix_low, ratio, *refs):
+    pieces, (modal, ends) = refs[:-2], refs[-2:]
+    rows, layers, width = modal.shape
+    share = layers // len(pieces)
     decay = ratio[...]
 
     def tile(t, sums):
         last, first, scale = sums
         at = pl.ds(pl.multiple_of(8 * t, 8), 8)
-        high, low = split(source[:, at, :].reshape(8 * layers, width))
+        lines = [piece[:, at, :].reshape(8 * share, width) for piece in pieces]
+        high, low = split(jnp.concatenate(lines, axis=0))
         mixed = dot(mix_high[...], high) + dot(mix_low[...], high) + dot(mix_high[...], low)
         block = mixed.reshape(8, layers, width)
         modal[at] = block
@@ -470,11 +493,12 @@
     ends[1] = first
 
 
-def project(stacked, mix_high, mix_low, ratio):
-    layers, rows, width = stacked.shape
+def project(pieces, mix_high, mix_low, ratio):
+    share, rows, width = pieces[0].shape
+    layers = share * len(pieces)
     return pl.pallas_call(
         project_kernel,
-        in_specs=[vmem()] * 4,
+        in_specs=[vmem()] * (3 + len(pieces)),
         out_specs=[vmem()] * 2,
         out_shape=[
             jax.ShapeDtypeStruct((rows, layers, width), F32),
@@ -482,7 +506,7 @@
         ],
         compiler_params=params(8),
         name="project",
-    )(stacked, mix_high, mix_low, ratio)
+    )(mix_high, mix_low, ratio, *pieces)
 
 
 RADICES = (2, 4, 4)
@@ -557,8 +581,9 @@
 
 def solve_kernel(blocks, place, theta, modal, ratio, scale, mix_high, mix_low, *refs):
     count = sum(RADICES)
-    parts, (result, down) = refs[:count], refs[count:]
+    parts, results, down = refs[:count], refs[count:-1], refs[-1]
     rows, layers, width = modal.shape
+    share = layers // len(results)
     decay, factor = ratio[...], scale[...]
     levels, at = [], 0
     for radix in RADICES:
@@ -582,7 +607,9 @@
             solved[row] = factor * (down[base + row] + value)
         high, low = split(jnp.stack(solved).reshape(8 * layers, width))
         mixed = dot(mix_high[...], high) + dot(mix_low[...], high) + dot(mix_high[...], low)
-        result[:, pl.ds(base, 8), :] = mixed.reshape(layers, 8, width)
+        for number, result in enumerate(results):
+            piece = mixed[8 * share * number : 8 * share * (number + 1)]
+            result[:, pl.ds(base, 8), :] = piece.reshape(share, 8, width)
         return beyond
 
     lax.fori_loop(0, rows // 8, tile, below, unroll=2)
@@ -593,34 +620,50 @@
     return pl.pallas_call(
         functools.partial(solve_kernel, blocks),
         in_specs=[smem()] + [vmem()] * (6 + len(parts)),
-        out_specs=vmem(),
-        out_shape=jax.ShapeDtypeStruct((layers, rows, width), F32),
+        out_specs=[vmem()] * len(MOVES),
+        out_shape=[jax.ShapeDtypeStruct((layers // len(MOVES), rows, width), F32)] * len(MOVES),
         scratch_shapes=[pltpu.VMEM((rows, layers, width), F32)],
         compiler_params=params(12),
         name="solve",
     )(place, theta, modal, ratio, scale, mix_high, mix_low, *parts)
 
 
-def inverse_kernel(source, table_high, table_low, result, high, low, held, sems):
-    shards, lines, width = source.shape
+def gather_pieces(shard, numbers, pieces, table_high, table_low, high, low, rows_high, rows_low):
+    lines, width = pieces[0].shape
     width //= 2
-    for part in range(shards):
-        column = slice(part * width, (part + 1) * width)
+    for slot, (number, piece) in enumerate(zip(numbers, pieces)):
+        column = slice(slot * width, (slot + 1) * width)
         for parity in range(2):
             line = slice(parity * lines, (parity + 1) * lines)
-            high[line, column], low[line, column] = split(source[part, :, parity * width : (parity + 1) * width])
-
-    count, _, step = held.shape
+            high[line, column], low[line, column] = split(piece[:, parity * width : (parity + 1) * width])
+        at = pl.ds(pl.multiple_of(source_shard(shard, MOVES[number]) * width, width), width)
+        rows_high[column, :] = table_high[at, :]
+        rows_low[column, :] = table_low[at, :]
+
+
+def inverse_part_kernel(numbers, shard, table_high, table_low, *refs):
+    pieces, (result, *scratch) = refs[: len(numbers)], refs[len(numbers) :]
+    gather_pieces(shard[0], numbers, pieces, table_high, table_low, *scratch)
+    high, low, rows_high, rows_low = scratch
+    step = 256
+    for start in range(0, result.shape[1], step):
+        span = slice(start, start + step)
+        result[:, span] = three_dots(high[...], low[...], rows_high[:, span], rows_low[:, span])
+
+
+def inverse_rest_kernel(numbers, shard, table_high, table_low, partial, *refs):
+    pieces, (result, high, low, rows_high, rows_low, held, sems) = refs[: len(numbers)], refs[len(numbers) :]
+    gather_pieces(shard[0], numbers, pieces, table_high, table_low, high, low, rows_high, rows_low)
+    count, lines, step = held.shape
     order = LANES - 1 - lax.broadcasted_iota(jnp.int32, (lines, LANES), 1)
     sign = alternating((1, step))
 
     def copy(block):
-        column = pl.ds(block * step, step)
-        return pltpu.make_async_copy(held.at[block], result.at[:, column], sems.at[block])
-
-    def columns(index):
+        return pltpu.make_async_copy(held.at[block], result.at[:, pl.ds(block * step, step)], sems.at[block])
+
+    for index in range(count // 2):
         span = slice(index * step, (index + 1) * step)
-        value = three_dots(high[...], low[...], table_high[:, span], table_low[:, span])
+        value = partial[:, span] + three_dots(high[...], low[...], rows_high[:, span], rows_low[:, span])
         odd, even = value[:lines] * sign, value[lines:]
         held[index] = odd + even
         copy(index).start()
@@ -629,28 +672,51 @@
             block = mirror[:, step - LANES * (part + 1) : step - LANES * part]
             held[count - 1 - index, :, LANES * part : LANES * (part + 1)] = jnp.take_along_axis(block, order, axis=1)
         copy(count - 1 - index).start()
-
-    for index in range(count // 2):
-        columns(index)
     for block in range(count):
         copy(block).wait()
 
 
-def inverse(source, table_high, table_low):
-    shards, lines, width = source.shape
-    depth = shards * width // 2
+def inverse(shard, pieces, table_high, table_low, first):
+    lines, width = pieces[0].shape
+    depth = len(pieces) * width // 2
     step = 256
     count = 2 * depth // step
+
+    def scratch(taken):
+        columns = taken * width // 2
+        return [pltpu.VMEM((2 * lines, columns), BF16)] * 2 + [pltpu.VMEM((columns, depth), BF16)] * 2
+
+    numbers = tuple(range(first))
+    partial = pl.pallas_call(
+        functools.partial(inverse_part_kernel, numbers),
+        in_specs=[smem()] + [vmem()] * (2 + first),
+        out_specs=vmem(),
+        out_shape=jax.ShapeDtypeStruct((2 * lines, depth), F32),
+        scratch_shapes=scratch(first),
+        compiler_params=params(10),
+        cost_estimate=pl.CostEstimate(flops=6 * lines * depth * depth, bytes_accessed=2 << 20, transcendentals=0),
+        name="inverse_part",
+    )(shard, table_high, table_low, *pieces[:first])
+    numbers = tuple(range(first, len(pieces)))
     return pl.pallas_call(
-        inverse_kernel,
-        in_specs=[vmem()] * 3,
+        functools.partial(inverse_rest_kernel, numbers),
+        in_specs=[smem()] + [vmem()] * (3 + len(numbers)),
         out_specs=pl.BlockSpec(memory_space=pltpu.HBM),
         out_shape=jax.ShapeDtypeStruct((lines, 2 * depth), F32),
-        scratch_shapes=[pltpu.VMEM((2 * lines, depth), BF16)] * 2
+        scratch_shapes=scratch(len(numbers))
         + [pltpu.VMEM((count, lines, step), F32), pltpu.SemaphoreType.DMA((count,))],
         compiler_params=params(14),
-        name="inverse",
-    )(source, table_high, table_low)
+        name="inverse_rest",
+    )(shard, table_high, table_low, partial, *pieces[first:])
+
+
+def move_pieces(leaving):
+    shards = len(MOVES)
+    arrived = leaving[:1]
+    for (around, across), piece in zip(MOVES[1:], leaving[1:]):
+        pairs = [(i, ((i // 2 + around) % 4) * 2 + (i % 2 + across) % 2) for i in range(shards)]
+        arrived.append(lax.ppermute(piece, "layer", pairs))
+    return arrived
 
 
 def on_device(q_prev, q_now, psi_now, layers_to_modes, modes_to_layers, stretch):
@@ -669,20 +735,22 @@
     bottom = lax.ppermute(initial, "row", [(j, i) for i, j in pairs])
     theta, ratio, scale, *mixes = prepare(shard, eigen, stretch, layers_to_modes, modes_to_layers)
     q_next, *folded, table_high, table_low = inner_step(q_prev, q_now, psi_now, table_high, table_low)
-    q_next, spectrum = outer_step(place, top, bottom, *folded, table_high, table_low, q_next, shards, blocks)
-    stacked = lax.all_to_all(spectrum, "layer", split_axis=0, concat_axis=0, tiled=True)
-    stacked = stacked.reshape(shards * layer_count, row_count, -1)
-    modal, total = project(stacked, mixes[0], mixes[1], ratio)
+    q_next, *leaving = outer_step(
+        place, shard, top, bottom, *folded, table_high, table_low, q_next, shards, blocks
+    )
+    arrived = move_pieces(leaving)
+    arrived = [piece.reshape(layer_count, row_count, -1) for piece in arrived]
+    modal, total = project(arrived, mixes[0], mixes[1], ratio)
     parts = []
     for level in range(len(RADICES)):
         group = [total] + exchange(total, level, blocks)
         parts.extend(group)
         if level + 1 < len(RADICES):
             total = join_level(level, row_count, place, theta, group)
-    layered = solve(place, theta, modal, ratio, scale, mixes[2], mixes[3], parts, blocks)
-    layered = layered.reshape(shards, layer_count * row_count, -1)
-    returned = lax.all_to_all(layered, "layer", split_axis=0, concat_axis=0, tiled=True)
-    psi_next = inverse(returned, table_high, table_low)
+    leaving = solve(place, theta, modal, ratio, scale, mixes[2], mixes[3], parts, blocks)
+    leaving = [piece.reshape(layer_count * row_count, -1) for piece in leaving]
+    pieces = move_pieces(leaving)
+    psi_next = inverse(shard, pieces, table_high, table_low, 4)
     return (q_next, psi_next.reshape(q_prev.shape))
 
 

time: 121 us -> 118 us (0.975)
  blocking collectives: 28.1 us -> 0 us
  waiting for transfers between devices: 36.9 us -> 51.3 us
  starting transfers between devices: 25.4 us -> 38.3 us
  local copies, waits for them, and re-layouts: 1.35 us -> 0.03 us
    ppermute x0 -> x14, waiting for transfers between devices: none -> 38.1 us  [move_pieces(): arrived.append(lax.ppermute(piece, 'layer', pairs))]
    all_to_all x1 -> x0, blocking collectives: 28.1 us -> none  [on_device(): lax.all_to_all(layered, 'layer', split_axis=0, concat_axis=0, tiled=True)]
    all_to_all x1 -> x0, waiting for transfers between devices: 24.4 us -> none  [on_device(): lax.all_to_all(spectrum, 'layer', split_axis=0, concat_axis=0, tiled=True)]
    ppermute x0 -> x14, starting transfers between devices: none -> 20.2 us  [move_pieces(): arrived.append(lax.ppermute(piece, 'layer', pairs))]
    all_to_all x1 -> x0, starting transfers between devices: 6.08 us -> none  [on_device(): lax.all_to_all(spectrum, 'layer', split_axis=0, concat_axis=0, tiled=True)]
    unnamed x18 -> x8, local copies, waits for them, and re-layouts: 1.35 us -> 0.03 us
    ppermute x7, starting transfers between devices: 16.3 us -> 15.1 us  [exchange(): parts.append(lax.ppermute(total, 'row', pairs))]
    pallas_call x2 -> x3, Pallas kernels: 6.29 us -> 6.67 us  [the longest x1 3.08 us: inverse(): pl.pallas_call(functools.partial(inverse_rest_kernel, numbers), in_specs=...]
  transfers between devices with their start and end apart: 10 -> 23, of which waited for: 7 -> 14; matrix products, arithmetic and copies ran while one was open for 0% -> 0% of each run, Pallas kernels for 8% -> 10%
where the time goes in v4:
time: 118 us
  waiting for transfers between devices  51.3 us (43%)
  starting transfers between devices  38.3 us (32%)
  Pallas kernels  27 us (23%)
    ppermute x14, waiting for transfers between devices, move_pieces(): arrived.append(lax.ppermute(piece, 'layer', pairs))  38.1 us
    ppermute x14, starting transfers between devices, move_pieces(): arrived.append(lax.ppermute(piece, 'layer', pairs))  20.2 us
    ppermute x7, starting transfers between devices, exchange(): parts.append(lax.ppermute(total, 'row', pairs))  15.1 us
    ppermute x7, waiting for transfers between devices, exchange(): parts.append(lax.ppermute(total, 'row', pairs))  13.2 us
    pallas_call x1, Pallas kernels, inner_step(): pl.pallas_call(inner_kernel, grid=(layers,), in_specs=[hbm] * 5, out_spec...  8.23 us
    pallas_call x1, Pallas kernels, outer_step(): pl.pallas_call(functools.partial(outer_kernel, blocks), in_specs=[smem()]...  6.18 us
    pallas_call x1, Pallas kernels, inverse(): pl.pallas_call(functools.partial(inverse_rest_kernel, numbers), in_specs=...  3.08 us
  transfers between devices with their start and end apart: 23, of which 14 were waited for; matrix products, arithmetic and copies ran while one was open for 0% of the time, Pallas kernels for 10%

profile of v4, /device:TPU:32, one launch (start us, length us, event | category | flops | bytes accessed | tf_op | source)
XLA Modules:
  0.0 117.6 jit_solution(16160598579635872786)
XLA Ops:
  0.6 2.1 %rims.1 = (f32[4,4,2048]{2,1,0:T(4,128)}, f32[4,4,2048]{2,1,0:T(4,128)}) custom-call(f32[4,64,2048]{2,1,0:T(8,128)} %prev.1, f32[4,64,2048]{2,1,0:T(8,128)} %now.1, f32[4,64,2048]{2,1,0:T(8,128)} %psi.1, f32[4,64,2048]{2,1,0:T(8,128)} %prev.1, f32[4,64,2048]{2,1,0:T(8,128)} %now.1, f32[4,64,2048]{2,1,0:T(8,128)} %psi.1), custom_call_target="tpu_custom_call" | custom-call | tf_op jit(solution)/shard_map/rims/pallas_call | solution.py:98
  2.7 1.7 %collective-permute-start = (f32[4,4,2048]{2,1,0:T(4,128)}, f32[4,4,2048]{2,1,0:T(4,128)S(1)}, u32[]{:S(2)}, u32[]{:S(2)}) collective-permute-start(f32[4,4,2048]{2,1,0:T(4,128)} %get-tuple-element.37), channel_id=1, source_target_pairs={{0,1},{1,2},{2,3},{3,4},{4,5},{5,6},{6,7},{7,8},{8,9},{9,10},{10,1... | collective-permute-start | bytes 393224 | tf_op jit(solution)/shard_map/ppermute | solution.py:734
  4.5 1.3 %collective-permute-start.1 = (f32[4,4,2048]{2,1,0:T(4,128)}, f32[4,4,2048]{2,1,0:T(4,128)S(1)}, u32[]{:S(2)}, u32[]{:S(2)}) collective-permute-start(f32[4,4,2048]{2,1,0:T(4,128)} %get-tuple-element.38), channel_id=1, source_target_pairs={{1,0},{2,1},{3,2},{4,3},{5,4},{6,5},{7,6},{8,7},{9,8},{10,9},{11,1... | collective-permute-start | bytes 393224 | tf_op jit(solution)/shard_map/ppermute | solution.py:735
  5.8 8.2 %inner_step.1 = (f32[4,64,2048]{2,1,0:T(8,128)}, bf16[384,1024]{1,0:T(8,128)(2,1)S(1)}, bf16[384,1024]{1,0:T(8,128)(2,1)S(1)}, f32[4,16,2048]{2,1,0:T(8,128)S(1)...) custom-call(f32[4,64,2048]{2,1,0:T(8,128)} %prev.1, ...), custom_call_target="tpu_custom_call" | custom-call | flops 31457280 | bytes 12582912 | tf_op jit(solution)/shard_map/inner_step/pallas_call | solution.py:275
  14.0 0.0 collective-permute-done.top
  14.0 0.0 collective-permute-done.1.bottom
  14.0 0.0 copy-start
  14.0 0.0 copy-start.1
  14.1 0.0 copy-start.2
  14.1 0.0 copy-start.3
  14.1 6.2 %outer_step.1 = (f32[4,64,2048]{2,1,0:T(8,128)}, f32[256,256]{1,0:T(8,128)S(1)}, f32[256,256]{1,0:T(8,128)S(1)}, f32[256,256]{1,0:T(8,128)S(1)}, f32[256,256]{1,...) custom-call(s32[1]{0:T(128)} %bitcast.place, ...), custom_call_target="tpu_custom_call", output_to_operand_aliasing={{0}: (10, {})} | custom-call | flops 3221225472 | bytes 4194304 | tf_op jit(solution)/shard_map/outer_step/pallas_call | solution.py:389
  20.3 2.8 %collective-permute-start.2 = (f32[256,256]{1,0:T(8,128)S(1)}, f32[256,256]{1,0:T(8,128)S(1)}, u32[]{:S(2)}, u32[]{:S(2)}) collective-permute-start(f32[256,256]{1,0:T(8,128)S(1)} %get-tuple-element.52), channel_id=1, source_target_pairs={{0,160},{32,128},{64,224},{96,192},{128,32},{160,0},{192,96},{224,... | collective-permute-start | bytes 786440 | tf_op jit(solution)/shard_map/ppermute | solution.py:718
  23.1 1.6 %collective-permute-start.3 = (f32[256,256]{1,0:T(8,128)S(1)}, f32[256,256]{1,0:T(8,128)S(1)}, u32[]{:S(2)}, u32[]{:S(2)}) collective-permute-start(f32[256,256]{1,0:T(8,128)S(1)} %get-tuple-element.53), channel_id=1, source_target_pairs={{0,128},{32,160},{64,192},{96,224},{128,0},{160,32},{192,64},{224,... | collective-permute-start | bytes 786440 | tf_op jit(solution)/shard_map/ppermute | solution.py:718
  24.7 1.6 %collective-permute-start.4 = (f32[256,256]{1,0:T(8,128)S(1)}, f32[256,256]{1,0:T(8,128)S(1)}, u32[]{:S(2)}, u32[]{:S(2)}) collective-permute-start(f32[256,256]{1,0:T(8,128)S(1)} %get-tuple-element.54), channel_id=1, source_target_pairs={{0,96},{32,64},{64,160},{96,128},{128,224},{160,192},{192,32},{224... | collective-permute-start | bytes 786440 | tf_op jit(solution)/shard_map/ppermute | solution.py:718
  26.4 2.5 %collective-permute-start.5 = (f32[256,256]{1,0:T(8,128)S(1)}, f32[256,256]{1,0:T(8,128)S(1)}, u32[]{:S(2)}, u32[]{:S(2)}) collective-permute-start(f32[256,256]{1,0:T(8,128)S(1)} %get-tuple-element.55), channel_id=1, source_target_pairs={{0,224},{32,192},{64,32},{96,0},{128,96},{160,64},{192,160},{224,1... | collective-permute-start | bytes 786440 | tf_op jit(solution)/shard_map/ppermute | solution.py:718
  28.8 0.0 collective-permute-start.6
  28.8 1.7 %collective-permute-done.2 = f32[256,256]{1,0:T(8,128)S(1)} collective-permute-done((f32[256,256]{1,0:T(8,128)S(1)}, f32[256,256]{1,0:T(8,128)S(1)}, u32[]{:S(2)}, u32[]{:S(2)}) %collective-permute-start.2) | collective-permute-done | bytes 262176 | tf_op jit(solution)/shard_map/ppermute | solution.py:718
  30.6 3.0 %collective-permute-start.7 = (f32[256,256]{1,0:T(8,128)S(1)}, f32[256,256]{1,0:T(8,128)S(1)}, u32[]{:S(2)}, u32[]{:S(2)}) collective-permute-start(f32[256,256]{1,0:T(8,128)S(1)} %get-tuple-element.57), channel_id=1, source_target_pairs={{0,192},{32,224},{64,0},{96,32},{128,64},{160,96},{192,128},{224,1... | collective-permute-start | bytes 786440 | tf_op jit(solution)/shard_map/ppermute | solution.py:718
  33.6 10.2 %collective-permute-done.3 = f32[256,256]{1,0:T(8,128)S(1)} collective-permute-done((f32[256,256]{1,0:T(8,128)S(1)}, f32[256,256]{1,0:T(8,128)S(1)}, u32[]{:S(2)}, u32[]{:S(2)}) %collective-permute-start.3) | collective-permute-done | bytes 262176 | tf_op jit(solution)/shard_map/ppermute | solution.py:718
  43.8 1.4 %collective-permute-start.8 = (f32[256,256]{1,0:T(8,128)S(1)}, f32[256,256]{1,0:T(8,128)S(1)}, u32[]{:S(2)}, u32[]{:S(2)}) collective-permute-start(f32[256,256]{1,0:T(8,128)S(1)} %get-tuple-element.58), channel_id=1, source_target_pairs={{0,32},{32,0},{64,96},{96,64},{128,160},{160,128},{192,224},{224,1... | collective-permute-start | bytes 786440 | tf_op jit(solution)/shard_map/ppermute | solution.py:718
  45.2 0.0 copy-done
  45.2 0.0 copy-done.1
  45.2 0.0 copy-done.2
  45.2 0.0 copy-done.3
  45.2 1.6 %prepare.1 = (f32[32,256]{1,0:T(8,128)S(1)}, f32[32,256]{1,0:T(8,128)S(1)}, f32[32,256]{1,0:T(8,128)S(1)}, bf16[256,256]{1,0:T(8,128)(2,1)S(1)}, bf16[256,256]{1...) custom-call(s32[1]{0:T(128)} %bitcast.1.shard, f32[8,256]{1,0:T(8,128)S(1)} %copy-done.2, ...), custom_call_target="tpu_custom_call" | custom-call | tf_op jit(solution)/shard_map/prepare/pallas_call | solution.py:460
  46.8 0.0 collective-permute-done.4
  46.9 0.0 collective-permute-done.5
  46.9 2.2 %collective-permute-done.6 = f32[256,256]{1,0:T(8,128)S(1)} collective-permute-done((f32[256,256]{1,0:T(8,128)S(1)}, f32[256,256]{1,0:T(8,128)S(1)}, u32[]{:S(2)}, u32[]{:S(2)}) %collective-permute-start.6) | collective-permute-done | bytes 262176 | tf_op jit(solution)/shard_map/ppermute | solution.py:718
  49.1 0.0 collective-permute-done.7
  49.1 2.9 %collective-permute-done.8 = f32[256,256]{1,0:T(8,128)S(1)} collective-permute-done((f32[256,256]{1,0:T(8,128)S(1)}, f32[256,256]{1,0:T(8,128)S(1)}, u32[]{:S(2)}, u32[]{:S(2)}) %collective-permute-start.8) | collective-permute-done | bytes 262176 | tf_op jit(solution)/shard_map/ppermute | solution.py:718
  52.1 1.7 %project.1 = (f32[64,32,256]{2,1,0:T(8,128)S(1)}, f32[2,32,256]{2,1,0:T(8,128)S(1)}) custom-call(bf16[256,256]{1,0:T(8,128)(2,1)S(1)} %get-tuple-element.48.mix_high, bf16[256,256]{1,0:T(8,128)(2,1)S(1)} %get-tuple-element.49.mix_low, f32[32,256]{1,0:T(8,128)S(1)} %get-tuple-element.50.ratio, f32[4,64,256]{2,1,0:T(8,128)S(1)} %bitcast.19, ...), custom_call_target="tpu_custom_call" | custom-call | tf_op jit(solution)/shard_map/project/pallas_call | solution.py:499
  53.8 0.1 collective-permute-start.9
  53.9 1.2 %collective-permute-done.9.refs_1_ = f32[2,32,256]{2,1,0:T(8,128)S(1)} collective-permute-done((f32[2,32,256]{2,1,0:T(8,128)S(1)}, f32[2,32,256]{2,1,0:T(8,128)S(1)}, u32[]{:S(2)}, u32[]{:S(2)}) %collective-permute-start.9) | collective-permute-done | bytes 65568 | tf_op jit(solution)/shard_map/ppermute | solution.py:523
  55.2 5.6 %collective-permute-start.10 = (f32[2,32,256]{2,1,0:T(8,128)S(1)}, f32[2,32,256]{2,1,0:T(8,128)S(1)}, u32[]{:S(2)}, u32[]{:S(2)}) collective-permute-start(f32[2,32,256]{2,1,0:T(8,128)S(1)} %join.2.refs_0_.refs_2_), channel_id=1, source_target_pairs={{2,0},{3,1},{4,2},{5,3},{6,4},{7,5},{0,6},{1,7},{10,8},{11,9},{12,... | collective-permute-start | bytes 196616 | tf_op jit(solution)/shard_map/ppermute | solution.py:523
  60.8 0.0 collective-permute-start.11
  60.8 1.0 collective-permute-start.12
  61.8 2.2 %collective-permute-done.10.refs_1_.refs_3_ = f32[2,32,256]{2,1,0:T(8,128)S(1)} collective-permute-done((f32[2,32,256]{2,1,0:T(8,128)S(1)}, f32[2,32,256]{2,1,0:T(8,128)S(1)}, u32[]{:S(2)}, u32[]{:S(2)}) %collective-permute-start.10) | collective-permute-done | bytes 65568 | tf_op jit(solution)/shard_map/ppermute | solution.py:523
  63.9 3.0 %collective-permute-done.11.refs_2_.refs_4_ = f32[2,32,256]{2,1,0:T(8,128)S(1)} collective-permute-done((f32[2,32,256]{2,1,0:T(8,128)S(1)}, f32[2,32,256]{2,1,0:T(8,128)S(1)}, u32[]{:S(2)}, u32[]{:S(2)}) %collective-permute-start.11) | collective-permute-done | bytes 65568 | tf_op jit(solution)/shard_map/ppermute | solution.py:523
  66.9 0.4 collective-permute-done.12.refs_3_.refs_5_
  67.3 0.1 join.3.refs_6_
  67.3 4.1 %collective-permute-start.13 = (f32[2,32,256]{2,1,0:T(8,128)S(1)}, f32[2,32,256]{2,1,0:T(8,128)S(1)}, u32[]{:S(2)}, u32[]{:S(2)}) collective-permute-start(f32[2,32,256]{2,1,0:T(8,128)S(1)} %join.3.refs_6_), channel_id=1, source_target_pairs={{8,0},{9,1},{10,2},{11,3},{12,4},{13,5},{14,6},{15,7},{16,8},{17,9... | collective-permute-start | bytes 196616 | tf_op jit(solution)/shard_map/ppermute | solution.py:523
  71.4 2.8 %collective-permute-start.14 = (f32[2,32,256]{2,1,0:T(8,128)S(1)}, f32[2,32,256]{2,1,0:T(8,128)S(1)}, u32[]{:S(2)}, u32[]{:S(2)}) collective-permute-start(f32[2,32,256]{2,1,0:T(8,128)S(1)} %join.3.refs_6_), channel_id=1, source_target_pairs={{16,0},{17,1},{18,2},{19,3},{20,4},{21,5},{22,6},{23,7},{24,8},{25... | collective-permute-start | bytes 196616 | tf_op jit(solution)/shard_map/ppermute | solution.py:523
  74.3 1.5 %collective-permute-start.15 = (f32[2,32,256]{2,1,0:T(8,128)S(1)}, f32[2,32,256]{2,1,0:T(8,128)S(1)}, u32[]{:S(2)}, u32[]{:S(2)}) collective-permute-start(f32[2,32,256]{2,1,0:T(8,128)S(1)} %join.3.refs_6_), channel_id=1, source_target_pairs={{24,0},{25,1},{26,2},{27,3},{28,4},{29,5},{30,6},{31,7},{0,8},{1,9... | collective-permute-start | bytes 196616 | tf_op jit(solution)/shard_map/ppermute | solution.py:523
  75.8 0.0 collective-permute-done.13.refs_7_
  75.8 4.6 %collective-permute-done.14.refs_8_ = f32[2,32,256]{2,1,0:T(8,128)S(1)} collective-permute-done((f32[2,32,256]{2,1,0:T(8,128)S(1)}, f32[2,32,256]{2,1,0:T(8,128)S(1)}, u32[]{:S(2)}, u32[]{:S(2)}) %collective-permute-start.14) | collective-permute-done | bytes 65568 | tf_op jit(solution)/shard_map/ppermute | solution.py:523
  80.4 1.8 %collective-permute-done.15.refs_9_ = f32[2,32,256]{2,1,0:T(8,128)S(1)} collective-permute-done((f32[2,32,256]{2,1,0:T(8,128)S(1)}, f32[2,32,256]{2,1,0:T(8,128)S(1)}, u32[]{:S(2)}, u32[]{:S(2)}) %collective-permute-start.15) | collective-permute-done | bytes 65568 | tf_op jit(solution)/shard_map/ppermute | solution.py:523
  82.2 2.1 %solve.1 = (f32[4,64,256]{2,1,0:T(8,128)S(1)}, f32[4,64,256]{2,1,0:T(8,128)S(1)}, f32[4,64,256]{2,1,0:T(8,128)S(1)}, f32[4,64,256]{2,1,0:T(8,128)S(1)}, f32[4,64...) custom-call(s32[1]{0:T(128)} %bitcast.place, ...), custom_call_target="tpu_custom_call" | custom-call | tf_op jit(solution)/shard_map/solve/pallas_call | solution.py:620
  84.3 1.1 collective-permute-start.16
  85.4 1.9 %collective-permute-start.17 = (f32[256,256]{1,0:T(8,128)S(1)}, f32[256,256]{1,0:T(8,128)S(1)}, u32[]{:S(2)}, u32[]{:S(2)}) collective-permute-start(f32[256,256]{1,0:T(8,128)S(1)} %bitcast.33), channel_id=1, source_target_pairs={{0,128},{32,160},{64,192},{96,224},{128,0},{160,32},{192,64},{224,... | collective-permute-start | bytes 786440 | tf_op jit(solution)/shard_map/ppermute | solution.py:718
  87.3 1.1 collective-permute-start.18
  88.4 3.0 %collective-permute-start.19 = (f32[256,256]{1,0:T(8,128)S(1)}, f32[256,256]{1,0:T(8,128)S(1)}, u32[]{:S(2)}, u32[]{:S(2)}) collective-permute-start(f32[256,256]{1,0:T(8,128)S(1)} %bitcast.31), channel_id=1, source_target_pairs={{0,224},{32,192},{64,32},{96,0},{128,96},{160,64},{192,160},{224,1... | collective-permute-start | bytes 786440 | tf_op jit(solution)/shard_map/ppermute | solution.py:718
  91.5 0.0 collective-permute-start.20
  91.5 7.2 %collective-permute-done.16.refs_1_ = f32[256,256]{1,0:T(8,128)S(1)} collective-permute-done((f32[256,256]{1,0:T(8,128)S(1)}, f32[256,256]{1,0:T(8,128)S(1)}, u32[]{:S(2)}, u32[]{:S(2)}) %collective-permute-start.16) | collective-permute-done | bytes 262176 | tf_op jit(solution)/shard_map/ppermute | solution.py:718
  98.6 0.0 collective-permute-start.21
  98.6 9.3 %collective-permute-done.17.refs_2_ = f32[256,256]{1,0:T(8,128)S(1)} collective-permute-done((f32[256,256]{1,0:T(8,128)S(1)}, f32[256,256]{1,0:T(8,128)S(1)}, u32[]{:S(2)}, u32[]{:S(2)}) %collective-permute-start.17) | collective-permute-done | bytes 262176 | tf_op jit(solution)/shard_map/ppermute | solution.py:718
  107.9 0.0 collective-permute-start.22
  107.9 0.0 collective-permute-done.18.refs_3_
  107.9 1.9 %inverse_part.1.partial = f32[512,1024]{1,0:T(8,128)S(1)} custom-call(s32[1]{0:T(128)} %bitcast.1.shard, bf16[1024,1024]{1,0:T(8,128)(2,1)S(1)} %get-tuple-element.43.table_high, bf16[1024,1024]{1,0:T(8,128)(2,1)S(1)} %get-tuple-element.44.table_low, f32[256,256]{1,0:T(8,128)S(1)} %bitcast.27, f32[256,256]{1,0:T(8,128)S(1)} %collective-permute-done.16.refs_1_, ...), custom_call_target="tpu_custom_call" | custom-call | flops 1610612736 | bytes 2097152 | tf_op jit(solution)/shard_map/inverse_part/pallas_call | solution.py:690
  109.8 0.0 collective-permute-done.19.refs_0_
  109.8 1.3 %collective-permute-done.20.refs_1_ = f32[256,256]{1,0:T(8,128)S(1)} collective-permute-done((f32[256,256]{1,0:T(8,128)S(1)}, f32[256,256]{1,0:T(8,128)S(1)}, u32[]{:S(2)}, u32[]{:S(2)}) %collective-permute-start.20) | collective-permute-done | bytes 262176 | tf_op jit(solution)/shard_map/ppermute | solution.py:718
  111.1 0.0 collective-permute-done.21.refs_2_
  111.1 3.2 %collective-permute-done.22.refs_3_ = f32[256,256]{1,0:T(8,128)S(1)} collective-permute-done((f32[256,256]{1,0:T(8,128)S(1)}, f32[256,256]{1,0:T(8,128)S(1)}, u32[]{:S(2)}, u32[]{:S(2)}) %collective-permute-start.22) | collective-permute-done | bytes 262176 | tf_op jit(solution)/shard_map/ppermute | solution.py:718
  114.3 3.1 %inverse_rest.1 = f32[256,2048]{1,0:T(8,128)} custom-call(s32[1]{0:T(128)} %bitcast.1.shard, bf16[1024,1024]{1,0:T(8,128)(2,1)S(1)} %get-tuple-element.43.table_high, bf16[1024,1024]{1,0:T(8,128)(2,1)S(1)} %get-tuple-element.44.table_low, f32[512,1024]{1,0:T(8,128)S(1)} %inverse_part.1.partial, f32[256,256]{1,0:T(8,128)S(1)} %collective-permute-done.19.refs_0_, ...), custom_call_target="tpu_custom_call" | custom-call | tf_op jit(solution)/shard_map/inverse_rest/pallas_call | solution.py:701
  (1 shorter events, 0.0 us)
Async XLA Ops:
  2.7 11.3 %collective-permute-start = (f32[4,4,2048]{2,1,0:T(4,128)}, f32[4,4,2048]{2,1,0:T(4,128)S(1)}, u32[]{:S(2)}, u32[]{:S(2)}) collective-permute-start(f32[4,4,2048]{2,1,0:T(4,128)} %get-tuple-element.37), channel_id=1, source_target_pairs={{0,1},{1,2},{2,3},{3,4},{4,5},{5,6},{6,7},{7,8},{8,9},{9,10},{10,1... | collective-permute-start | bytes 393224 | tf_op jit(solution)/shard_map/ppermute | solution.py:734
  4.5 9.6 %collective-permute-start.1 = (f32[4,4,2048]{2,1,0:T(4,128)}, f32[4,4,2048]{2,1,0:T(4,128)S(1)}, u32[]{:S(2)}, u32[]{:S(2)}) collective-permute-start(f32[4,4,2048]{2,1,0:T(4,128)} %get-tuple-element.38), channel_id=1, source_target_pairs={{1,0},{2,1},{3,2},{4,3},{5,4},{6,5},{7,6},{8,7},{9,8},{10,9},{11,1... | collective-permute-start | bytes 393224 | tf_op jit(solution)/shard_map/ppermute | solution.py:735
  14.0 31.2 %copy-start = (f32[32,32]{1,0:T(8,128)S(1)}, f32[32,32]{1,0:T(8,128)}, u32[]{:S(2)}) copy-start(f32[32,32]{1,0:T(8,128)} %to_modes.1) | copy-start | bytes 12292
  14.0 31.2 %copy-start.1 = (f32[32,32]{1,0:T(8,128)S(1)}, f32[32,32]{1,0:T(8,128)}, u32[]{:S(2)}) copy-start(f32[32,32]{1,0:T(8,128)} %to_layers.1) | copy-start | bytes 12292
  14.1 31.1 %copy-start.2 = (f32[8,256]{1,0:T(8,128)S(1)}, f32[8,256]{1,0:T(8,128)}, u32[]{:S(2)}) copy-start(f32[8,256]{1,0:T(8,128)} %constant.17.clone.eigen) | copy-start | bytes 24580
  14.1 31.1 %copy-start.3 = (f32[32]{0:T(128)S(1)}, f32[32]{0:T(128)}, u32[]{:S(2)}) copy-start(f32[32]{0:T(128)} %stretch.1) | copy-start | bytes 388
  20.3 10.3 %collective-permute-start.2 = (f32[256,256]{1,0:T(8,128)S(1)}, f32[256,256]{1,0:T(8,128)S(1)}, u32[]{:S(2)}, u32[]{:S(2)}) collective-permute-start(f32[256,256]{1,0:T(8,128)S(1)} %get-tuple-element.52), channel_id=1, source_target_pairs={{0,160},{32,128},{64,224},{96,192},{128,32},{160,0},{192,96},{224,... | collective-permute-start | bytes 786440 | tf_op jit(solution)/shard_map/ppermute | solution.py:718
  23.1 20.7 %collective-permute-start.3 = (f32[256,256]{1,0:T(8,128)S(1)}, f32[256,256]{1,0:T(8,128)S(1)}, u32[]{:S(2)}, u32[]{:S(2)}) collective-permute-start(f32[256,256]{1,0:T(8,128)S(1)} %get-tuple-element.53), channel_id=1, source_target_pairs={{0,128},{32,160},{64,192},{96,224},{128,0},{160,32},{192,64},{224,... | collective-permute-start | bytes 786440 | tf_op jit(solution)/shard_map/ppermute | solution.py:718
  24.7 22.1 %collective-permute-start.4 = (f32[256,256]{1,0:T(8,128)S(1)}, f32[256,256]{1,0:T(8,128)S(1)}, u32[]{:S(2)}, u32[]{:S(2)}) collective-permute-start(f32[256,256]{1,0:T(8,128)S(1)} %get-tuple-element.54), channel_id=1, source_target_pairs={{0,96},{32,64},{64,160},{96,128},{128,224},{160,192},{192,32},{224... | collective-permute-start | bytes 786440 | tf_op jit(solution)/shard_map/ppermute | solution.py:718
  26.4 20.5 %collective-permute-start.5 = (f32[256,256]{1,0:T(8,128)S(1)}, f32[256,256]{1,0:T(8,128)S(1)}, u32[]{:S(2)}, u32[]{:S(2)}) collective-permute-start(f32[256,256]{1,0:T(8,128)S(1)} %get-tuple-element.55), channel_id=1, source_target_pairs={{0,224},{32,192},{64,32},{96,0},{128,96},{160,64},{192,160},{224,1... | collective-permute-start | bytes 786440 | tf_op jit(solution)/shard_map/ppermute | solution.py:718
  28.8 20.3 %collective-permute-start.6 = (f32[256,256]{1,0:T(8,128)S(1)}, f32[256,256]{1,0:T(8,128)S(1)}, u32[]{:S(2)}, u32[]{:S(2)}) collective-permute-start(f32[256,256]{1,0:T(8,128)S(1)} %get-tuple-element.56), channel_id=1, source_target_pairs={{0,64},{32,96},{64,128},{96,160},{128,192},{160,224},{192,0},{224,... | collective-permute-start | bytes 786440 | tf_op jit(solution)/shard_map/ppermute | solution.py:718
  30.6 18.6 %collective-permute-start.7 = (f32[256,256]{1,0:T(8,128)S(1)}, f32[256,256]{1,0:T(8,128)S(1)}, u32[]{:S(2)}, u32[]{:S(2)}) collective-permute-start(f32[256,256]{1,0:T(8,128)S(1)} %get-tuple-element.57), channel_id=1, source_target_pairs={{0,192},{32,224},{64,0},{96,32},{128,64},{160,96},{192,128},{224,1... | collective-permute-start | bytes 786440 | tf_op jit(solution)/shard_map/ppermute | solution.py:718
  43.8 8.3 %collective-permute-start.8 = (f32[256,256]{1,0:T(8,128)S(1)}, f32[256,256]{1,0:T(8,128)S(1)}, u32[]{:S(2)}, u32[]{:S(2)}) collective-permute-start(f32[256,256]{1,0:T(8,128)S(1)} %get-tuple-element.58), channel_id=1, source_target_pairs={{0,32},{32,0},{64,96},{96,64},{128,160},{160,128},{192,224},{224,1... | collective-permute-start | bytes 786440 | tf_op jit(solution)/shard_map/ppermute | solution.py:718
  53.8 1.3 %collective-permute-start.9 = (f32[2,32,256]{2,1,0:T(8,128)S(1)}, f32[2,32,256]{2,1,0:T(8,128)S(1)}, u32[]{:S(2)}, u32[]{:S(2)}) collective-permute-start(f32[2,32,256]{2,1,0:T(8,128)S(1)} %get-tuple-element.63.refs_0_), channel_id=1, source_target_pairs={{1,0},{0,1},{3,2},{2,3},{5,4},{4,5},{7,6},{6,7},{9,8},{8,9},{11,10... | collective-permute-start | bytes 196616 | tf_op jit(solution)/shard_map/ppermute | solution.py:523
  55.2 8.7 %collective-permute-start.10 = (f32[2,32,256]{2,1,0:T(8,128)S(1)}, f32[2,32,256]{2,1,0:T(8,128)S(1)}, u32[]{:S(2)}, u32[]{:S(2)}) collective-permute-start(f32[2,32,256]{2,1,0:T(8,128)S(1)} %join.2.refs_0_.refs_2_), channel_id=1, source_target_pairs={{2,0},{3,1},{4,2},{5,3},{6,4},{7,5},{0,6},{1,7},{10,8},{11,9},{12,... | collective-permute-start | bytes 196616 | tf_op jit(solution)/shard_map/ppermute | solution.py:523
  60.8 6.1 %collective-permute-start.11 = (f32[2,32,256]{2,1,0:T(8,128)S(1)}, f32[2,32,256]{2,1,0:T(8,128)S(1)}, u32[]{:S(2)}, u32[]{:S(2)}) collective-permute-start(f32[2,32,256]{2,1,0:T(8,128)S(1)} %join.2.refs_0_.refs_2_), channel_id=1, source_target_pairs={{4,0},{5,1},{6,2},{7,3},{0,4},{1,5},{2,6},{3,7},{12,8},{13,9},{14,... | collective-permute-start | bytes 196616 | tf_op jit(solution)/shard_map/ppermute | solution.py:523
  60.8 6.5 %collective-permute-start.12 = (f32[2,32,256]{2,1,0:T(8,128)S(1)}, f32[2,32,256]{2,1,0:T(8,128)S(1)}, u32[]{:S(2)}, u32[]{:S(2)}) collective-permute-start(f32[2,32,256]{2,1,0:T(8,128)S(1)} %join.2.refs_0_.refs_2_), channel_id=1, source_target_pairs={{6,0},{7,1},{0,2},{1,3},{2,4},{3,5},{4,6},{5,7},{14,8},{15,9},{8,1... | collective-permute-start | bytes 196616 | tf_op jit(solution)/shard_map/ppermute | solution.py:523
  67.3 8.4 %collective-permute-start.13 = (f32[2,32,256]{2,1,0:T(8,128)S(1)}, f32[2,32,256]{2,1,0:T(8,128)S(1)}, u32[]{:S(2)}, u32[]{:S(2)}) collective-permute-start(f32[2,32,256]{2,1,0:T(8,128)S(1)} %join.3.refs_6_), channel_id=1, source_target_pairs={{8,0},{9,1},{10,2},{11,3},{12,4},{13,5},{14,6},{15,7},{16,8},{17,9... | collective-permute-start | bytes 196616 | tf_op jit(solution)/shard_map/ppermute | solution.py:523
  71.4 8.9 %collective-permute-start.14 = (f32[2,32,256]{2,1,0:T(8,128)S(1)}, f32[2,32,256]{2,1,0:T(8,128)S(1)}, u32[]{:S(2)}, u32[]{:S(2)}) collective-permute-start(f32[2,32,256]{2,1,0:T(8,128)S(1)} %join.3.refs_6_), channel_id=1, source_target_pairs={{16,0},{17,1},{18,2},{19,3},{20,4},{21,5},{22,6},{23,7},{24,8},{25... | collective-permute-start | bytes 196616 | tf_op jit(solution)/shard_map/ppermute | solution.py:523
  74.3 7.9 %collective-permute-start.15 = (f32[2,32,256]{2,1,0:T(8,128)S(1)}, f32[2,32,256]{2,1,0:T(8,128)S(1)}, u32[]{:S(2)}, u32[]{:S(2)}) collective-permute-start(f32[2,32,256]{2,1,0:T(8,128)S(1)} %join.3.refs_6_), channel_id=1, source_target_pairs={{24,0},{25,1},{26,2},{27,3},{28,4},{29,5},{30,6},{31,7},{0,8},{1,9... | collective-permute-start | bytes 196616 | tf_op jit(solution)/shard_map/ppermute | solution.py:523
  84.3 14.3 %collective-permute-start.16 = (f32[256,256]{1,0:T(8,128)S(1)}, f32[256,256]{1,0:T(8,128)S(1)}, u32[]{:S(2)}, u32[]{:S(2)}) collective-permute-start(f32[256,256]{1,0:T(8,128)S(1)} %bitcast.34), channel_id=1, source_target_pairs={{0,160},{32,128},{64,224},{96,192},{128,32},{160,0},{192,96},{224,... | collective-permute-start | bytes 786440 | tf_op jit(solution)/shard_map/ppermute | solution.py:718
  85.4 22.5 %collective-permute-start.17 = (f32[256,256]{1,0:T(8,128)S(1)}, f32[256,256]{1,0:T(8,128)S(1)}, u32[]{:S(2)}, u32[]{:S(2)}) collective-permute-start(f32[256,256]{1,0:T(8,128)S(1)} %bitcast.33), channel_id=1, source_target_pairs={{0,128},{32,160},{64,192},{96,224},{128,0},{160,32},{192,64},{224,... | collective-permute-start | bytes 786440 | tf_op jit(solution)/shard_map/ppermute | solution.py:718
  87.3 20.6 %collective-permute-start.18 = (f32[256,256]{1,0:T(8,128)S(1)}, f32[256,256]{1,0:T(8,128)S(1)}, u32[]{:S(2)}, u32[]{:S(2)}) collective-permute-start(f32[256,256]{1,0:T(8,128)S(1)} %bitcast.32), channel_id=1, source_target_pairs={{0,96},{32,64},{64,160},{96,128},{128,224},{160,192},{192,32},{224... | collective-permute-start | bytes 786440 | tf_op jit(solution)/shard_map/ppermute | solution.py:718
  88.4 21.4 %collective-permute-start.19 = (f32[256,256]{1,0:T(8,128)S(1)}, f32[256,256]{1,0:T(8,128)S(1)}, u32[]{:S(2)}, u32[]{:S(2)}) collective-permute-start(f32[256,256]{1,0:T(8,128)S(1)} %bitcast.31), channel_id=1, source_target_pairs={{0,224},{32,192},{64,32},{96,0},{128,96},{160,64},{192,160},{224,1... | collective-permute-start | bytes 786440 | tf_op jit(solution)/shard_map/ppermute | solution.py:718
  91.5 19.6 %collective-permute-start.20 = (f32[256,256]{1,0:T(8,128)S(1)}, f32[256,256]{1,0:T(8,128)S(1)}, u32[]{:S(2)}, u32[]{:S(2)}) collective-permute-start(f32[256,256]{1,0:T(8,128)S(1)} %bitcast.30), channel_id=1, source_target_pairs={{0,64},{32,96},{64,128},{96,160},{128,192},{160,224},{192,0},{224,... | collective-permute-start | bytes 786440 | tf_op jit(solution)/shard_map/ppermute | solution.py:718
  98.6 12.5 %collective-permute-start.21 = (f32[256,256]{1,0:T(8,128)S(1)}, f32[256,256]{1,0:T(8,128)S(1)}, u32[]{:S(2)}, u32[]{:S(2)}) collective-permute-start(f32[256,256]{1,0:T(8,128)S(1)} %bitcast.29), channel_id=1, source_target_pairs={{0,192},{32,224},{64,0},{96,32},{128,64},{160,96},{192,128},{224,1... | collective-permute-start | bytes 786440 | tf_op jit(solution)/shard_map/ppermute | solution.py:718
  107.9 6.4 %collective-permute-start.22 = (f32[256,256]{1,0:T(8,128)S(1)}, f32[256,256]{1,0:T(8,128)S(1)}, u32[]{:S(2)}, u32[]{:S(2)}) collective-permute-start(f32[256,256]{1,0:T(8,128)S(1)} %bitcast.28), channel_id=1, source_target_pairs={{0,32},{32,0},{64,96},{96,64},{128,160},{160,128},{192,224},{224,1... | collective-permute-start | bytes 786440 | tf_op jit(solution)/shard_map/ppermute | solution.py:718

commit v5 on v4

--- a/solution.py
+++ b/solution.py
@@ -68,7 +68,7 @@
     return pl.BlockSpec(memory_space=pltpu.SMEM)
 
 
-MOVES = ((0, 0), (2, 1), (2, 0), (1, 1), (3, 1), (1, 0), (3, 0), (0, 1))
+MOVES = ((0, 0), (2, 1), (0, 1), (2, 0), (1, 1), (3, 1), (1, 0), (3, 0))
 
 
 def target_shard(shard, move):
@@ -514,14 +514,14 @@
 
 def exchange(total, level, blocks):
     radix, group = RADICES[level], math.prod(RADICES[:level])
-    parts = []
-    for shift in range(1, radix):
+    parts = {}
+    for shift in sorted(range(1, radix), key=lambda shift: min(shift, radix - shift)):
         pairs = []
         for target in range(blocks):
             spot = (target // group) % radix
             pairs.append((target + ((spot + shift) % radix - spot) * group, target))
-        parts.append(lax.ppermute(total, "row", pairs))
-    return parts
+        parts[shift] = lax.ppermute(total, "row", pairs)
+    return [parts[shift] for shift in range(1, radix)]
 
 
 def decayed(unit, count):

time: 118 us -> 113 us (0.958)
  waiting for transfers between devices: 51.3 us -> 39.2 us
  starting transfers between devices: 38.3 us -> 44.6 us
    ppermute x14, waiting for transfers between devices: 38.1 us -> 27.1 us  [move_pieces(): arrived.append(lax.ppermute(piece, 'layer', pairs))]
    ppermute x14, starting transfers between devices: 20.2 us -> 23.8 us  [move_pieces(): arrived.append(lax.ppermute(piece, 'layer', pairs))]
    ppermute x7, starting transfers between devices: 15.1 us -> 17.8 us  [exchange(): parts[shift] = lax.ppermute(total, 'row', pairs)]
  transfers between devices with their start and end apart: 23 -> 23, of which waited for: 14 -> 17; matrix products, arithmetic and copies ran while one was open for 0% -> 0% of each run, Pallas kernels for 10% -> 10%
where the time goes in v5:
time: 113 us; the launch traced here: 112 us
  starting transfers between devices  44.6 us (39%)
  waiting for transfers between devices  39.2 us (35%)
  Pallas kernels  27.1 us (24%)
    ppermute x14, waiting for transfers between devices, move_pieces(): arrived.append(lax.ppermute(piece, 'layer', pairs))  27.1 us
    ppermute x14, starting transfers between devices, move_pieces(): arrived.append(lax.ppermute(piece, 'layer', pairs))  23.8 us
    ppermute x7, starting transfers between devices, exchange(): parts[shift] = lax.ppermute(total, 'row', pairs)  17.8 us
    ppermute x7, waiting for transfers between devices, exchange(): parts[shift] = lax.ppermute(total, 'row', pairs)  12.1 us
    pallas_call x1, Pallas kernels, inner_step(): pl.pallas_call(inner_kernel, grid=(layers,), in_specs=[hbm] * 5, out_spec...  8.23 us
    pallas_call x1, Pallas kernels, outer_step(): pl.pallas_call(functools.partial(outer_kernel, blocks), in_specs=[smem()]...  6.18 us
    pallas_call x1, Pallas kernels, inverse(): pl.pallas_call(functools.partial(inverse_rest_kernel, numbers), in_specs=...  3.08 us
  transfers between devices with their start and end apart: 23, of which 17 were waited for; matrix products, arithmetic and copies ran while one was open for 0% of the time, Pallas kernels for 10%

profile of v5, /device:TPU:32, one launch (start us, length us, event | category | flops | bytes accessed | tf_op | source)
XLA Modules:
  0.0 111.8 jit_solution(1473662604252139662)
XLA Ops:
  0.6 2.1 %rims.1 = (f32[4,4,2048]{2,1,0:T(4,128)}, f32[4,4,2048]{2,1,0:T(4,128)}) custom-call(f32[4,64,2048]{2,1,0:T(8,128)} %prev.1, f32[4,64,2048]{2,1,0:T(8,128)} %now.1, f32[4,64,2048]{2,1,0:T(8,128)} %psi.1, f32[4,64,2048]{2,1,0:T(8,128)} %prev.1, f32[4,64,2048]{2,1,0:T(8,128)} %now.1, f32[4,64,2048]{2,1,0:T(8,128)} %psi.1), custom_call_target="tpu_custom_call" | custom-call | tf_op jit(solution)/shard_map/rims/pallas_call | solution.py:98
  2.7 1.7 %collective-permute-start = (f32[4,4,2048]{2,1,0:T(4,128)}, f32[4,4,2048]{2,1,0:T(4,128)S(1)}, u32[]{:S(2)}, u32[]{:S(2)}) collective-permute-start(f32[4,4,2048]{2,1,0:T(4,128)} %get-tuple-element.37), channel_id=1, source_target_pairs={{0,1},{1,2},{2,3},{3,4},{4,5},{5,6},{6,7},{7,8},{8,9},{9,10},{10,1... | collective-permute-start | bytes 393224 | tf_op jit(solution)/shard_map/ppermute | solution.py:734
  4.5 1.3 %collective-permute-start.1 = (f32[4,4,2048]{2,1,0:T(4,128)}, f32[4,4,2048]{2,1,0:T(4,128)S(1)}, u32[]{:S(2)}, u32[]{:S(2)}) collective-permute-start(f32[4,4,2048]{2,1,0:T(4,128)} %get-tuple-element.38), channel_id=1, source_target_pairs={{1,0},{2,1},{3,2},{4,3},{5,4},{6,5},{7,6},{8,7},{9,8},{10,9},{11,1... | collective-permute-start | bytes 393224 | tf_op jit(solution)/shard_map/ppermute | solution.py:735
  5.8 8.2 %inner_step.1 = (f32[4,64,2048]{2,1,0:T(8,128)}, bf16[384,1024]{1,0:T(8,128)(2,1)S(1)}, bf16[384,1024]{1,0:T(8,128)(2,1)S(1)}, f32[4,16,2048]{2,1,0:T(8,128)S(1)...) custom-call(f32[4,64,2048]{2,1,0:T(8,128)} %prev.1, ...), custom_call_target="tpu_custom_call" | custom-call | flops 31457280 | bytes 12582912 | tf_op jit(solution)/shard_map/inner_step/pallas_call | solution.py:275
  14.0 0.0 collective-permute-done.top
  14.0 0.0 collective-permute-done.1.bottom
  14.0 0.0 copy-start
  14.0 0.0 copy-start.1
  14.1 0.0 copy-start.2
  14.1 0.0 copy-start.3
  14.1 6.2 %outer_step.1 = (f32[4,64,2048]{2,1,0:T(8,128)}, f32[256,256]{1,0:T(8,128)S(1)}, f32[256,256]{1,0:T(8,128)S(1)}, f32[256,256]{1,0:T(8,128)S(1)}, f32[256,256]{1,...) custom-call(s32[1]{0:T(128)} %bitcast.place, ...), custom_call_target="tpu_custom_call", output_to_operand_aliasing={{0}: (10, {})} | custom-call | flops 3221225472 | bytes 4194304 | tf_op jit(solution)/shard_map/outer_step/pallas_call | solution.py:389
  20.3 2.8 %collective-permute-start.2 = (f32[256,256]{1,0:T(8,128)S(1)}, f32[256,256]{1,0:T(8,128)S(1)}, u32[]{:S(2)}, u32[]{:S(2)}) collective-permute-start(f32[256,256]{1,0:T(8,128)S(1)} %get-tuple-element.52), channel_id=1, source_target_pairs={{0,160},{32,128},{64,224},{96,192},{128,32},{160,0},{192,96},{224,... | collective-permute-start | bytes 786440 | tf_op jit(solution)/shard_map/ppermute | solution.py:718
  23.1 1.9 %collective-permute-start.3 = (f32[256,256]{1,0:T(8,128)S(1)}, f32[256,256]{1,0:T(8,128)S(1)}, u32[]{:S(2)}, u32[]{:S(2)}) collective-permute-start(f32[256,256]{1,0:T(8,128)S(1)} %get-tuple-element.53), channel_id=1, source_target_pairs={{0,32},{32,0},{64,96},{96,64},{128,160},{160,128},{192,224},{224,1... | collective-permute-start | bytes 786440 | tf_op jit(solution)/shard_map/ppermute | solution.py:718
  25.0 0.3 collective-permute-start.4
  25.3 1.1 collective-permute-start.5
  26.5 3.0 %collective-permute-start.6 = (f32[256,256]{1,0:T(8,128)S(1)}, f32[256,256]{1,0:T(8,128)S(1)}, u32[]{:S(2)}, u32[]{:S(2)}) collective-permute-start(f32[256,256]{1,0:T(8,128)S(1)} %get-tuple-element.56), channel_id=1, source_target_pairs={{0,224},{32,192},{64,32},{96,0},{128,96},{160,64},{192,160},{224,1... | collective-permute-start | bytes 786440 | tf_op jit(solution)/shard_map/ppermute | solution.py:718
  29.5 1.0 collective-permute-done.2
  30.5 1.6 %collective-permute-start.7 = (f32[256,256]{1,0:T(8,128)S(1)}, f32[256,256]{1,0:T(8,128)S(1)}, u32[]{:S(2)}, u32[]{:S(2)}) collective-permute-start(f32[256,256]{1,0:T(8,128)S(1)} %get-tuple-element.57), channel_id=1, source_target_pairs={{0,64},{32,96},{64,128},{96,160},{128,192},{160,224},{192,0},{224,... | collective-permute-start | bytes 786440 | tf_op jit(solution)/shard_map/ppermute | solution.py:718
  32.1 4.2 %collective-permute-done.3 = f32[256,256]{1,0:T(8,128)S(1)} collective-permute-done((f32[256,256]{1,0:T(8,128)S(1)}, f32[256,256]{1,0:T(8,128)S(1)}, u32[]{:S(2)}, u32[]{:S(2)}) %collective-permute-start.3) | collective-permute-done | bytes 262176 | tf_op jit(solution)/shard_map/ppermute | solution.py:718
  36.3 1.0 collective-permute-start.8
  37.3 0.0 copy-done
  37.4 0.0 copy-done.1
  37.4 0.0 copy-done.2
  37.4 0.0 copy-done.3
  37.4 1.6 %prepare.1 = (f32[32,256]{1,0:T(8,128)S(1)}, f32[32,256]{1,0:T(8,128)S(1)}, f32[32,256]{1,0:T(8,128)S(1)}, bf16[256,256]{1,0:T(8,128)(2,1)S(1)}, bf16[256,256]{1...) custom-call(s32[1]{0:T(128)} %bitcast.1.shard, f32[8,256]{1,0:T(8,128)S(1)} %copy-done.2, ...), custom_call_target="tpu_custom_call" | custom-call | tf_op jit(solution)/shard_map/prepare/pallas_call | solution.py:460
  39.0 0.0 collective-permute-done.4
  39.0 3.5 %collective-permute-done.5 = f32[256,256]{1,0:T(8,128)S(1)} collective-permute-done((f32[256,256]{1,0:T(8,128)S(1)}, f32[256,256]{1,0:T(8,128)S(1)}, u32[]{:S(2)}, u32[]{:S(2)}) %collective-permute-start.5) | collective-permute-done | bytes 262176 | tf_op jit(solution)/shard_map/ppermute | solution.py:718
  42.5 6.0 %collective-permute-done.6 = f32[256,256]{1,0:T(8,128)S(1)} collective-permute-done((f32[256,256]{1,0:T(8,128)S(1)}, f32[256,256]{1,0:T(8,128)S(1)}, u32[]{:S(2)}, u32[]{:S(2)}) %collective-permute-start.6) | collective-permute-done | bytes 262176 | tf_op jit(solution)/shard_map/ppermute | solution.py:718
  48.6 0.0 collective-permute-done.7
  48.6 0.0 collective-permute-done.8
  48.6 1.8 %project.1 = (f32[64,32,256]{2,1,0:T(8,128)S(1)}, f32[2,32,256]{2,1,0:T(8,128)S(1)}) custom-call(bf16[256,256]{1,0:T(8,128)(2,1)S(1)} %get-tuple-element.48.mix_high, bf16[256,256]{1,0:T(8,128)(2,1)S(1)} %get-tuple-element.49.mix_low, f32[32,256]{1,0:T(8,128)S(1)} %get-tuple-element.50.ratio, f32[4,64,256]{2,1,0:T(8,128)S(1)} %bitcast.19, ...), custom_call_target="tpu_custom_call" | custom-call | tf_op jit(solution)/shard_map/project/pallas_call | solution.py:499
  50.3 2.4 %collective-permute-start.9 = (f32[2,32,256]{2,1,0:T(8,128)S(1)}, f32[2,32,256]{2,1,0:T(8,128)S(1)}, u32[]{:S(2)}, u32[]{:S(2)}) collective-permute-start(f32[2,32,256]{2,1,0:T(8,128)S(1)} %get-tuple-element.63.refs_0_), channel_id=1, source_target_pairs={{1,0},{0,1},{3,2},{2,3},{5,4},{4,5},{7,6},{6,7},{9,8},{8,9},{11,10... | collective-permute-start | bytes 196616 | tf_op jit(solution)/shard_map/ppermute | solution.py:523
  52.8 0.9 collective-permute-done.9.refs_1_
  53.7 6.8 %collective-permute-start.10 = (f32[2,32,256]{2,1,0:T(8,128)S(1)}, f32[2,32,256]{2,1,0:T(8,128)S(1)}, u32[]{:S(2)}, u32[]{:S(2)}) collective-permute-start(f32[2,32,256]{2,1,0:T(8,128)S(1)} %join.2.refs_0_.refs_2_), channel_id=1, source_target_pairs={{2,0},{3,1},{4,2},{5,3},{6,4},{7,5},{0,6},{1,7},{10,8},{11,9},{12,... | collective-permute-start | bytes 196616 | tf_op jit(solution)/shard_map/ppermute | solution.py:523
  60.5 0.0 collective-permute-start.11
  60.5 1.0 collective-permute-start.12
  61.5 2.2 %collective-permute-done.10.refs_1_.refs_3_ = f32[2,32,256]{2,1,0:T(8,128)S(1)} collective-permute-done((f32[2,32,256]{2,1,0:T(8,128)S(1)}, f32[2,32,256]{2,1,0:T(8,128)S(1)}, u32[]{:S(2)}, u32[]{:S(2)}) %collective-permute-start.10) | collective-permute-done | bytes 65568 | tf_op jit(solution)/shard_map/ppermute | solution.py:523
  63.6 3.0 %collective-permute-done.11.refs_2_.refs_4_ = f32[2,32,256]{2,1,0:T(8,128)S(1)} collective-permute-done((f32[2,32,256]{2,1,0:T(8,128)S(1)}, f32[2,32,256]{2,1,0:T(8,128)S(1)}, u32[]{:S(2)}, u32[]{:S(2)}) %collective-permute-start.11) | collective-permute-done | bytes 65568 | tf_op jit(solution)/shard_map/ppermute | solution.py:523
  66.6 0.4 collective-permute-done.12.refs_3_.refs_5_
  67.0 0.1 join.3.refs_6_
  67.1 3.3 %collective-permute-start.13 = (f32[2,32,256]{2,1,0:T(8,128)S(1)}, f32[2,32,256]{2,1,0:T(8,128)S(1)}, u32[]{:S(2)}, u32[]{:S(2)}) collective-permute-start(f32[2,32,256]{2,1,0:T(8,128)S(1)} %join.3.refs_6_), channel_id=1, source_target_pairs={{8,0},{9,1},{10,2},{11,3},{12,4},{13,5},{14,6},{15,7},{16,8},{17,9... | collective-permute-start | bytes 196616 | tf_op jit(solution)/shard_map/ppermute | solution.py:523
  70.3 2.1 %collective-permute-start.14 = (f32[2,32,256]{2,1,0:T(8,128)S(1)}, f32[2,32,256]{2,1,0:T(8,128)S(1)}, u32[]{:S(2)}, u32[]{:S(2)}) collective-permute-start(f32[2,32,256]{2,1,0:T(8,128)S(1)} %join.3.refs_6_), channel_id=1, source_target_pairs={{16,0},{17,1},{18,2},{19,3},{20,4},{21,5},{22,6},{23,7},{24,8},{25... | collective-permute-start | bytes 196616 | tf_op jit(solution)/shard_map/ppermute | solution.py:523
  72.5 2.2 %collective-permute-start.15 = (f32[2,32,256]{2,1,0:T(8,128)S(1)}, f32[2,32,256]{2,1,0:T(8,128)S(1)}, u32[]{:S(2)}, u32[]{:S(2)}) collective-permute-start(f32[2,32,256]{2,1,0:T(8,128)S(1)} %join.3.refs_6_), channel_id=1, source_target_pairs={{24,0},{25,1},{26,2},{27,3},{28,4},{29,5},{30,6},{31,7},{0,8},{1,9... | collective-permute-start | bytes 196616 | tf_op jit(solution)/shard_map/ppermute | solution.py:523
  74.6 0.0 collective-permute-done.13.refs_7_
  74.6 4.8 %collective-permute-done.14.refs_8_ = f32[2,32,256]{2,1,0:T(8,128)S(1)} collective-permute-done((f32[2,32,256]{2,1,0:T(8,128)S(1)}, f32[2,32,256]{2,1,0:T(8,128)S(1)}, u32[]{:S(2)}, u32[]{:S(2)}) %collective-permute-start.14) | collective-permute-done | bytes 65568 | tf_op jit(solution)/shard_map/ppermute | solution.py:523
  79.4 0.9 collective-permute-done.15.refs_9_
  80.3 2.1 %solve.1 = (f32[4,64,256]{2,1,0:T(8,128)S(1)}, f32[4,64,256]{2,1,0:T(8,128)S(1)}, f32[4,64,256]{2,1,0:T(8,128)S(1)}, f32[4,64,256]{2,1,0:T(8,128)S(1)}, f32[4,64...) custom-call(s32[1]{0:T(128)} %bitcast.place, ...), custom_call_target="tpu_custom_call" | custom-call | tf_op jit(solution)/shard_map/solve/pallas_call | solution.py:620
  82.4 0.7 collective-permute-start.16
  83.2 2.0 %collective-permute-start.17 = (f32[256,256]{1,0:T(8,128)S(1)}, f32[256,256]{1,0:T(8,128)S(1)}, u32[]{:S(2)}, u32[]{:S(2)}) collective-permute-start(f32[256,256]{1,0:T(8,128)S(1)} %bitcast.33), channel_id=1, source_target_pairs={{0,32},{32,0},{64,96},{96,64},{128,160},{160,128},{192,224},{224,1... | collective-permute-start | bytes 786440 | tf_op jit(solution)/shard_map/ppermute | solution.py:718
  85.2 2.3 %collective-permute-start.18 = (f32[256,256]{1,0:T(8,128)S(1)}, f32[256,256]{1,0:T(8,128)S(1)}, u32[]{:S(2)}, u32[]{:S(2)}) collective-permute-start(f32[256,256]{1,0:T(8,128)S(1)} %bitcast.32), channel_id=1, source_target_pairs={{0,128},{32,160},{64,192},{96,224},{128,0},{160,32},{192,64},{224,... | collective-permute-start | bytes 786440 | tf_op jit(solution)/shard_map/ppermute | solution.py:718
  87.5 0.6 collective-permute-start.19
  88.1 3.5 %collective-permute-start.20 = (f32[256,256]{1,0:T(8,128)S(1)}, f32[256,256]{1,0:T(8,128)S(1)}, u32[]{:S(2)}, u32[]{:S(2)}) collective-permute-start(f32[256,256]{1,0:T(8,128)S(1)} %bitcast.30), channel_id=1, source_target_pairs={{0,224},{32,192},{64,32},{96,0},{128,96},{160,64},{192,160},{224,1... | collective-permute-start | bytes 786440 | tf_op jit(solution)/shard_map/ppermute | solution.py:718
  91.7 3.1 %collective-permute-done.16.refs_1_ = f32[256,256]{1,0:T(8,128)S(1)} collective-permute-done((f32[256,256]{1,0:T(8,128)S(1)}, f32[256,256]{1,0:T(8,128)S(1)}, u32[]{:S(2)}, u32[]{:S(2)}) %collective-permute-start.16) | collective-permute-done | bytes 262176 | tf_op jit(solution)/shard_map/ppermute | solution.py:718
  94.7 0.4 collective-permute-start.21
  95.1 3.0 %collective-permute-done.17.refs_2_ = f32[256,256]{1,0:T(8,128)S(1)} collective-permute-done((f32[256,256]{1,0:T(8,128)S(1)}, f32[256,256]{1,0:T(8,128)S(1)}, u32[]{:S(2)}, u32[]{:S(2)}) %collective-permute-start.17) | collective-permute-done | bytes 262176 | tf_op jit(solution)/shard_map/ppermute | solution.py:718
  98.1 2.3 %collective-permute-start.22 = (f32[256,256]{1,0:T(8,128)S(1)}, f32[256,256]{1,0:T(8,128)S(1)}, u32[]{:S(2)}, u32[]{:S(2)}) collective-permute-start(f32[256,256]{1,0:T(8,128)S(1)} %bitcast.28), channel_id=1, source_target_pairs={{0,192},{32,224},{64,0},{96,32},{128,64},{160,96},{192,128},{224,1... | collective-permute-start | bytes 786440 | tf_op jit(solution)/shard_map/ppermute | solution.py:718
  100.4 1.2 %collective-permute-done.18.refs_3_ = f32[256,256]{1,0:T(8,128)S(1)} collective-permute-done((f32[256,256]{1,0:T(8,128)S(1)}, f32[256,256]{1,0:T(8,128)S(1)}, u32[]{:S(2)}, u32[]{:S(2)}) %collective-permute-start.18) | collective-permute-done | bytes 262176 | tf_op jit(solution)/shard_map/ppermute | solution.py:718
  101.6 1.9 %inverse_part.1.partial = f32[512,1024]{1,0:T(8,128)S(1)} custom-call(s32[1]{0:T(128)} %bitcast.1.shard, bf16[1024,1024]{1,0:T(8,128)(2,1)S(1)} %get-tuple-element.43.table_high, bf16[1024,1024]{1,0:T(8,128)(2,1)S(1)} %get-tuple-element.44.table_low, f32[256,256]{1,0:T(8,128)S(1)} %bitcast.27, f32[256,256]{1,0:T(8,128)S(1)} %collective-permute-done.16.refs_1_, ...), custom_call_target="tpu_custom_call" | custom-call | flops 1610612736 | bytes 2097152 | tf_op jit(solution)/shard_map/inverse_part/pallas_call | solution.py:690
  103.5 1.1 collective-permute-done.19.refs_0_
  104.6 3.0 %collective-permute-done.20.refs_1_ = f32[256,256]{1,0:T(8,128)S(1)} collective-permute-done((f32[256,256]{1,0:T(8,128)S(1)}, f32[256,256]{1,0:T(8,128)S(1)}, u32[]{:S(2)}, u32[]{:S(2)}) %collective-permute-start.20) | collective-permute-done | bytes 262176 | tf_op jit(solution)/shard_map/ppermute | solution.py:718
  107.6 0.2 collective-permute-done.21.refs_2_
  107.8 0.8 collective-permute-done.22.refs_3_
  108.6 3.1 %inverse_rest.1 = f32[256,2048]{1,0:T(8,128)} custom-call(s32[1]{0:T(128)} %bitcast.1.shard, bf16[1024,1024]{1,0:T(8,128)(2,1)S(1)} %get-tuple-element.43.table_high, bf16[1024,1024]{1,0:T(8,128)(2,1)S(1)} %get-tuple-element.44.table_low, f32[512,1024]{1,0:T(8,128)S(1)} %inverse_part.1.partial, f32[256,256]{1,0:T(8,128)S(1)} %collective-permute-done.19.refs_0_, ...), custom_call_target="tpu_custom_call" | custom-call | tf_op jit(solution)/shard_map/inverse_rest/pallas_call | solution.py:701
  (1 shorter events, 0.0 us)
Async XLA Ops:
  2.7 11.3 %collective-permute-start = (f32[4,4,2048]{2,1,0:T(4,128)}, f32[4,4,2048]{2,1,0:T(4,128)S(1)}, u32[]{:S(2)}, u32[]{:S(2)}) collective-permute-start(f32[4,4,2048]{2,1,0:T(4,128)} %get-tuple-element.37), channel_id=1, source_target_pairs={{0,1},{1,2},{2,3},{3,4},{4,5},{5,6},{6,7},{7,8},{8,9},{9,10},{10,1... | collective-permute-start | bytes 393224 | tf_op jit(solution)/shard_map/ppermute | solution.py:734
  4.5 9.6 %collective-permute-start.1 = (f32[4,4,2048]{2,1,0:T(4,128)}, f32[4,4,2048]{2,1,0:T(4,128)S(1)}, u32[]{:S(2)}, u32[]{:S(2)}) collective-permute-start(f32[4,4,2048]{2,1,0:T(4,128)} %get-tuple-element.38), channel_id=1, source_target_pairs={{1,0},{2,1},{3,2},{4,3},{5,4},{6,5},{7,6},{8,7},{9,8},{10,9},{11,1... | collective-permute-start | bytes 393224 | tf_op jit(solution)/shard_map/ppermute | solution.py:735
  14.0 23.3 %copy-start = (f32[32,32]{1,0:T(8,128)S(1)}, f32[32,32]{1,0:T(8,128)}, u32[]{:S(2)}) copy-start(f32[32,32]{1,0:T(8,128)} %to_modes.1) | copy-start | bytes 12292
  14.0 23.3 %copy-start.1 = (f32[32,32]{1,0:T(8,128)S(1)}, f32[32,32]{1,0:T(8,128)}, u32[]{:S(2)}) copy-start(f32[32,32]{1,0:T(8,128)} %to_layers.1) | copy-start | bytes 12292
  14.1 23.3 %copy-start.2 = (f32[8,256]{1,0:T(8,128)S(1)}, f32[8,256]{1,0:T(8,128)}, u32[]{:S(2)}) copy-start(f32[8,256]{1,0:T(8,128)} %constant.17.clone.eigen) | copy-start | bytes 24580
  14.1 23.3 %copy-start.3 = (f32[32]{0:T(128)S(1)}, f32[32]{0:T(128)}, u32[]{:S(2)}) copy-start(f32[32]{0:T(128)} %stretch.1) | copy-start | bytes 388
  20.3 10.2 %collective-permute-start.2 = (f32[256,256]{1,0:T(8,128)S(1)}, f32[256,256]{1,0:T(8,128)S(1)}, u32[]{:S(2)}, u32[]{:S(2)}) collective-permute-start(f32[256,256]{1,0:T(8,128)S(1)} %get-tuple-element.52), channel_id=1, source_target_pairs={{0,160},{32,128},{64,224},{96,192},{128,32},{160,0},{192,96},{224,... | collective-permute-start | bytes 786440 | tf_op jit(solution)/shard_map/ppermute | solution.py:718
  23.1 13.3 %collective-permute-start.3 = (f32[256,256]{1,0:T(8,128)S(1)}, f32[256,256]{1,0:T(8,128)S(1)}, u32[]{:S(2)}, u32[]{:S(2)}) collective-permute-start(f32[256,256]{1,0:T(8,128)S(1)} %get-tuple-element.53), channel_id=1, source_target_pairs={{0,32},{32,0},{64,96},{96,64},{128,160},{160,128},{192,224},{224,1... | collective-permute-start | bytes 786440 | tf_op jit(solution)/shard_map/ppermute | solution.py:718
  25.0 14.0 %collective-permute-start.4 = (f32[256,256]{1,0:T(8,128)S(1)}, f32[256,256]{1,0:T(8,128)S(1)}, u32[]{:S(2)}, u32[]{:S(2)}) collective-permute-start(f32[256,256]{1,0:T(8,128)S(1)} %get-tuple-element.54), channel_id=1, source_target_pairs={{0,128},{32,160},{64,192},{96,224},{128,0},{160,32},{192,64},{224,... | collective-permute-start | bytes 786440 | tf_op jit(solution)/shard_map/ppermute | solution.py:718
  25.3 17.2 %collective-permute-start.5 = (f32[256,256]{1,0:T(8,128)S(1)}, f32[256,256]{1,0:T(8,128)S(1)}, u32[]{:S(2)}, u32[]{:S(2)}) collective-permute-start(f32[256,256]{1,0:T(8,128)S(1)} %get-tuple-element.55), channel_id=1, source_target_pairs={{0,96},{32,64},{64,160},{96,128},{128,224},{160,192},{192,32},{224... | collective-permute-start | bytes 786440 | tf_op jit(solution)/shard_map/ppermute | solution.py:718
  26.5 22.1 %collective-permute-start.6 = (f32[256,256]{1,0:T(8,128)S(1)}, f32[256,256]{1,0:T(8,128)S(1)}, u32[]{:S(2)}, u32[]{:S(2)}) collective-permute-start(f32[256,256]{1,0:T(8,128)S(1)} %get-tuple-element.56), channel_id=1, source_target_pairs={{0,224},{32,192},{64,32},{96,0},{128,96},{160,64},{192,160},{224,1... | collective-permute-start | bytes 786440 | tf_op jit(solution)/shard_map/ppermute | solution.py:718
  30.5 18.1 %collective-permute-start.7 = (f32[256,256]{1,0:T(8,128)S(1)}, f32[256,256]{1,0:T(8,128)S(1)}, u32[]{:S(2)}, u32[]{:S(2)}) collective-permute-start(f32[256,256]{1,0:T(8,128)S(1)} %get-tuple-element.57), channel_id=1, source_target_pairs={{0,64},{32,96},{64,128},{96,160},{128,192},{160,224},{192,0},{224,... | collective-permute-start | bytes 786440 | tf_op jit(solution)/shard_map/ppermute | solution.py:718
  36.3 12.2 %collective-permute-start.8 = (f32[256,256]{1,0:T(8,128)S(1)}, f32[256,256]{1,0:T(8,128)S(1)}, u32[]{:S(2)}, u32[]{:S(2)}) collective-permute-start(f32[256,256]{1,0:T(8,128)S(1)} %get-tuple-element.58), channel_id=1, source_target_pairs={{0,192},{32,224},{64,0},{96,32},{128,64},{160,96},{192,128},{224,1... | collective-permute-start | bytes 786440 | tf_op jit(solution)/shard_map/ppermute | solution.py:718
  50.3 3.4 %collective-permute-start.9 = (f32[2,32,256]{2,1,0:T(8,128)S(1)}, f32[2,32,256]{2,1,0:T(8,128)S(1)}, u32[]{:S(2)}, u32[]{:S(2)}) collective-permute-start(f32[2,32,256]{2,1,0:T(8,128)S(1)} %get-tuple-element.63.refs_0_), channel_id=1, source_target_pairs={{1,0},{0,1},{3,2},{2,3},{5,4},{4,5},{7,6},{6,7},{9,8},{8,9},{11,10... | collective-permute-start | bytes 196616 | tf_op jit(solution)/shard_map/ppermute | solution.py:523
  53.7 9.9 %collective-permute-start.10 = (f32[2,32,256]{2,1,0:T(8,128)S(1)}, f32[2,32,256]{2,1,0:T(8,128)S(1)}, u32[]{:S(2)}, u32[]{:S(2)}) collective-permute-start(f32[2,32,256]{2,1,0:T(8,128)S(1)} %join.2.refs_0_.refs_2_), channel_id=1, source_target_pairs={{2,0},{3,1},{4,2},{5,3},{6,4},{7,5},{0,6},{1,7},{10,8},{11,9},{12,... | collective-permute-start | bytes 196616 | tf_op jit(solution)/shard_map/ppermute | solution.py:523
  60.5 6.1 %collective-permute-start.11 = (f32[2,32,256]{2,1,0:T(8,128)S(1)}, f32[2,32,256]{2,1,0:T(8,128)S(1)}, u32[]{:S(2)}, u32[]{:S(2)}) collective-permute-start(f32[2,32,256]{2,1,0:T(8,128)S(1)} %join.2.refs_0_.refs_2_), channel_id=1, source_target_pairs={{4,0},{5,1},{6,2},{7,3},{0,4},{1,5},{2,6},{3,7},{12,8},{13,9},{14,... | collective-permute-start | bytes 196616 | tf_op jit(solution)/shard_map/ppermute | solution.py:523
  60.5 6.5 %collective-permute-start.12 = (f32[2,32,256]{2,1,0:T(8,128)S(1)}, f32[2,32,256]{2,1,0:T(8,128)S(1)}, u32[]{:S(2)}, u32[]{:S(2)}) collective-permute-start(f32[2,32,256]{2,1,0:T(8,128)S(1)} %join.2.refs_0_.refs_2_), channel_id=1, source_target_pairs={{6,0},{7,1},{0,2},{1,3},{2,4},{3,5},{4,6},{5,7},{14,8},{15,9},{8,1... | collective-permute-start | bytes 196616 | tf_op jit(solution)/shard_map/ppermute | solution.py:523
  67.1 7.6 %collective-permute-start.13 = (f32[2,32,256]{2,1,0:T(8,128)S(1)}, f32[2,32,256]{2,1,0:T(8,128)S(1)}, u32[]{:S(2)}, u32[]{:S(2)}) collective-permute-start(f32[2,32,256]{2,1,0:T(8,128)S(1)} %join.3.refs_6_), channel_id=1, source_target_pairs={{8,0},{9,1},{10,2},{11,3},{12,4},{13,5},{14,6},{15,7},{16,8},{17,9... | collective-permute-start | bytes 196616 | tf_op jit(solution)/shard_map/ppermute | solution.py:523
  70.3 9.1 %collective-permute-start.14 = (f32[2,32,256]{2,1,0:T(8,128)S(1)}, f32[2,32,256]{2,1,0:T(8,128)S(1)}, u32[]{:S(2)}, u32[]{:S(2)}) collective-permute-start(f32[2,32,256]{2,1,0:T(8,128)S(1)} %join.3.refs_6_), channel_id=1, source_target_pairs={{16,0},{17,1},{18,2},{19,3},{20,4},{21,5},{22,6},{23,7},{24,8},{25... | collective-permute-start | bytes 196616 | tf_op jit(solution)/shard_map/ppermute | solution.py:523
  72.5 7.8 %collective-permute-start.15 = (f32[2,32,256]{2,1,0:T(8,128)S(1)}, f32[2,32,256]{2,1,0:T(8,128)S(1)}, u32[]{:S(2)}, u32[]{:S(2)}) collective-permute-start(f32[2,32,256]{2,1,0:T(8,128)S(1)} %join.3.refs_6_), channel_id=1, source_target_pairs={{24,0},{25,1},{26,2},{27,3},{28,4},{29,5},{30,6},{31,7},{0,8},{1,9... | collective-permute-start | bytes 196616 | tf_op jit(solution)/shard_map/ppermute | solution.py:523
  82.4 12.3 %collective-permute-start.16 = (f32[256,256]{1,0:T(8,128)S(1)}, f32[256,256]{1,0:T(8,128)S(1)}, u32[]{:S(2)}, u32[]{:S(2)}) collective-permute-start(f32[256,256]{1,0:T(8,128)S(1)} %bitcast.34), channel_id=1, source_target_pairs={{0,160},{32,128},{64,224},{96,192},{128,32},{160,0},{192,96},{224,... | collective-permute-start | bytes 786440 | tf_op jit(solution)/shard_map/ppermute | solution.py:718
  83.2 14.9 %collective-permute-start.17 = (f32[256,256]{1,0:T(8,128)S(1)}, f32[256,256]{1,0:T(8,128)S(1)}, u32[]{:S(2)}, u32[]{:S(2)}) collective-permute-start(f32[256,256]{1,0:T(8,128)S(1)} %bitcast.33), channel_id=1, source_target_pairs={{0,32},{32,0},{64,96},{96,64},{128,160},{160,128},{192,224},{224,1... | collective-permute-start | bytes 786440 | tf_op jit(solution)/shard_map/ppermute | solution.py:718
  85.2 16.4 %collective-permute-start.18 = (f32[256,256]{1,0:T(8,128)S(1)}, f32[256,256]{1,0:T(8,128)S(1)}, u32[]{:S(2)}, u32[]{:S(2)}) collective-permute-start(f32[256,256]{1,0:T(8,128)S(1)} %bitcast.32), channel_id=1, source_target_pairs={{0,128},{32,160},{64,192},{96,224},{128,0},{160,32},{192,64},{224,... | collective-permute-start | bytes 786440 | tf_op jit(solution)/shard_map/ppermute | solution.py:718
  87.5 17.1 %collective-permute-start.19 = (f32[256,256]{1,0:T(8,128)S(1)}, f32[256,256]{1,0:T(8,128)S(1)}, u32[]{:S(2)}, u32[]{:S(2)}) collective-permute-start(f32[256,256]{1,0:T(8,128)S(1)} %bitcast.31), channel_id=1, source_target_pairs={{0,96},{32,64},{64,160},{96,128},{128,224},{160,192},{192,32},{224... | collective-permute-start | bytes 786440 | tf_op jit(solution)/shard_map/ppermute | solution.py:718
  88.1 19.5 %collective-permute-start.20 = (f32[256,256]{1,0:T(8,128)S(1)}, f32[256,256]{1,0:T(8,128)S(1)}, u32[]{:S(2)}, u32[]{:S(2)}) collective-permute-start(f32[256,256]{1,0:T(8,128)S(1)} %bitcast.30), channel_id=1, source_target_pairs={{0,224},{32,192},{64,32},{96,0},{128,96},{160,64},{192,160},{224,1... | collective-permute-start | bytes 786440 | tf_op jit(solution)/shard_map/ppermute | solution.py:718
  94.7 13.0 %collective-permute-start.21 = (f32[256,256]{1,0:T(8,128)S(1)}, f32[256,256]{1,0:T(8,128)S(1)}, u32[]{:S(2)}, u32[]{:S(2)}) collective-permute-start(f32[256,256]{1,0:T(8,128)S(1)} %bitcast.29), channel_id=1, source_target_pairs={{0,64},{32,96},{64,128},{96,160},{128,192},{160,224},{192,0},{224,... | collective-permute-start | bytes 786440 | tf_op jit(solution)/shard_map/ppermute | solution.py:718
  98.1 10.5 %collective-permute-start.22 = (f32[256,256]{1,0:T(8,128)S(1)}, f32[256,256]{1,0:T(8,128)S(1)}, u32[]{:S(2)}, u32[]{:S(2)}) collective-permute-start(f32[256,256]{1,0:T(8,128)S(1)} %bitcast.28), channel_id=1, source_target_pairs={{0,192},{32,224},{64,0},{96,32},{128,64},{160,96},{192,128},{224,1... | collective-permute-start | bytes 786440 | tf_op jit(solution)/shard_map/ppermute | solution.py:718

commit v6 on v5

--- a/solution.py
+++ b/solution.py
@@ -191,8 +191,8 @@
             write(c - LAG, (lower + upper) * sign, lower - upper)
 
 
-def inner_kernel(prev, now, psi, table_high_in, table_low_in, q_out, high, low, rim, near, table_high, table_low, *scratch):
-    fields, q_held, p, z, ze, zw, q, qe, qw, sems, q_sems, table_sems = scratch
+def inner_kernel(prev, now, psi, q_out, high, low, rim, near, *scratch):
+    fields, q_held, p, z, ze, zw, q, qe, qw, sems, q_sems = scratch
     layers, rows, cols = prev.shape
     inner = rows - 16
     layer = pl.program_id(0)
@@ -206,11 +206,6 @@
         return pltpu.make_async_copy(
             q_held.at[index, pl.ds(8, inner)], q_out.at[index, pl.ds(8, inner)], q_sems.at[index]
         )
-
-    tables = [
-        pltpu.make_async_copy(table_high_in, table_high, table_sems.at[0]),
-        pltpu.make_async_copy(table_low_in, table_low, table_sems.at[1]),
-    ]
 
     @pl.when(layer == 0)
     def _():
@@ -231,11 +226,6 @@
         for which in range(3):
             load(layer + 2, which).start()
 
-    @pl.when(layer == layers - 2)
-    def _():
-        for table in tables:
-            table.start()
-
     shift_columns(z, ze, zw)
     shift_columns(q, qe, qw)
 
@@ -262,46 +252,46 @@
     def _():
         for index in range(layers):
             save(index).wait()
-        for table in tables:
-            table.wait()
-
-
-def inner_step(q_prev, q_now, psi_now, table_high, table_low):
+
+
+def inner_step(q_prev, q_now, psi_now):
     layers, rows, cols = q_prev.shape
     depth = cols // 2
     hbm = pl.BlockSpec(memory_space=pltpu.HBM)
     lines = jax.ShapeDtypeStruct((2 * layers * (rows - 16), depth), BF16)
-    table = jax.ShapeDtypeStruct((depth, depth), BF16)
     return pl.pallas_call(
         inner_kernel,
         grid=(layers,),
-        in_specs=[hbm] * 5,
-        out_specs=[hbm] + [vmem()] * 6,
+        in_specs=[hbm] * 3,
+        out_specs=[hbm] + [vmem()] * 4,
         out_shape=[
             jax.ShapeDtypeStruct(q_prev.shape, F32),
             lines,
             lines,
             jax.ShapeDtypeStruct((layers, 16, cols), F32),
             jax.ShapeDtypeStruct((3, layers, 8, cols), F32),
-            table,
-            table,
         ],
         scratch_shapes=[pltpu.VMEM((2, 3, rows, cols), F32), pltpu.VMEM((layers, rows, cols), F32)]
         + [pltpu.VMEM((cols // LANES, rows + 16, LANES), F32)] * 7
         + [
             pltpu.SemaphoreType.DMA((2, 3)),
             pltpu.SemaphoreType.DMA((layers,)),
-            pltpu.SemaphoreType.DMA((2,)),
         ],
         compiler_params=params(INNER_LIMIT),
         cost_estimate=pl.CostEstimate(flops=60 * layers * rows * cols, bytes_accessed=12 << 20, transcendentals=0),
         name="inner_step",
-    )(q_prev, q_now, psi_now, table_high, table_low)
-
-
-def outer_kernel(blocks, place, shard, top, bottom, high_in, low_in, rim, near, table_high, table_low, q_in, q_out, *refs):
+    )(q_prev, q_now, psi_now)
+
+
+def outer_kernel(blocks, place, shard, top, bottom, high_in, low_in, rim, near, table_high_in, table_low_in, q_in, q_out, table_high, table_low, *refs):
     leaving, scratch = refs[: len(MOVES)], refs[len(MOVES) :]
-    q_rim, p, z, ze, zw, q, qe, qw, high, low, held, q_sems = scratch
+    q_rim, p, z, ze, zw, q, qe, qw, high, low, held, q_sems, table_sems = scratch
+    tables = [
+        pltpu.make_async_copy(table_high_in, table_high, table_sems.at[0]),
+        pltpu.make_async_copy(table_low_in, table_low, table_sems.at[1]),
+    ]
+    for table in tables:
+        table.start()
     layers, _, cols = rim.shape
     shards, lines, width = held.shape
     width //= 2
@@ -372,6 +362,8 @@
                     held[2 * step + part, to + rows - 8 : to + rows, lane] = value[start + rows - 8 : start + rows, column]
         return carry
 
+    for table in tables:
+        table.wait()
     lax.fori_loop(0, shards // 2, columns, 0)
     for move, piece in zip(MOVES, leaving):
         piece[...] = held[target_shard(shard[0], move)]
@@ -388,9 +380,10 @@
     hbm = pl.BlockSpec(memory_space=pltpu.HBM)
     return pl.pallas_call(
         functools.partial(outer_kernel, blocks),
-        in_specs=[smem()] * 2 + [vmem()] * 8 + [hbm],
-        out_specs=[hbm] + [vmem()] * len(MOVES),
+        in_specs=[smem()] * 2 + [vmem()] * 6 + [hbm] * 3,
+        out_specs=[hbm] + [vmem()] * (2 + len(MOVES)),
         out_shape=[jax.ShapeDtypeStruct(q_next.shape, F32)]
+        + [jax.ShapeDtypeStruct((depth, depth), BF16)] * 2
         + [jax.ShapeDtypeStruct((lines, 2 * width), F32)] * len(MOVES),
         input_output_aliases={10: 0},
         scratch_shapes=[pltpu.VMEM((layers, 16, cols), F32)]
@@ -399,6 +392,7 @@
         + [
             pltpu.VMEM((shards, lines, 2 * width), F32),
             pltpu.SemaphoreType.DMA((layers, 2)),
+            pltpu.SemaphoreType.DMA((2,)),
         ],
         compiler_params=params(OUTER_LIMIT),
         cost_estimate=pl.CostEstimate(flops=12 * lines * depth * depth, bytes_accessed=4 << 20, transcendentals=0),
@@ -734,8 +728,8 @@
     top = lax.ppermute(last, "row", pairs)
     bottom = lax.ppermute(initial, "row", [(j, i) for i, j in pairs])
     theta, ratio, scale, *mixes = prepare(shard, eigen, stretch, layers_to_modes, modes_to_layers)
-    q_next, *folded, table_high, table_low = inner_step(q_prev, q_now, psi_now, table_high, table_low)
-    q_next, *leaving = outer_step(
+    q_next, *folded = inner_step(q_prev, q_now, psi_now)
+    q_next, table_high, table_low, *leaving = outer_step(
         place, shard, top, bottom, *folded, table_high, table_low, q_next, shards, blocks
     )
     arrived = move_pieces(leaving)

time: 113 us -> 117 us (1.035)
  local copies, waits for them, and re-layouts: 0.03 us -> 3.21 us
  waiting for transfers between devices: 39.2 us -> 40.6 us
    unnamed x8 -> x16, local copies, waits for them, and re-layouts: 0.03 us -> 3.21 us
    ppermute x14, waiting for transfers between devices: 27.1 us -> 28.4 us  [move_pieces(): arrived.append(lax.ppermute(piece, 'layer', pairs))]
where the time goes in v6:
time: 117 us
  starting transfers between devices  44.6 us (38%)
  waiting for transfers between devices  40.6 us (35%)
  Pallas kernels  27.5 us (24%)
  local copies, waits for them, and re-layouts  3.21 us (3%)
    ppermute x14, waiting for transfers between devices, move_pieces(): arrived.append(lax.ppermute(piece, 'layer', pairs))  28.4 us
    ppermute x14, starting transfers between devices, move_pieces(): arrived.append(lax.ppermute(piece, 'layer', pairs))  23.8 us
    ppermute x7, starting transfers between devices, exchange(): parts[shift] = lax.ppermute(total, 'row', pairs)  17.8 us
    ppermute x7, waiting for transfers between devices, exchange(): parts[shift] = lax.ppermute(total, 'row', pairs)  12.2 us
    pallas_call x1, Pallas kernels, inner_step(): pl.pallas_call(inner_kernel, grid=(layers,), in_specs=[hbm] * 3, out_spec...  8.32 us
    pallas_call x1, Pallas kernels, outer_step(): pl.pallas_call(functools.partial(outer_kernel, blocks), in_specs=[smem()]...  6.48 us
    unnamed x16, local copies, waits for them, and re-layouts  3.21 us
    pallas_call x1, Pallas kernels, inverse(): pl.pallas_call(functools.partial(inverse_rest_kernel, numbers), in_specs=...  3.09 us
  transfers between devices with their start and end apart: 23, of which 17 were waited for; matrix products, arithmetic and copies ran while one was open for 0% of the time, Pallas kernels for 10%

profile of v6, /device:TPU:32, one launch (start us, length us, event | category | flops | bytes accessed | tf_op | source)
XLA Modules:
  0.0 116.8 jit_solution(16928128938610169740)
XLA Ops:
  0.6 2.1 %rims.1 = (f32[4,4,2048]{2,1,0:T(4,128)}, f32[4,4,2048]{2,1,0:T(4,128)}) custom-call(f32[4,64,2048]{2,1,0:T(8,128)} %prev.1, f32[4,64,2048]{2,1,0:T(8,128)} %now.1, f32[4,64,2048]{2,1,0:T(8,128)} %psi.1, f32[4,64,2048]{2,1,0:T(8,128)} %prev.1, f32[4,64,2048]{2,1,0:T(8,128)} %now.1, f32[4,64,2048]{2,1,0:T(8,128)} %psi.1), custom_call_target="tpu_custom_call" | custom-call | tf_op jit(solution)/shard_map/rims/pallas_call | solution.py:98
  2.7 1.7 %collective-permute-start = (f32[4,4,2048]{2,1,0:T(4,128)}, f32[4,4,2048]{2,1,0:T(4,128)S(1)}, u32[]{:S(2)}, u32[]{:S(2)}) collective-permute-start(f32[4,4,2048]{2,1,0:T(4,128)} %get-tuple-element.37), channel_id=1, source_target_pairs={{0,1},{1,2},{2,3},{3,4},{4,5},{5,6},{6,7},{7,8},{8,9},{9,10},{10,1... | collective-permute-start | bytes 393224 | tf_op jit(solution)/shard_map/ppermute | solution.py:728
  4.5 1.3 %collective-permute-start.1 = (f32[4,4,2048]{2,1,0:T(4,128)}, f32[4,4,2048]{2,1,0:T(4,128)S(1)}, u32[]{:S(2)}, u32[]{:S(2)}) collective-permute-start(f32[4,4,2048]{2,1,0:T(4,128)} %get-tuple-element.38), channel_id=1, source_target_pairs={{1,0},{2,1},{3,2},{4,3},{5,4},{6,5},{7,6},{8,7},{9,8},{10,9},{11,1... | collective-permute-start | bytes 393224 | tf_op jit(solution)/shard_map/ppermute | solution.py:729
  5.8 0.0 copy-start
  5.8 1.6 %copy-done = f32[4,64,2048]{2,1,0:T(8,128)S(1)} copy-done((f32[4,64,2048]{2,1,0:T(8,128)S(1)}, f32[4,64,2048]{2,1,0:T(8,128)}, u32[]{:S(2)}) %copy-start) | copy-done | bytes 2097176
  7.4 1.6 %copy-done.1 = f32[4,64,2048]{2,1,0:T(8,128)S(1)} copy-done((f32[4,64,2048]{2,1,0:T(8,128)S(1)}, f32[4,64,2048]{2,1,0:T(8,128)}, u32[]{:S(2)}) %copy-start.1) | copy-done | bytes 2097176
  9.0 8.3 %inner_step.1 = (f32[4,64,2048]{2,1,0:T(8,128)}, bf16[384,1024]{1,0:T(8,128)(2,1)S(1)}, bf16[384,1024]{1,0:T(8,128)(2,1)S(1)}, f32[4,16,2048]{2,1,0:T(8,128)S(1)}, f32[3,4,8,2048]{3,2,1,0:T(8,128)S(1)}) custom-call(f32[4,64,2048]{2,1,0:T(8,128)S(1)} %copy-done, f32[4,64,2048]{2,1,0:T(8,128)S(1)} %copy-done.1, f32[4,64,2048]{2,1,0:T(8,128)} %psi.1), custom_call_target="tpu_custom_call" | custom-call | flops 31457280 | bytes 12582912 | tf_op jit(solution)/shard_map/inner_step/pallas_call | solution.py:262
  17.3 0.0 collective-permute-done.top
  17.3 0.0 collective-permute-done.1.bottom
  17.3 0.0 copy-done.6
  17.3 0.0 copy-start.2
  17.3 0.0 copy-start.3
  17.3 0.0 copy-start.4
  17.4 0.0 copy-start.5
  17.4 6.5 %outer_step.1 = (f32[4,64,2048]{2,1,0:T(8,128)}, bf16[1024,1024]{1,0:T(8,128)(2,1)S(1)}, bf16[1024,1024]{1,0:T(8,128)(2,1)S(1)}, f32[256,256]{1,0:T(8,128)S(1)},...) custom-call(s32[1]{0:T(128)} %bitcast.place, ...), custom_call_target="tpu_custom_call", output_to_operand_aliasing={{0}: (10, {})} | custom-call | flops 3221225472 | bytes 4194304 | tf_op jit(solution)/shard_map/outer_step/pallas_call | solution.py:381
  23.9 2.8 %collective-permute-start.2 = (f32[256,256]{1,0:T(8,128)S(1)}, f32[256,256]{1,0:T(8,128)S(1)}, u32[]{:S(2)}, u32[]{:S(2)}) collective-permute-start(f32[256,256]{1,0:T(8,128)S(1)} %get-tuple-element.52), channel_id=1, source_target_pairs={{0,160},{32,128},{64,224},{96,192},{128,32},{160,0},{192,96},{224,... | collective-permute-start | bytes 786440 | tf_op jit(solution)/shard_map/ppermute | solution.py:712
  26.7 1.9 %collective-permute-start.3 = (f32[256,256]{1,0:T(8,128)S(1)}, f32[256,256]{1,0:T(8,128)S(1)}, u32[]{:S(2)}, u32[]{:S(2)}) collective-permute-start(f32[256,256]{1,0:T(8,128)S(1)} %get-tuple-element.53), channel_id=1, source_target_pairs={{0,32},{32,0},{64,96},{96,64},{128,160},{160,128},{192,224},{224,1... | collective-permute-start | bytes 786440 | tf_op jit(solution)/shard_map/ppermute | solution.py:712
  28.6 0.3 collective-permute-start.4
  28.9 1.1 collective-permute-start.5
  30.1 3.0 %collective-permute-start.6 = (f32[256,256]{1,0:T(8,128)S(1)}, f32[256,256]{1,0:T(8,128)S(1)}, u32[]{:S(2)}, u32[]{:S(2)}) collective-permute-start(f32[256,256]{1,0:T(8,128)S(1)} %get-tuple-element.56), channel_id=1, source_target_pairs={{0,224},{32,192},{64,32},{96,0},{128,96},{160,64},{192,160},{224,1... | collective-permute-start | bytes 786440 | tf_op jit(solution)/shard_map/ppermute | solution.py:712
  33.1 1.0 collective-permute-done.2
  34.1 1.6 %collective-permute-start.7 = (f32[256,256]{1,0:T(8,128)S(1)}, f32[256,256]{1,0:T(8,128)S(1)}, u32[]{:S(2)}, u32[]{:S(2)}) collective-permute-start(f32[256,256]{1,0:T(8,128)S(1)} %get-tuple-element.57), channel_id=1, source_target_pairs={{0,64},{32,96},{64,128},{96,160},{128,192},{160,224},{192,0},{224,... | collective-permute-start | bytes 786440 | tf_op jit(solution)/shard_map/ppermute | solution.py:712
  35.7 4.2 %collective-permute-done.3 = f32[256,256]{1,0:T(8,128)S(1)} collective-permute-done((f32[256,256]{1,0:T(8,128)S(1)}, f32[256,256]{1,0:T(8,128)S(1)}, u32[]{:S(2)}, u32[]{:S(2)}) %collective-permute-start.3) | collective-permute-done | bytes 262176 | tf_op jit(solution)/shard_map/ppermute | solution.py:712
  39.9 1.0 collective-permute-start.8
  41.0 0.0 copy-done.4
  41.0 1.6 %prepare.1 = (f32[32,256]{1,0:T(8,128)S(1)}, f32[32,256]{1,0:T(8,128)S(1)}, f32[32,256]{1,0:T(8,128)S(1)}, bf16[256,256]{1,0:T(8,128)(2,1)S(1)}, bf16[256,256]{1...) custom-call(s32[1]{0:T(128)} %bitcast.1.shard, f32[8,256]{1,0:T(8,128)S(1)} %copy-done.4, ...), custom_call_target="tpu_custom_call" | custom-call | tf_op jit(solution)/shard_map/prepare/pallas_call | solution.py:454
  42.6 0.0 collective-permute-done.4
  42.6 3.5 %collective-permute-done.5 = f32[256,256]{1,0:T(8,128)S(1)} collective-permute-done((f32[256,256]{1,0:T(8,128)S(1)}, f32[256,256]{1,0:T(8,128)S(1)}, u32[]{:S(2)}, u32[]{:S(2)}) %collective-permute-start.5) | collective-permute-done | bytes 262176 | tf_op jit(solution)/shard_map/ppermute | solution.py:712
  46.1 6.0 %collective-permute-done.6 = f32[256,256]{1,0:T(8,128)S(1)} collective-permute-done((f32[256,256]{1,0:T(8,128)S(1)}, f32[256,256]{1,0:T(8,128)S(1)}, u32[]{:S(2)}, u32[]{:S(2)}) %collective-permute-start.6) | collective-permute-done | bytes 262176 | tf_op jit(solution)/shard_map/ppermute | solution.py:712
  52.2 0.0 collective-permute-done.7
  52.2 0.0 collective-permute-done.8
  52.2 1.8 %project.1 = (f32[64,32,256]{2,1,0:T(8,128)S(1)}, f32[2,32,256]{2,1,0:T(8,128)S(1)}) custom-call(bf16[256,256]{1,0:T(8,128)(2,1)S(1)} %get-tuple-element.48.mix_high, bf16[256,256]{1,0:T(8,128)(2,1)S(1)} %get-tuple-element.49.mix_low, f32[32,256]{1,0:T(8,128)S(1)} %get-tuple-element.50.ratio, f32[4,64,256]{2,1,0:T(8,128)S(1)} %bitcast.19, ...), custom_call_target="tpu_custom_call" | custom-call | tf_op jit(solution)/shard_map/project/pallas_call | solution.py:493
  53.9 2.5 %collective-permute-start.9 = (f32[2,32,256]{2,1,0:T(8,128)S(1)}, f32[2,32,256]{2,1,0:T(8,128)S(1)}, u32[]{:S(2)}, u32[]{:S(2)}) collective-permute-start(f32[2,32,256]{2,1,0:T(8,128)S(1)} %get-tuple-element.63.refs_0_), channel_id=1, source_target_pairs={{1,0},{0,1},{3,2},{2,3},{5,4},{4,5},{7,6},{6,7},{9,8},{8,9},{11,10... | collective-permute-start | bytes 196616 | tf_op jit(solution)/shard_map/ppermute | solution.py:517
  56.4 0.9 collective-permute-done.9.refs_1_
  57.3 6.8 %collective-permute-start.10 = (f32[2,32,256]{2,1,0:T(8,128)S(1)}, f32[2,32,256]{2,1,0:T(8,128)S(1)}, u32[]{:S(2)}, u32[]{:S(2)}) collective-permute-start(f32[2,32,256]{2,1,0:T(8,128)S(1)} %join.2.refs_0_.refs_2_), channel_id=1, source_target_pairs={{2,0},{3,1},{4,2},{5,3},{6,4},{7,5},{0,6},{1,7},{10,8},{11,9},{12,... | collective-permute-start | bytes 196616 | tf_op jit(solution)/shard_map/ppermute | solution.py:517
  64.1 0.0 collective-permute-start.11
  64.1 1.0 collective-permute-start.12
  65.1 2.2 %collective-permute-done.10.refs_1_.refs_3_ = f32[2,32,256]{2,1,0:T(8,128)S(1)} collective-permute-done((f32[2,32,256]{2,1,0:T(8,128)S(1)}, f32[2,32,256]{2,1,0:T(8,128)S(1)}, u32[]{:S(2)}, u32[]{:S(2)}) %collective-permute-start.10) | collective-permute-done | bytes 65568 | tf_op jit(solution)/shard_map/ppermute | solution.py:517
  67.2 3.0 %collective-permute-done.11.refs_2_.refs_4_ = f32[2,32,256]{2,1,0:T(8,128)S(1)} collective-permute-done((f32[2,32,256]{2,1,0:T(8,128)S(1)}, f32[2,32,256]{2,1,0:T(8,128)S(1)}, u32[]{:S(2)}, u32[]{:S(2)}) %collective-permute-start.11) | collective-permute-done | bytes 65568 | tf_op jit(solution)/shard_map/ppermute | solution.py:517
  70.2 0.4 collective-permute-done.12.refs_3_.refs_5_
  70.6 0.1 join.3.refs_6_
  70.7 3.3 %collective-permute-start.13 = (f32[2,32,256]{2,1,0:T(8,128)S(1)}, f32[2,32,256]{2,1,0:T(8,128)S(1)}, u32[]{:S(2)}, u32[]{:S(2)}) collective-permute-start(f32[2,32,256]{2,1,0:T(8,128)S(1)} %join.3.refs_6_), channel_id=1, source_target_pairs={{8,0},{9,1},{10,2},{11,3},{12,4},{13,5},{14,6},{15,7},{16,8},{17,9... | collective-permute-start | bytes 196616 | tf_op jit(solution)/shard_map/ppermute | solution.py:517
  73.9 3.2 %collective-permute-start.14 = (f32[2,32,256]{2,1,0:T(8,128)S(1)}, f32[2,32,256]{2,1,0:T(8,128)S(1)}, u32[]{:S(2)}, u32[]{:S(2)}) collective-permute-start(f32[2,32,256]{2,1,0:T(8,128)S(1)} %join.3.refs_6_), channel_id=1, source_target_pairs={{16,0},{17,1},{18,2},{19,3},{20,4},{21,5},{22,6},{23,7},{24,8},{25... | collective-permute-start | bytes 196616 | tf_op jit(solution)/shard_map/ppermute | solution.py:517
  77.1 1.1 collective-permute-start.15
  78.2 0.0 collective-permute-done.13.refs_7_
  78.2 4.6 %collective-permute-done.14.refs_8_ = f32[2,32,256]{2,1,0:T(8,128)S(1)} collective-permute-done((f32[2,32,256]{2,1,0:T(8,128)S(1)}, f32[2,32,256]{2,1,0:T(8,128)S(1)}, u32[]{:S(2)}, u32[]{:S(2)}) %collective-permute-start.14) | collective-permute-done | bytes 65568 | tf_op jit(solution)/shard_map/ppermute | solution.py:517
  82.9 1.1 collective-permute-done.15.refs_9_
  84.0 2.1 %solve.1 = (f32[4,64,256]{2,1,0:T(8,128)S(1)}, f32[4,64,256]{2,1,0:T(8,128)S(1)}, f32[4,64,256]{2,1,0:T(8,128)S(1)}, f32[4,64,256]{2,1,0:T(8,128)S(1)}, f32[4,64...) custom-call(s32[1]{0:T(128)} %bitcast.place, ...), custom_call_target="tpu_custom_call" | custom-call | tf_op jit(solution)/shard_map/solve/pallas_call | solution.py:614
  86.2 1.0 collective-permute-start.16
  87.1 1.6 %collective-permute-start.17 = (f32[256,256]{1,0:T(8,128)S(1)}, f32[256,256]{1,0:T(8,128)S(1)}, u32[]{:S(2)}, u32[]{:S(2)}) collective-permute-start(f32[256,256]{1,0:T(8,128)S(1)} %bitcast.33), channel_id=1, source_target_pairs={{0,32},{32,0},{64,96},{96,64},{128,160},{160,128},{192,224},{224,1... | collective-permute-start | bytes 786440 | tf_op jit(solution)/shard_map/ppermute | solution.py:712
  88.7 2.5 %collective-permute-start.18 = (f32[256,256]{1,0:T(8,128)S(1)}, f32[256,256]{1,0:T(8,128)S(1)}, u32[]{:S(2)}, u32[]{:S(2)}) collective-permute-start(f32[256,256]{1,0:T(8,128)S(1)} %bitcast.32), channel_id=1, source_target_pairs={{0,128},{32,160},{64,192},{96,224},{128,0},{160,32},{192,64},{224,... | collective-permute-start | bytes 786440 | tf_op jit(solution)/shard_map/ppermute | solution.py:712
  91.2 0.0 collective-permute-start.19
  91.2 4.1 %collective-permute-start.20 = (f32[256,256]{1,0:T(8,128)S(1)}, f32[256,256]{1,0:T(8,128)S(1)}, u32[]{:S(2)}, u32[]{:S(2)}) collective-permute-start(f32[256,256]{1,0:T(8,128)S(1)} %bitcast.30), channel_id=1, source_target_pairs={{0,224},{32,192},{64,32},{96,0},{128,96},{160,64},{192,160},{224,1... | collective-permute-start | bytes 786440 | tf_op jit(solution)/shard_map/ppermute | solution.py:712
  95.4 2.6 %collective-permute-done.16.refs_1_ = f32[256,256]{1,0:T(8,128)S(1)} collective-permute-done((f32[256,256]{1,0:T(8,128)S(1)}, f32[256,256]{1,0:T(8,128)S(1)}, u32[]{:S(2)}, u32[]{:S(2)}) %collective-permute-start.16) | collective-permute-done | bytes 262176 | tf_op jit(solution)/shard_map/ppermute | solution.py:712
  97.9 0.5 collective-permute-start.21
  98.4 3.1 %collective-permute-done.17.refs_2_ = f32[256,256]{1,0:T(8,128)S(1)} collective-permute-done((f32[256,256]{1,0:T(8,128)S(1)}, f32[256,256]{1,0:T(8,128)S(1)}, u32[]{:S(2)}, u32[]{:S(2)}) %collective-permute-start.17) | collective-permute-done | bytes 262176 | tf_op jit(solution)/shard_map/ppermute | solution.py:712
  101.5 2.2 %collective-permute-start.22 = (f32[256,256]{1,0:T(8,128)S(1)}, f32[256,256]{1,0:T(8,128)S(1)}, u32[]{:S(2)}, u32[]{:S(2)}) collective-permute-start(f32[256,256]{1,0:T(8,128)S(1)} %bitcast.28), channel_id=1, source_target_pairs={{0,192},{32,224},{64,0},{96,32},{128,64},{160,96},{192,128},{224,1... | collective-permute-start | bytes 786440 | tf_op jit(solution)/shard_map/ppermute | solution.py:712
  103.8 2.3 %collective-permute-done.18.refs_3_ = f32[256,256]{1,0:T(8,128)S(1)} collective-permute-done((f32[256,256]{1,0:T(8,128)S(1)}, f32[256,256]{1,0:T(8,128)S(1)}, u32[]{:S(2)}, u32[]{:S(2)}) %collective-permute-start.18) | collective-permute-done | bytes 262176 | tf_op jit(solution)/shard_map/ppermute | solution.py:712
  106.0 1.9 %inverse_part.1.partial = f32[512,1024]{1,0:T(8,128)S(1)} custom-call(s32[1]{0:T(128)} %bitcast.1.shard, bf16[1024,1024]{1,0:T(8,128)(2,1)S(1)} %get-tuple-element.45.table_high, bf16[1024,1024]{1,0:T(8,128)(2,1)S(1)} %get-tuple-element.46.table_low, f32[256,256]{1,0:T(8,128)S(1)} %bitcast.27, f32[256,256]{1,0:T(8,128)S(1)} %collective-permute-done.16.refs_1_, ...), custom_call_target="tpu_custom_call" | custom-call | flops 1610612736 | bytes 2097152 | tf_op jit(solution)/shard_map/inverse_part/pallas_call | solution.py:684
  107.9 1.2 %collective-permute-done.19.refs_0_ = f32[256,256]{1,0:T(8,128)S(1)} collective-permute-done((f32[256,256]{1,0:T(8,128)S(1)}, f32[256,256]{1,0:T(8,128)S(1)}, u32[]{:S(2)}, u32[]{:S(2)}) %collective-permute-start.19) | collective-permute-done | bytes 262176 | tf_op jit(solution)/shard_map/ppermute | solution.py:712
  109.0 3.7 %collective-permute-done.20.refs_1_ = f32[256,256]{1,0:T(8,128)S(1)} collective-permute-done((f32[256,256]{1,0:T(8,128)S(1)}, f32[256,256]{1,0:T(8,128)S(1)}, u32[]{:S(2)}, u32[]{:S(2)}) %collective-permute-start.20) | collective-permute-done | bytes 262176 | tf_op jit(solution)/shard_map/ppermute | solution.py:712
  112.7 0.2 collective-permute-done.21.refs_2_
  112.9 0.7 collective-permute-done.22.refs_3_
  113.6 3.1 %inverse_rest.1 = f32[256,2048]{1,0:T(8,128)} custom-call(s32[1]{0:T(128)} %bitcast.1.shard, bf16[1024,1024]{1,0:T(8,128)(2,1)S(1)} %get-tuple-element.45.table_high, bf16[1024,1024]{1,0:T(8,128)(2,1)S(1)} %get-tuple-element.46.table_low, f32[512,1024]{1,0:T(8,128)S(1)} %inverse_part.1.partial, f32[256,256]{1,0:T(8,128)S(1)} %collective-permute-done.19.refs_0_, ...), custom_call_target="tpu_custom_call" | custom-call | tf_op jit(solution)/shard_map/inverse_rest/pallas_call | solution.py:695
  (8 shorter events, 0.0 us)
Async XLA Ops:
  2.7 14.6 %collective-permute-start = (f32[4,4,2048]{2,1,0:T(4,128)}, f32[4,4,2048]{2,1,0:T(4,128)S(1)}, u32[]{:S(2)}, u32[]{:S(2)}) collective-permute-start(f32[4,4,2048]{2,1,0:T(4,128)} %get-tuple-element.37), channel_id=1, source_target_pairs={{0,1},{1,2},{2,3},{3,4},{4,5},{5,6},{6,7},{7,8},{8,9},{9,10},{10,1... | collective-permute-start | bytes 393224 | tf_op jit(solution)/shard_map/ppermute | solution.py:728
  4.5 12.8 %collective-permute-start.1 = (f32[4,4,2048]{2,1,0:T(4,128)}, f32[4,4,2048]{2,1,0:T(4,128)S(1)}, u32[]{:S(2)}, u32[]{:S(2)}) collective-permute-start(f32[4,4,2048]{2,1,0:T(4,128)} %get-tuple-element.38), channel_id=1, source_target_pairs={{1,0},{2,1},{3,2},{4,3},{5,4},{6,5},{7,6},{8,7},{9,8},{10,9},{11,1... | collective-permute-start | bytes 393224 | tf_op jit(solution)/shard_map/ppermute | solution.py:729
  5.8 1.6 %copy-start = (f32[4,64,2048]{2,1,0:T(8,128)S(1)}, f32[4,64,2048]{2,1,0:T(8,128)}, u32[]{:S(2)}) copy-start(f32[4,64,2048]{2,1,0:T(8,128)} %prev.1) | copy-start | bytes 6291460
  7.4 1.6 %copy-start.1 = (f32[4,64,2048]{2,1,0:T(8,128)S(1)}, f32[4,64,2048]{2,1,0:T(8,128)}, u32[]{:S(2)}) copy-start(f32[4,64,2048]{2,1,0:T(8,128)} %now.1) | copy-start | bytes 6291460
  8.9 8.4 %copy-start.6 = (bf16[1024,1024]{1,0:T(8,128)(2,1)S(1)}, bf16[1024,1024]{1,0:T(8,128)(2,1)}, u32[]{:S(2)}) copy-start(bf16[1024,1024]{1,0:T(8,128)(2,1)} %constant.15.clone.table_high_in) | copy-start | bytes 6291460
  8.9 8.4 %copy-start.7 = (bf16[1024,1024]{1,0:T(8,128)(2,1)S(1)}, bf16[1024,1024]{1,0:T(8,128)(2,1)}, u32[]{:S(2)}) copy-start(bf16[1024,1024]{1,0:T(8,128)(2,1)} %constant.16.clone.table_low_in) | copy-start | bytes 6291460
  17.3 23.6 %copy-start.2 = (f32[32,32]{1,0:T(8,128)S(1)}, f32[32,32]{1,0:T(8,128)}, u32[]{:S(2)}) copy-start(f32[32,32]{1,0:T(8,128)} %to_modes.1) | copy-start | bytes 12292
  17.3 23.6 %copy-start.3 = (f32[32,32]{1,0:T(8,128)S(1)}, f32[32,32]{1,0:T(8,128)}, u32[]{:S(2)}) copy-start(f32[32,32]{1,0:T(8,128)} %to_layers.1) | copy-start | bytes 12292
  17.3 23.6 %copy-start.4 = (f32[8,256]{1,0:T(8,128)S(1)}, f32[8,256]{1,0:T(8,128)}, u32[]{:S(2)}) copy-start(f32[8,256]{1,0:T(8,128)} %constant.17.clone.eigen) | copy-start | bytes 24580
  17.4 23.6 %copy-start.5 = (f32[32]{0:T(128)S(1)}, f32[32]{0:T(128)}, u32[]{:S(2)}) copy-start(f32[32]{0:T(128)} %stretch.1) | copy-start | bytes 388
  23.9 10.2 %collective-permute-start.2 = (f32[256,256]{1,0:T(8,128)S(1)}, f32[256,256]{1,0:T(8,128)S(1)}, u32[]{:S(2)}, u32[]{:S(2)}) collective-permute-start(f32[256,256]{1,0:T(8,128)S(1)} %get-tuple-element.52), channel_id=1, source_target_pairs={{0,160},{32,128},{64,224},{96,192},{128,32},{160,0},{192,96},{224,... | collective-permute-start | bytes 786440 | tf_op jit(solution)/shard_map/ppermute | solution.py:712
  26.7 13.3 %collective-permute-start.3 = (f32[256,256]{1,0:T(8,128)S(1)}, f32[256,256]{1,0:T(8,128)S(1)}, u32[]{:S(2)}, u32[]{:S(2)}) collective-permute-start(f32[256,256]{1,0:T(8,128)S(1)} %get-tuple-element.53), channel_id=1, source_target_pairs={{0,32},{32,0},{64,96},{96,64},{128,160},{160,128},{192,224},{224,1... | collective-permute-start | bytes 786440 | tf_op jit(solution)/shard_map/ppermute | solution.py:712
  28.6 14.0 %collective-permute-start.4 = (f32[256,256]{1,0:T(8,128)S(1)}, f32[256,256]{1,0:T(8,128)S(1)}, u32[]{:S(2)}, u32[]{:S(2)}) collective-permute-start(f32[256,256]{1,0:T(8,128)S(1)} %get-tuple-element.54), channel_id=1, source_target_pairs={{0,128},{32,160},{64,192},{96,224},{128,0},{160,32},{192,64},{224,... | collective-permute-start | bytes 786440 | tf_op jit(solution)/shard_map/ppermute | solution.py:712
  28.9 17.2 %collective-permute-start.5 = (f32[256,256]{1,0:T(8,128)S(1)}, f32[256,256]{1,0:T(8,128)S(1)}, u32[]{:S(2)}, u32[]{:S(2)}) collective-permute-start(f32[256,256]{1,0:T(8,128)S(1)} %get-tuple-element.55), channel_id=1, source_target_pairs={{0,96},{32,64},{64,160},{96,128},{128,224},{160,192},{192,32},{224... | collective-permute-start | bytes 786440 | tf_op jit(solution)/shard_map/ppermute | solution.py:712
  30.1 22.1 %collective-permute-start.6 = (f32[256,256]{1,0:T(8,128)S(1)}, f32[256,256]{1,0:T(8,128)S(1)}, u32[]{:S(2)}, u32[]{:S(2)}) collective-permute-start(f32[256,256]{1,0:T(8,128)S(1)} %get-tuple-element.56), channel_id=1, source_target_pairs={{0,224},{32,192},{64,32},{96,0},{128,96},{160,64},{192,160},{224,1... | collective-permute-start | bytes 786440 | tf_op jit(solution)/shard_map/ppermute | solution.py:712
  34.1 18.1 %collective-permute-start.7 = (f32[256,256]{1,0:T(8,128)S(1)}, f32[256,256]{1,0:T(8,128)S(1)}, u32[]{:S(2)}, u32[]{:S(2)}) collective-permute-start(f32[256,256]{1,0:T(8,128)S(1)} %get-tuple-element.57), channel_id=1, source_target_pairs={{0,64},{32,96},{64,128},{96,160},{128,192},{160,224},{192,0},{224,... | collective-permute-start | bytes 786440 | tf_op jit(solution)/shard_map/ppermute | solution.py:712
  39.9 12.2 %collective-permute-start.8 = (f32[256,256]{1,0:T(8,128)S(1)}, f32[256,256]{1,0:T(8,128)S(1)}, u32[]{:S(2)}, u32[]{:S(2)}) collective-permute-start(f32[256,256]{1,0:T(8,128)S(1)} %get-tuple-element.58), channel_id=1, source_target_pairs={{0,192},{32,224},{64,0},{96,32},{128,64},{160,96},{192,128},{224,1... | collective-permute-start | bytes 786440 | tf_op jit(solution)/shard_map/ppermute | solution.py:712
  53.9 3.4 %collective-permute-start.9 = (f32[2,32,256]{2,1,0:T(8,128)S(1)}, f32[2,32,256]{2,1,0:T(8,128)S(1)}, u32[]{:S(2)}, u32[]{:S(2)}) collective-permute-start(f32[2,32,256]{2,1,0:T(8,128)S(1)} %get-tuple-element.63.refs_0_), channel_id=1, source_target_pairs={{1,0},{0,1},{3,2},{2,3},{5,4},{4,5},{7,6},{6,7},{9,8},{8,9},{11,10... | collective-permute-start | bytes 196616 | tf_op jit(solution)/shard_map/ppermute | solution.py:517
  57.3 9.9 %collective-permute-start.10 = (f32[2,32,256]{2,1,0:T(8,128)S(1)}, f32[2,32,256]{2,1,0:T(8,128)S(1)}, u32[]{:S(2)}, u32[]{:S(2)}) collective-permute-start(f32[2,32,256]{2,1,0:T(8,128)S(1)} %join.2.refs_0_.refs_2_), channel_id=1, source_target_pairs={{2,0},{3,1},{4,2},{5,3},{6,4},{7,5},{0,6},{1,7},{10,8},{11,9},{12,... | collective-permute-start | bytes 196616 | tf_op jit(solution)/shard_map/ppermute | solution.py:517
  64.1 6.1 %collective-permute-start.11 = (f32[2,32,256]{2,1,0:T(8,128)S(1)}, f32[2,32,256]{2,1,0:T(8,128)S(1)}, u32[]{:S(2)}, u32[]{:S(2)}) collective-permute-start(f32[2,32,256]{2,1,0:T(8,128)S(1)} %join.2.refs_0_.refs_2_), channel_id=1, source_target_pairs={{4,0},{5,1},{6,2},{7,3},{0,4},{1,5},{2,6},{3,7},{12,8},{13,9},{14,... | collective-permute-start | bytes 196616 | tf_op jit(solution)/shard_map/ppermute | solution.py:517
  64.1 6.5 %collective-permute-start.12 = (f32[2,32,256]{2,1,0:T(8,128)S(1)}, f32[2,32,256]{2,1,0:T(8,128)S(1)}, u32[]{:S(2)}, u32[]{:S(2)}) collective-permute-start(f32[2,32,256]{2,1,0:T(8,128)S(1)} %join.2.refs_0_.refs_2_), channel_id=1, source_target_pairs={{6,0},{7,1},{0,2},{1,3},{2,4},{3,5},{4,6},{5,7},{14,8},{15,9},{8,1... | collective-permute-start | bytes 196616 | tf_op jit(solution)/shard_map/ppermute | solution.py:517
  70.7 7.6 %collective-permute-start.13 = (f32[2,32,256]{2,1,0:T(8,128)S(1)}, f32[2,32,256]{2,1,0:T(8,128)S(1)}, u32[]{:S(2)}, u32[]{:S(2)}) collective-permute-start(f32[2,32,256]{2,1,0:T(8,128)S(1)} %join.3.refs_6_), channel_id=1, source_target_pairs={{8,0},{9,1},{10,2},{11,3},{12,4},{13,5},{14,6},{15,7},{16,8},{17,9... | collective-permute-start | bytes 196616 | tf_op jit(solution)/shard_map/ppermute | solution.py:517
  73.9 8.9 %collective-permute-start.14 = (f32[2,32,256]{2,1,0:T(8,128)S(1)}, f32[2,32,256]{2,1,0:T(8,128)S(1)}, u32[]{:S(2)}, u32[]{:S(2)}) collective-permute-start(f32[2,32,256]{2,1,0:T(8,128)S(1)} %join.3.refs_6_), channel_id=1, source_target_pairs={{16,0},{17,1},{18,2},{19,3},{20,4},{21,5},{22,6},{23,7},{24,8},{25... | collective-permute-start | bytes 196616 | tf_op jit(solution)/shard_map/ppermute | solution.py:517
  77.1 6.9 %collective-permute-start.15 = (f32[2,32,256]{2,1,0:T(8,128)S(1)}, f32[2,32,256]{2,1,0:T(8,128)S(1)}, u32[]{:S(2)}, u32[]{:S(2)}) collective-permute-start(f32[2,32,256]{2,1,0:T(8,128)S(1)} %join.3.refs_6_), channel_id=1, source_target_pairs={{24,0},{25,1},{26,2},{27,3},{28,4},{29,5},{30,6},{31,7},{0,8},{1,9... | collective-permute-start | bytes 196616 | tf_op jit(solution)/shard_map/ppermute | solution.py:517
  86.2 11.8 %collective-permute-start.16 = (f32[256,256]{1,0:T(8,128)S(1)}, f32[256,256]{1,0:T(8,128)S(1)}, u32[]{:S(2)}, u32[]{:S(2)}) collective-permute-start(f32[256,256]{1,0:T(8,128)S(1)} %bitcast.34), channel_id=1, source_target_pairs={{0,160},{32,128},{64,224},{96,192},{128,32},{160,0},{192,96},{224,... | collective-permute-start | bytes 786440 | tf_op jit(solution)/shard_map/ppermute | solution.py:712
  87.1 14.4 %collective-permute-start.17 = (f32[256,256]{1,0:T(8,128)S(1)}, f32[256,256]{1,0:T(8,128)S(1)}, u32[]{:S(2)}, u32[]{:S(2)}) collective-permute-start(f32[256,256]{1,0:T(8,128)S(1)} %bitcast.33), channel_id=1, source_target_pairs={{0,32},{32,0},{64,96},{96,64},{128,160},{160,128},{192,224},{224,1... | collective-permute-start | bytes 786440 | tf_op jit(solution)/shard_map/ppermute | solution.py:712
  88.7 17.3 %collective-permute-start.18 = (f32[256,256]{1,0:T(8,128)S(1)}, f32[256,256]{1,0:T(8,128)S(1)}, u32[]{:S(2)}, u32[]{:S(2)}) collective-permute-start(f32[256,256]{1,0:T(8,128)S(1)} %bitcast.32), channel_id=1, source_target_pairs={{0,128},{32,160},{64,192},{96,224},{128,0},{160,32},{192,64},{224,... | collective-permute-start | bytes 786440 | tf_op jit(solution)/shard_map/ppermute | solution.py:712
  91.2 17.8 %collective-permute-start.19 = (f32[256,256]{1,0:T(8,128)S(1)}, f32[256,256]{1,0:T(8,128)S(1)}, u32[]{:S(2)}, u32[]{:S(2)}) collective-permute-start(f32[256,256]{1,0:T(8,128)S(1)} %bitcast.31), channel_id=1, source_target_pairs={{0,96},{32,64},{64,160},{96,128},{128,224},{160,192},{192,32},{224... | collective-permute-start | bytes 786440 | tf_op jit(solution)/shard_map/ppermute | solution.py:712
  91.2 21.5 %collective-permute-start.20 = (f32[256,256]{1,0:T(8,128)S(1)}, f32[256,256]{1,0:T(8,128)S(1)}, u32[]{:S(2)}, u32[]{:S(2)}) collective-permute-start(f32[256,256]{1,0:T(8,128)S(1)} %bitcast.30), channel_id=1, source_target_pairs={{0,224},{32,192},{64,32},{96,0},{128,96},{160,64},{192,160},{224,1... | collective-permute-start | bytes 786440 | tf_op jit(solution)/shard_map/ppermute | solution.py:712
  97.9 14.9 %collective-permute-start.21 = (f32[256,256]{1,0:T(8,128)S(1)}, f32[256,256]{1,0:T(8,128)S(1)}, u32[]{:S(2)}, u32[]{:S(2)}) collective-permute-start(f32[256,256]{1,0:T(8,128)S(1)} %bitcast.29), channel_id=1, source_target_pairs={{0,64},{32,96},{64,128},{96,160},{128,192},{160,224},{192,0},{224,... | collective-permute-start | bytes 786440 | tf_op jit(solution)/shard_map/ppermute | solution.py:712
  101.5 12.0 %collective-permute-start.22 = (f32[256,256]{1,0:T(8,128)S(1)}, f32[256,256]{1,0:T(8,128)S(1)}, u32[]{:S(2)}, u32[]{:S(2)}) collective-permute-start(f32[256,256]{1,0:T(8,128)S(1)} %bitcast.28), channel_id=1, source_target_pairs={{0,192},{32,224},{64,0},{96,32},{128,64},{160,96},{192,128},{224,1... | collective-permute-start | bytes 786440 | tf_op jit(solution)/shard_map/ppermute | solution.py:712
